TPU v7x, 128 devices: a whole 4x4x4 slice. The times are simulated.
128 devices in a mesh: dp: 8 (over z, core), fsdp: 16 (over x, y).
Axes of the slice: x: 4, y: 4, z: 4, core: 2. Of those that a mesh axis runs over, the one named last changes fastest.
Arguments:
- tokens: bfloat16 [65536, 768], P(('dp', 'fsdp')), may hold values from -24 to 24
- lengths: int32 [8, 2], P('dp'), may hold values from 1024 to 7168, as said below
- routed: int32 [8, 1024], P('dp'), may hold values from 0 to 8191, as said below
- cotangent: bfloat16 [65536, 768], P(('dp', 'fsdp')), may hold values from -6 to 6
- gain_attn: float32 [768], P(('dp', 'fsdp')), may hold values from 0.5 to 1.5
- gain_ffn: float32 [768], P(('dp', 'fsdp')), may hold values from 0.5 to 1.5
- router_attn: float32 [768], P(('dp', 'fsdp')), may hold values from -0.15625 to 0.15625
- router_ffn: float32 [768], P(('dp', 'fsdp')), may hold values from -0.15625 to 0.15625
- light_q: float32 [768, 768], P(('dp', 'fsdp')), may hold values from -0.21875 to 0.21875
- light_k: float32 [768, 768], P(('dp', 'fsdp')), may hold values from -0.21875 to 0.21875
- light_v: float32 [768, 768], P(('dp', 'fsdp')), may hold values from -0.21875 to 0.21875
- light_o: float32 [768, 768], P(('dp', 'fsdp')), may hold values from -1.75 to 1.75
- light_gate: float32 [768, 1024], P(('dp', 'fsdp')), may hold values from -0.21875 to 0.21875
- light_up: float32 [768, 1024], P(('dp', 'fsdp')), may hold values from -0.21875 to 0.21875
- light_down: float32 [1024, 768], P(('dp', 'fsdp')), may hold values from -0.1875 to 0.1875
- heavy_q: float32 [768, 768], P(('dp', 'fsdp')), may hold values from -0.21875 to 0.21875
- heavy_k: float32 [768, 768], P(('dp', 'fsdp')), may hold values from -0.21875 to 0.21875
- heavy_v: float32 [768, 768], P(('dp', 'fsdp')), may hold values from -0.21875 to 0.21875
- heavy_o: float32 [768, 768], P(('dp', 'fsdp')), may hold values from -2.5 to 2.5
- heavy_gate: float32 [768, 4096], P(('dp', 'fsdp')), may hold values from -0.21875 to 0.21875
- heavy_up: float32 [768, 4096], P(('dp', 'fsdp')), may hold values from -0.21875 to 0.21875
- heavy_down: float32 [4096, 768], P(('dp', 'fsdp')), may hold values from -0.1875 to 0.1875
Outputs:
- output: bfloat16 [65536, 768], P(('dp', 'fsdp'))
- grad_tokens: bfloat16 [65536, 768], P(('dp', 'fsdp'))
- grad_gain_attn: float32 [768], P(('dp', 'fsdp'))
- grad_gain_ffn: float32 [768], P(('dp', 'fsdp'))
- grad_router_attn: float32 [768], P(('dp', 'fsdp'))
- grad_router_ffn: float32 [768], P(('dp', 'fsdp'))
- grad_light_q: float32 [768, 768], P(('dp', 'fsdp'))
- grad_light_k: float32 [768, 768], P(('dp', 'fsdp'))
- grad_light_v: float32 [768, 768], P(('dp', 'fsdp'))
- grad_light_o: float32 [768, 768], P(('dp', 'fsdp'))
- grad_light_gate: float32 [768, 1024], P(('dp', 'fsdp'))
- grad_light_up: float32 [768, 1024], P(('dp', 'fsdp'))
- grad_light_down: float32 [1024, 768], P(('dp', 'fsdp'))
- grad_heavy_q: float32 [768, 768], P(('dp', 'fsdp'))
- grad_heavy_k: float32 [768, 768], P(('dp', 'fsdp'))
- grad_heavy_v: float32 [768, 768], P(('dp', 'fsdp'))
- grad_heavy_o: float32 [768, 768], P(('dp', 'fsdp'))
- grad_heavy_gate: float32 [768, 4096], P(('dp', 'fsdp'))
- grad_heavy_up: float32 [768, 4096], P(('dp', 'fsdp'))
- grad_heavy_down: float32 [4096, 768], P(('dp', 'fsdp'))
Inputs may be any that keep to these rules, and one draw needn't show every extreme that they name: Each row holds 2 lengths, each a multiple of 8, that add up to 8192. `routed`: each row lists, in increasing order, positions within its pack: from every sequence exactly its length / 8 distinct positions, among them the sequence's first and last position.
All inputs are finite; a program needn't handle non-finite values.
Results may differ from a plain program's by a relative error of at most 0.013.
The roundings to bfloat16 on the way count: a program that leaves them out, or rounds other values in their place, can miss the bound.
Values may be sent and summed in bfloat16 or wider, within the bound.
No kernel may reach another device: no remote copies, remote signals or barrier semaphores. Data moves between devices by JAX's collectives and lax.ppermute only.
A program may use at most 256 MiB of HBM per device.

v0:
```python
import jax
import jax.numpy as jnp
from jax import lax
from jax.experimental import pallas as pl
from jax.experimental.pallas import tpu as pltpu
from jax.sharding import PartitionSpec as P

BF = jnp.bfloat16
F32 = jnp.float32
EPS = 1e-6
NEG = -1e30
ALL = ("dp", "fsdp")
CAP = 96
LIGHT_SCALE = 96**-0.5
HEAVY_SCALE = 64**-0.5
PARAMS = pltpu.CompilerParams(vmem_limit_bytes=60 * 1024 * 1024)
SMEM = pl.BlockSpec(memory_space=pltpu.SMEM)
VMEM = pl.BlockSpec(memory_space=pltpu.VMEM)
HBM = pl.BlockSpec(memory_space=pl.ANY)

C_QKVO, C_VEC, C_DOWN, C_HO, C_ALL = 2048, 5120, 5248, 6016, 6784
F_DOWN, F_ALL = 2048, 3072
R_HEAVY, R_HO, R_VEC, R_DOWN, R_ALL = 3072, 3968, 4736, 4864, 5120
S_DOWN, S_REST, S_BACK, S_ALL = 1536, 2304, 6144, 7680

def dot(a, b):
    return jnp.dot(a, b, preferred_element_type=F32)


def dot_nt(a, b):
    return lax.dot_general(a, b, (((1,), (1,)), ((), ())), preferred_element_type=F32)


def dot_tn(a, b):
    return lax.dot_general(a, b, (((0,), (0,)), ((), ())), preferred_element_type=F32)


def pick6(rows, cols, shift=0):
    r = lax.broadcasted_iota(jnp.int32, (rows, cols), 0) + shift
    c = lax.broadcasted_iota(jnp.int32, (rows, cols), 1)
    low = c & 7
    return ((6 * (c >> 3) + low == r) & (low < 6)).astype(F32).astype(BF)


def unpad_rows(ref, out_ref, pick, at=0, width=None):
    width = width or ref.shape[1]
    for b in range(8):
        block = dot(pick, ref[128 * b : 128 * b + 128, at : at + width])
        out_ref[96 * b : 96 * b + 96, at : at + width] = block.astype(BF)


def vector_rows(vec_ref, pick):
    blocks = [dot(pick, vec_ref[128 * b : 128 * b + 128, :]) for b in range(8)]
    return jnp.concatenate(blocks, axis=0).T


class Copies:
    def __init__(self, sems, used=0):
        self.sems, self.used, self.open = sems, used, []

    def start(self, src, dst):
        copy = pltpu.make_async_copy(src, dst, self.sems.at[self.used])
        self.used += 1
        copy.start()
        return copy

    def send(self, src, dst):
        self.open.append(self.start(src, dst))

    def finish(self):
        for copy in self.open:
            copy.wait()


def unit(rows):
    scale = lax.rsqrt(jnp.mean(rows * rows, axis=-1, keepdims=True) + EPS)
    return rows * scale, scale


def gelu_parts(gate):
    c0, c1 = 0.7978845608, 0.044715
    sq = gate * gate
    t = jnp.tanh(gate * (c0 + (c0 * c1) * sq))
    half = 0.5 * (1.0 + t)
    slope = half + (0.5 * gate) * (1.0 - t * t) * (c0 + (3.0 * c0 * c1) * sq)
    return gate * half, slope


def prep_kernel(
    q, k, v, o, gate, up, down, hq, hk, hv, ho, hgate, hup, hdown, ga, gf, ra, rf, pack, hsend, hd, scr, rows
):
    scr[...] = jnp.zeros_like(scr)
    zero128 = jnp.zeros((8, 128), BF)

    def padded(ref):
        cols = ref.shape[1]
        scr[0:6, 0:cols] = ref[...]
        return scr[:, 0:cols].astype(BF)

    gp, upp = padded(gate), padded(up)
    for c in range(4):
        pack[:, 512 * c : 512 * c + 256] = gp[:, 256 * c : 256 * c + 256]
        pack[:, 512 * c + 256 : 512 * c + 512] = upp[:, 256 * c : 256 * c + 256]
    for n, ref in enumerate((q, k, v, o)):
        pack[:, C_QKVO + 768 * n : C_QKVO + 768 * n + 768] = padded(ref)
    rows[...] = jnp.zeros_like(rows)
    for n, ref in enumerate((ga, gf, ra, rf)):
        rows[n : n + 1, 0:6] = ref[...]
    pack[:, C_VEC : C_VEC + 128] = rows[...].T[0:8, :].astype(BF)
    pack[:, C_DOWN : C_DOWN + 768] = down[...].astype(BF)
    pack[:, C_HO : C_HO + 768] = padded(ho)
    wq, wk, wv = padded(hq), padded(hk), padded(hv)
    wg, wu = padded(hgate), padded(hup)
    for j in range(16):
        hsend[j, :, 0:256] = wg[:, 256 * j : 256 * j + 256]
        hsend[j, :, 256:512] = wu[:, 256 * j : 256 * j + 256]
        for n, w in enumerate((wq, wk, wv)):
            p = j // 2
            part = w[:, 128 * p : 128 * p + 128] if j < 12 else zero128
            hsend[j, :, 512 + 128 * n : 640 + 128 * n] = part
    hd[...] = hdown[...].astype(BF)


def light_ffn_kernel(
    x_in, g_in, wall, ffn, cf, light, gvec, vrows, x, g, gu, fin, fin_t, gbuf, gu_pad, down, vec, in_sems, out_sems
):
    def wide(c, at=0):
        return pl.ds(pl.multiple_of(at + 512 * c, 128), 512)

    def loads(c):
        rows = pl.ds(pl.multiple_of(256 * c, 256), 256)
        yield pltpu.make_async_copy(wall.at[:, wide(c)], gu_pad.at[:, wide(c)], in_sems.at[2 * c])
        yield pltpu.make_async_copy(
            wall.at[rows, C_DOWN : C_DOWN + 768], down.at[rows, :], in_sems.at[2 * c + 1]
        )

    def stores(c):
        rows = pl.ds(pl.multiple_of(192 * c, 64), 192)
        yield pltpu.make_async_copy(gbuf.at[:, wide(c)], light.at[:, wide(c)], out_sems.at[2 * c])
        yield pltpu.make_async_copy(
            gbuf.at[rows, 2048:3072], light.at[rows, F_DOWN:F_ALL], out_sems.at[2 * c + 1]
        )

    first = Copies(in_sems, 8)
    got_x = first.start(x_in, x)
    got_vec = first.start(wall.at[:, C_VEC : C_VEC + 128], vec)
    got_g = first.start(g_in, g)
    for c in range(4):
        for copy in loads(c):
            copy.start()
    pick = pick6(96, 128)
    got_x.wait()
    u, _ = unit(x[...].astype(F32))
    got_vec.wait()
    vrows[...] = vector_rows(vec, pick)[0:8, :]
    gain_f = vrows[1:2, :]
    f = (u * gain_f).astype(BF)
    fin[...] = f
    fin_t[...] = f.T
    ffn[...] = jnp.zeros_like(ffn)
    cf[...] = jnp.zeros_like(cf)
    got_g.wait()

    @pl.loop(0, 4)
    def _(c):
        for copy in loads(c):
            copy.wait()
        for b in range(8):
            block = dot(pick, gu_pad[128 * b : 128 * b + 128, wide(c)])
            gu[96 * b : 96 * b + 96, :] = block.astype(BF)
        w = gu[...]
        wd = down[pl.ds(pl.multiple_of(256 * c, 256), 256), :]
        both = dot(fin[...], w)
        act, slope = gelu_parts(both[:, 0:256])
        up = both[:, 256:512]
        hidden = (act * up).astype(BF)
        dh = dot_nt(g[...], wd)
        dgu = jnp.concatenate([(dh * up * slope).astype(BF), (dh * act).astype(BF)], axis=1)
        ffn[...] += dot(hidden, wd)
        cf[...] += dot_nt(dgu, w)
        gbuf[:, wide(c)] = dot(fin_t[...], dgu).astype(BF)
        gd = dot_tn(hidden, g[...]).astype(BF)
        for n in range(2):
            r0 = 128 * n
            at = pl.multiple_of(192 * c + 96 * n, 32)
            gbuf[pl.ds(at, 96), 2048:2816] = gd[r0 : r0 + 96, :]
            for t in range(3):
                gbuf[pl.ds(pl.multiple_of(at + 32 * t, 32), 32), 2816:3072] = gd[
                    r0 + 96 : r0 + 128, 256 * t : 256 * t + 256
                ]
        for copy in stores(c):
            copy.start()

    u, _ = unit(x[...].astype(F32))
    d_f = cf[...]
    gvec[...] = jnp.zeros_like(gvec)
    gvec[1:2, :] = jnp.sum(d_f * u, axis=0, keepdims=True)
    cf[...] = d_f * gain_f
    for c in range(4):
        for copy in stores(c):
            copy.wait()


def light_attn_kernel(
    meta, xl, x_in, xr, g_in, wall, ffn_in, cf_in, gin, vrows,
    lo, dxg, halo, rest, gvec,
    w, xs, a, a_t, qkv, o, do, dqkv, dk, dv, mask, w_pad, g, ffn, cf, lo_buf, d_a, gbuf, in_sems, out_sems,
):
    def wide(n, at=0):
        return pl.ds(pl.multiple_of(at + 768 * n, 128), 768)

    def load(n):
        return pltpu.make_async_copy(wall.at[:, wide(n, C_QKVO)], w_pad.at[:, wide(n)], in_sems.at[n])

    def store(n):
        return pltpu.make_async_copy(gbuf.at[:, wide(n)], rest.at[:, wide(n)], out_sems.at[n])

    loads, stores = Copies(in_sems, 4), Copies(out_sems, 4)
    x = xs.at[64:576, :]
    got_x = loads.start(x_in, x)
    for n in range(4):
        load(n).start()
    got_g = loads.start(g_in, g)
    got_ffn = loads.start(ffn_in, ffn)
    got_cf = loads.start(cf_in, cf)
    pick = pick6(96, 128)
    xs[0:64, :] = xl[...]
    xs[576:640, :] = xr[...]
    first, base, pack_len = meta[0], meta[1], meta[2]
    key = lax.broadcasted_iota(jnp.int32, (256, 256), 0)
    qry = lax.broadcasted_iota(jnp.int32, (256, 256), 1) & 127
    gap = key - qry

    @pl.loop(0, 4)
    def _(b):
        qpos = base + 128 * b + qry
        kpos = base + 128 * b - 64 + key
        ok = (gap >= 0) & (gap <= 128) & ((qpos < first) == (kpos < first))
        ok = ok & (kpos >= 0) & (kpos < pack_len)
        mask[b] = jnp.where(ok, 0.0, NEG)

    dk[...] = jnp.zeros_like(dk)
    dv[...] = jnp.zeros_like(dv)
    dqkv[0:64, 0:768] = jnp.zeros((64, 768), BF)
    dqkv[576:640, 0:768] = jnp.zeros((64, 768), BF)
    got_x.wait()
    u, _ = unit(xs[...].astype(F32))
    gain_a = vrows[0:1, :]
    a[...] = (u * gain_a).astype(BF)

    def unpad(n):
        load(n).wait()
        for b in range(8):
            w[96 * b : 96 * b + 96, wide(n)] = dot(pick, w_pad[128 * b : 128 * b + 128, wide(n)]).astype(BF)

    @pl.loop(0, 3)
    def _(n):
        unpad(n)
        qkv[:, wide(n)] = dot(a[...], w[:, wide(n)]).astype(BF)

    unpad(3)
    got_g.wait()
    do[...] = dot_nt(g[...], w[:, 2304:3072]).astype(BF)

    lane = lax.broadcasted_iota(jnp.int32, (128, 256), 1)

    def pair(b, group, second):
        low = 64 * second
        even = (lane >= low) & (lane < low + 96)
        odd = (lane >= low + 96) & (lane < low + 192)

        def split(t):
            zero = jnp.zeros_like(t)
            return jnp.concatenate([jnp.where(even, t, zero), jnp.where(odd, t, zero)], axis=0)

        def join(t):
            return jnp.where(even, t[0:128], 0.0) + jnp.where(odd, t[128:256], 0.0)

        def win(part):
            return pl.ds(pl.multiple_of(768 * part + 384 * group + 128 * second, 128), 256)

        rq = pl.ds(pl.multiple_of(128 * b, 128), 128)
        rd = pl.ds(pl.multiple_of(128 * b + 64, 64), 128)
        rk = pl.ds(pl.multiple_of(128 * b, 128), 256)
        kw, vw = qkv[rk, win(1)], qkv[rk, win(2)]
        q2, do2 = split(qkv[rd, win(0)]), split(do[rq, win(0)])
        s = dot_nt(kw, q2) * LIGHT_SCALE + mask[b]
        dp = dot_nt(vw, do2)
        e = jnp.exp(s - jnp.max(s, axis=0, keepdims=True))
        p = e * (1.0 / jnp.sum(e, axis=0, keepdims=True))
        pb = p.astype(BF)
        ds = (p * (dp - jnp.sum(p * dp, axis=0, keepdims=True))).astype(BF)
        dk[rk, win(0)] += dot(ds, q2) * LIGHT_SCALE
        dv[rk, win(0)] += dot(pb, do2)
        return join(dot_tn(pb, vw)), join(dot_tn(ds, kw)) * LIGHT_SCALE

    @pl.loop(0, 8)
    def _(i):
        b, group = i >> 1, i & 1
        rq = pl.ds(pl.multiple_of(128 * b, 128), 128)
        rd = pl.ds(pl.multiple_of(128 * b + 64, 64), 128)
        o0, dq0 = pair(b, group, 0)
        o1, dq1 = pair(b, group, 1)

        def tile(n):
            return pl.ds(pl.multiple_of(384 * group + 128 * n, 128), 128)

        for ref, rows, t0, t1 in ((o, rq, o0, o1), (dqkv, rd, dq0, dq1)):
            ref[rows, tile(0)] = t0[:, 0:128].astype(BF)
            ref[rows, tile(1)] = (t0[:, 128:256] + t1[:, 0:128]).astype(BF)
            ref[rows, tile(2)] = t1[:, 128:256].astype(BF)

    got_ffn.wait()
    lo_buf[...] = x[...].astype(F32) + ffn[...] + dot(o[...], w[:, 2304:3072])
    stores.send(lo_buf, lo)
    gbuf[:, 2304:3072] = dot_tn(o[...], g[...]).astype(BF)
    store(3).start()
    dqkv[:, 768:1536] = dk[...].astype(BF)
    dqkv[:, 1536:2304] = dv[...].astype(BF)
    a_t[...] = a[...].T
    d_a[...] = jnp.zeros_like(d_a)

    @pl.loop(0, 3)
    def _(n):
        part = dqkv[:, wide(n)]
        gbuf[:, wide(n)] = dot(a_t[...], part).astype(BF)
        store(n).start()
        d_a[...] += dot_nt(part, w[:, wide(n)])

    u, scale = unit(xs[...].astype(F32))
    c = d_a[...]
    gvec[...] = gin[...]
    gvec[0:1, :] = jnp.sum(c * u, axis=0, keepdims=True)
    c = c * gain_a
    got_cf.wait()

    def norm_back(c, rows):
        ur = u[rows]
        return scale[rows] * (c - ur * jnp.mean(ur * c, axis=-1, keepdims=True))

    own = slice(64, 576)
    dxg[...] = norm_back(c[own] + cf[...], own) + g[...].astype(F32)
    halo[0:64, :] = norm_back(c[0:64], slice(0, 64)).astype(BF)
    halo[64:128, :] = norm_back(c[576:640], slice(576, 640)).astype(BF)
    stores.finish()
    for n in range(4):
        store(n).wait()


def slots_kernel(meta, routed, x, g, slots, st):
    me = meta[20]
    start = meta[me]
    token = lax.broadcasted_iota(jnp.int32, (512, 1024), 0) + 512 * me
    r = jnp.broadcast_to(routed[...], (512, 1024))
    rank = jnp.sum((r < token).astype(F32), axis=1, keepdims=True).astype(jnp.int32) - start
    hit = jnp.sum((r == token).astype(F32), axis=1, keepdims=True)
    row = ((start + rank) & 15) * 8 + (rank >> 4)
    row = jnp.where((hit > 0.5) & (rank < CAP), row, -1)
    lane = lax.broadcasted_iota(jnp.int32, (512, 128), 1)
    onehot = (lane == row).astype(F32).astype(BF)
    st[...] = onehot
    slots[:, 0:768] = dot_tn(onehot, x[...]).astype(BF)
    slots[:, 768:1536] = dot_tn(onehot, g[...]).astype(BF)


def entry_slots(meta):
    p = 16 * lax.broadcasted_iota(jnp.int32, (64, 128), 0) + meta[20]
    source, before = jnp.zeros_like(p), jnp.zeros_like(p)
    for d in range(1, 16):
        source = source + (p >= meta[d]).astype(jnp.int32)
        before = jnp.where(p >= meta[d], meta[d], before)
    rank = p - before
    lane = lax.broadcasted_iota(jnp.int32, (64, 128), 1)
    return ((lane == source * 8 + (rank >> 4)) & (rank < CAP)).astype(F32).astype(BF)


def entries_kernel(meta, got, own, many, kmask):
    entry = entry_of(lax.broadcasted_iota(jnp.int32, (1024, 128), 0))
    bias = jnp.zeros((1024, 128), F32)
    for d in range(16):
        bias = jnp.where((entry >= meta[d] + CAP) & (entry < meta[d + 1]), NEG, bias)
    kmask[:, 0:128] = jnp.where(entry < meta[17], bias, NEG)
    kmask[:, 128:256] = jnp.where(entry < meta[17], NEG, bias)
    rows = dot(entry_slots(meta), got[...]).astype(BF)
    own[...] = rows
    for t in range(16):
        many[t] = rows


def home_kernel(meta, parts, own_in, send_in, send, back, own, sems):
    copies = Copies(sems)
    got_own = copies.start(own_in, own)
    total = parts[0].astype(F32)
    for t in range(1, 16):
        total = total + parts[t].astype(F32)
    got_own.wait()
    u, scale = unit(own[:, 0:768].astype(F32))
    c = total[:, 768:1536]
    dxr = scale * (c - u * jnp.mean(u * c, axis=-1, keepdims=True))
    onehot = entry_slots(meta)
    back[:, 0:768] = dot_tn(onehot, total[:, 0:768].astype(BF)).astype(BF)
    back[:, 768:1536] = dot_tn(onehot, dxr.astype(BF)).astype(BF)
    copies.start(back, send.at[:, S_BACK:S_ALL]).wait()


def entry_of(row):
    return ((row & 63) << 4) + (row >> 6)


def heavy_kernel(
    meta, xg_in, hw_in, wall, kmask_in, gin, vrows, rest_in,
    parts, rest,
    xg, w, wd, wo, ar, fr, q, k, v, o, do, dqkv, dk, dv, kmask, da, dgu, hid, sa, sf, la,
    hw, wo_pad, pbuf, gbuf, gvec, in_sems, out_sems,
):
    loads, stores = Copies(in_sems), Copies(out_sems)
    got_hw = loads.start(hw_in, hw)
    got_wo = loads.start(wall.at[:, C_HO : C_HO + 768], wo_pad)
    got_xg = loads.start(xg_in, xg)
    got_kmask = loads.start(kmask_in, kmask)
    pick = pick6(96, 128)
    gain_a, gain_f, r_a, r_f = (vrows[n : n + 1, :] for n in range(4))
    got_hw.wait()
    for b in range(8):
        w[96 * b : 96 * b + 96, :] = dot(pick, hw[b, 0:128, :]).astype(BF)
        wd[32 * b : 32 * b + 32, :] = hw[b, 128:160, 0:768]
    got_wo.wait()
    low, head = meta[18], meta[19]
    head_row = lax.broadcasted_iota(jnp.int32, (128, 1024), 0) >> 6
    mine = jnp.where(head_row == head, pick6(128, 1024, low).astype(F32), 0.0).astype(BF)
    wo[...] = dot(mine, wo_pad[...]).astype(BF)
    on = (lax.broadcasted_iota(jnp.int32, (256, 128), 1) >> 6) == head
    got_xg.wait()

    @pl.loop(0, 4)
    def _(b):
        rows = pl.ds(pl.multiple_of(256 * b, 256), 256)
        u, _ = unit(xg[rows, 0:768].astype(F32))
        arb, frb = (u * gain_a).astype(BF), (u * gain_f).astype(BF)
        ar[rows, :], fr[rows, :] = arb, frb
        sab = jax.nn.sigmoid(jnp.sum(arb.astype(F32) * r_a, axis=-1, keepdims=True))
        sfb = jax.nn.sigmoid(jnp.sum(frb.astype(F32) * r_f, axis=-1, keepdims=True))
        sa[rows, :], sf[rows, :] = sab, sfb
        qkv = dot(arb, w[:, 512:896])
        q[rows, :] = jnp.where(on, qkv[:, 0:128], 0.0).astype(BF)
        k[rows, :] = qkv[:, 128:256].astype(BF)
        v[rows, :] = jnp.where(on, qkv[:, 256:384], 0.0).astype(BF)
        dab = (sab * xg[rows, 768:1536].astype(F32)).astype(BF)
        da[rows, :] = dab
        do[rows, :] = dot_nt(dab, wo[...]).astype(BF)

    got_kmask.wait()
    n0 = meta[17]
    dk[...] = jnp.zeros_like(dk)
    dv[...] = jnp.zeros_like(dv)

    @pl.loop(0, 4, unroll=2)
    def _(b):
        rows = pl.ds(pl.multiple_of(256 * b, 256), 256)
        first = entry_of(lax.broadcasted_iota(jnp.int32, (1, 128), 1) + 256 * b) < n0
        second = entry_of(lax.broadcasted_iota(jnp.int32, (1, 128), 1) + 256 * b + 128) < n0
        bias = jnp.concatenate(
            [jnp.where(first, kmask[:, 0:128], kmask[:, 128:256]),
             jnp.where(second, kmask[:, 0:128], kmask[:, 128:256])],
            axis=1,
        )
        qb, dob = q[rows, :], do[rows, :]
        s = dot_nt(k[...], qb) * HEAVY_SCALE + bias
        e = jnp.exp(s - jnp.max(s, axis=0, keepdims=True))
        p = e * (1.0 / jnp.sum(e, axis=0, keepdims=True))
        pb = p.astype(BF)
        ob = dot_tn(pb, v[...]).astype(BF)
        o[rows, :] = ob
        la[rows, :] = (1.0 - sa[rows, :]) * jnp.sum(
            ob.astype(F32) * dob.astype(F32), axis=-1, keepdims=True
        )
        dp = dot_nt(v[...], dob)
        ds = (p * (dp - jnp.sum(p * dp, axis=0, keepdims=True))).astype(BF)
        dqkv[rows, 0:128] = jnp.where(on, dot_tn(ds, k[...]) * HEAVY_SCALE, 0.0).astype(BF)
        dk[...] += dot(ds, qb) * HEAVY_SCALE
        dv[...] += dot(pb, dob)

    dqkv[:, 128:256] = dk[...].astype(BF)
    dqkv[:, 256:384] = dv[...].astype(BF)
    gbuf[:, 512:896] = dot_tn(ar[...], dqkv[...]).astype(BF)
    gbuf[:, R_HO - R_HEAVY : R_VEC - R_HEAVY] = jnp.zeros((768, 768), BF)
    gbuf[pl.ds(pl.multiple_of(low, 128), 128), R_HO - R_HEAVY : R_VEC - R_HEAVY] = dot_tn(o[...], da[...]).astype(BF)
    at = R_HEAVY
    stores.send(gbuf.at[:, 512 : R_VEC - at], rest.at[:, at + 512 : R_VEC])
    gvec[...] = gin[...]

    def send_parts(b):
        rows = pl.ds(pl.multiple_of(256 * b, 256), 256)
        return pltpu.make_async_copy(pbuf.at[rows, :], parts.at[rows, :], out_sems.at[3 + b])

    @pl.loop(0, 4, unroll=2)
    def _(b):
        rows = pl.ds(pl.multiple_of(256 * b, 256), 256)
        frb = fr[rows, :]
        sfb = sf[rows, :]
        dfb = (sfb * xg[rows, 768:1536].astype(F32)).astype(BF)
        both = dot(frb, w[:, 0:512])
        act, slope = gelu_parts(both[:, 0:256])
        up = both[:, 256:512]
        hidden = (act * up).astype(BF)
        hid[rows, :] = hidden
        dh = dot_nt(dfb, wd[...])
        lfb = (1.0 - sfb) * jnp.sum(hidden.astype(F32) * dh, axis=-1, keepdims=True)
        dgub = jnp.concatenate([(dh * up * slope).astype(BF), (dh * act).astype(BF)], axis=1)
        dgu[rows, :] = dgub
        y = sa[rows, :] * dot(o[rows, :], wo[...]) + sfb * dot(hidden, wd[...])
        lab = la[rows, :]
        d_f = dot_nt(dgub, w[:, 0:512]) + lfb * r_f
        d_a = dot_nt(dqkv[rows, :], w[:, 512:896]) + lab * r_a
        u, _ = unit(xg[rows, 0:768].astype(F32))
        gvec[0:1, :] += jnp.sum(d_a * u, axis=0, keepdims=True)
        gvec[1:2, :] += jnp.sum(d_f * u, axis=0, keepdims=True)
        gvec[2:3, :] += jnp.sum(lab * ar[rows, :].astype(F32), axis=0, keepdims=True)
        gvec[3:4, :] += jnp.sum(lfb * frb.astype(F32), axis=0, keepdims=True)
        da[rows, :] = dfb
        pbuf[rows, 0:768] = y.astype(BF)
        pbuf[rows, 768:1536] = (d_a * gain_a + d_f * gain_f).astype(BF)
        send_parts(b).start()

    gbuf[:, 0:512] = dot_tn(fr[...], dgu[...]).astype(BF)
    stores.send(gbuf.at[:, 0:512], rest.at[:, at : at + 512])
    vecs = jnp.concatenate([gvec[...], jnp.zeros((120, 768), F32)], axis=0)
    gbuf[:, R_VEC - R_HEAVY : R_DOWN - R_HEAVY] = vecs.T.astype(BF)
    gd = dot_tn(hid[...], da[...]).astype(BF)
    for r in range(8):
        for t in range(3):
            gbuf[96 * r + 32 * t : 96 * r + 32 * t + 32, R_DOWN - R_HEAVY : R_ALL - R_HEAVY] = gd[
                32 * r : 32 * r + 32, 256 * t : 256 * t + 256
            ]
    stores.send(gbuf.at[:, R_VEC - at : R_ALL - at], rest.at[:, R_VEC:R_ALL])
    stores.finish()
    for b in range(4):
        send_parts(b).wait()


def tokens_kernel(got, st, lo, dxg, hl, hr, out, grad):
    back = dot(st[...], got[:, :, S_BACK:S_ALL].reshape(128, 1536))
    out[...] = (lo[...] + back[:, 0:768]).astype(BF)
    dx = dxg[...] + back[:, 768:1536]
    grad[0:64, :] = (dx[0:64, :] + hl[...].astype(F32)).astype(BF)
    grad[64:448, :] = dx[64:448, :].astype(BF)
    grad[448:512, :] = (dx[448:512, :] + hr[...].astype(F32)).astype(BF)


def tail_rows(block, low):
    last = jnp.concatenate([block[32 * t : 32 * t + 32, low + 768 : low + 1024] for t in range(3)], axis=1)
    return jnp.concatenate([block[:, low : low + 768], last], axis=0)


def owner_rows(r, cols):
    quarter = cols // 4
    row = lax.broadcasted_iota(jnp.int32, (128, 96), 0)
    col = lax.broadcasted_iota(jnp.int32, (128, 96), 1)
    device, low = 6 * (row >> 3), row & 7
    main = ((low < 6) & (col == device + low)).astype(F32).astype(BF)
    tail = r[:, 3 * quarter : cols]
    pieces = []
    for t in range(3):
        extra = ((low >= 6) & (col == device + 3 * (low - 6) + t)).astype(F32).astype(BF)
        pieces.append((dot(main, r[:, quarter * t : quarter * t + quarter]) + dot(extra, tail)).astype(BF))
    return jnp.concatenate(pieces, axis=1)


def tail_of(block):
    cols = block.shape[1] // 3
    return jnp.concatenate(
        [block[6 + n : 7 + n, cols * t : cols * t + cols] for n in range(2) for t in range(3)], axis=0
    )


def spread_ffn_kernel(r, send, rows, sems):
    rows[:, 0:S_DOWN] = owner_rows(r, F_DOWN)
    rows[:, S_DOWN:S_REST] = tail_rows(r[...], F_DOWN)
    Copies(sems).start(rows, send.at[:, 0:S_REST]).wait()


def spread_rest_kernel(r, send_in, send, hd, rows, sems):
    rows[...] = owner_rows(r, R_ALL)
    copy = Copies(sems).start(rows, send.at[:, S_REST:S_BACK])
    hd[...] = jnp.concatenate([r[32 * t : 32 * t + 32, R_DOWN:R_ALL] for t in range(3)], axis=1)
    copy.wait()


def sum_parts(got, a, b):
    t = got[0, :, a:b].astype(F32)
    for d in range(1, 16):
        t = t + got[d, :, a:b].astype(F32)
    return t


def sum_ffn_kernel(got, gate, up, down):
    both = sum_parts(got, 0, S_DOWN)
    for c in range(3):
        gate[:, 256 * c : 256 * c + 256] = both[0:6, 512 * c : 512 * c + 256]
        up[:, 256 * c : 256 * c + 256] = both[0:6, 512 * c + 256 : 512 * c + 512]
    both = tail_of(both)
    gate[:, 768:1024] = both[:, 0:256]
    up[:, 768:1024] = both[:, 256:512]
    down[...] = sum_parts(got, S_DOWN, S_REST)


def sum_rest_kernel(got, q, k, v, o, hq, hk, hv, ho, hgate, hup, vecs):
    total = sum_parts(got, S_REST, S_BACK)
    for n, ref in enumerate((q, k, v, o)):
        ref[...] = total[0:6, 768 * n : 768 * n + 768]
    rest = tail_of(total)
    ho[...] = rest[:, 128:896]
    rows = jnp.concatenate([rest[:, 896:1024], jnp.zeros((122, 128), F32)], axis=0).T
    for n, ref in enumerate(vecs):
        ref[...] = rows[n : n + 1, 0:6]
    at = S_REST + R_HEAVY
    for j in range(16):
        hgate[:, 256 * j : 256 * j + 256] = got[j, :, at : at + 256].astype(F32)[0:6]
        hup[:, 256 * j : 256 * j + 256] = got[j, :, at + 256 : at + 512].astype(F32)[0:6]
    at = at + 512
    for p in range(6):
        two = [got[2 * p + n, :, S_REST:S_BACK].astype(F32) for n in range(2)]
        pair = two[0][:, R_HEAVY + 512 : R_HEAVY + 768] + two[1][:, R_HEAVY + 512 : R_HEAVY + 768]
        hq[:, 128 * p : 128 * p + 128] = pair[0:6, 0:128]
        hk[:, 128 * p : 128 * p + 128] = pair[0:6, 128:256]
        hv[:, 128 * p : 128 * p + 128] = tail_of(two[0] + two[1])[:, 0:128]


def last_kernel(
    got, st, lo, dxg, hl, hr,
    out, grad, q, k, v, o, gate, up, down, hq, hk, hv, ho, hgate, hup, *vecs,
):
    tokens_kernel(got, st, lo, dxg, hl, hr, out, grad)
    sum_ffn_kernel(got, gate, up, down)
    sum_rest_kernel(got, q, k, v, o, hq, hk, hv, ho, hgate, hup, vecs)


def call(kernel, outs, args, scratch=(), in_specs=None, out_specs=None, sems=(), name=None, us=0.05, aliases={}):
    return pl.pallas_call(
        kernel,
        out_shape=[jax.ShapeDtypeStruct(s, t) for s, t in outs],
        in_specs=in_specs or [VMEM] * len(args),
        out_specs=out_specs or [VMEM] * len(outs),
        scratch_shapes=[pltpu.VMEM(s, t) for s, t in scratch]
        + [pltpu.SemaphoreType.DMA((n,)) for n in sems],
        compiler_params=PARAMS,
        cost_estimate=pl.CostEstimate(
            flops=int(us * 1.0e9), bytes_accessed=int(us * 3.0e6), transcendentals=0
        ),
        input_output_aliases=aliases,
        name=name,
    )(*args)


def run_light_ffn(tokens, cotangent, wall):
    return call(
        light_ffn_kernel,
        [((512, 768), F32), ((512, 768), F32), ((768, F_ALL), BF), ((8, 768), F32), ((8, 768), F32)],
        (tokens, cotangent, wall),
        [
            ((512, 768), BF), ((512, 768), BF),
            ((768, 512), BF), ((512, 768), BF), ((768, 512), BF), ((768, 3072), BF),
            ((1024, 2048), BF), ((1024, 768), BF), ((1024, 128), BF),
        ],
        [HBM, HBM, HBM],
        [VMEM, VMEM, HBM, VMEM, VMEM],
        sems=(11, 8),
        name="light_ffn",
        us=200,
    )


def run_light_attn(meta, xl, tokens, xr, cotangent, wall, ffn, cf, gvec, vrows):
    return call(
        light_attn_kernel,
        [
            ((512, 768), F32), ((512, 768), F32), ((128, 768), BF), ((768, R_ALL), BF), ((8, 768), F32),
        ],
        (meta, xl, tokens, xr, cotangent, wall, ffn, cf, gvec, vrows),
        [
            ((768, 3072), BF), ((640, 768), BF), ((640, 768), BF), ((768, 640), BF), ((640, 2304), BF),
            ((512, 768), BF), ((512, 768), BF), ((640, 2304), BF),
            ((640, 768), F32), ((640, 768), F32), ((4, 256, 256), F32),
            ((1024, 3072), BF), ((512, 768), BF), ((512, 768), F32), ((512, 768), F32),
            ((512, 768), F32), ((640, 768), F32), ((768, 3072), BF),
        ],
        [SMEM, VMEM, HBM, VMEM, HBM] + [HBM] * 3 + [VMEM, VMEM],
        [HBM, VMEM, VMEM, HBM, VMEM],
        sems=(8, 5),
        name="light_attn",
        us=2,
    )


def run_heavy(meta, xg, hw, wall, kmask, gvec, vrows, rest):
    col = ((1024, 1), F32)
    rows, narrow = ((1024, 768), BF), ((1024, 128), BF)
    return call(
        heavy_kernel,
        [((1024, 1536), BF), ((768, R_ALL), BF)],
        (meta, xg, hw, wall, kmask, gvec, vrows, rest),
        [
            ((1024, 1536), BF), ((768, 896), BF), ((256, 768), BF), ((128, 768), BF), rows, rows,
            narrow, narrow, narrow, narrow, narrow, ((1024, 384), BF),
            ((1024, 128), F32), ((1024, 128), F32), ((1024, 256), F32),
            rows, ((1024, 512), BF), ((1024, 256), BF), col, col, col,
            ((8, 160, 896), BF), rows, ((1024, 1536), BF), ((768, R_ALL - R_HEAVY), BF), ((8, 768), F32),
        ],
        [SMEM, HBM, HBM, HBM, HBM, VMEM, VMEM, HBM],
        [HBM, HBM],
        sems=(4, 7),
        aliases={7: 1},
        name="heavy",
        us=200,
    )


def body(
    tokens, lengths, routed, cotangent, gain_attn, gain_ffn, router_attn, router_ffn,
    light_q, light_k, light_v, light_o, light_gate, light_up, light_down,
    heavy_q, heavy_k, heavy_v, heavy_o, heavy_gate, heavy_up, heavy_down,
):
    me = lax.axis_index("fsdp")
    vectors = [v.reshape(1, 6) for v in (gain_attn, gain_ffn, router_attn, router_ffn)]
    pack, hsend, hd = call(
        prep_kernel,
        [((8, C_ALL), BF), ((16, 8, 896), BF), ((32, 768), BF)],
        (
            light_q, light_k, light_v, light_o, light_gate, light_up, light_down,
            heavy_q, heavy_k, heavy_v, heavy_o, heavy_gate, heavy_up, heavy_down, *vectors,
        ),
        [((8, 4096), F32), ((128, 128), F32)],
        name="prep",
    )
    wall = lax.all_gather(pack, ALL, axis=0, tiled=True)

    hcols = lax.all_to_all(hsend, "fsdp", split_axis=0, concat_axis=0, tiled=True)
    hd = lax.ppermute(hd, ALL, [(d, (d % 8) * 16 + d // 8) for d in range(128)])
    hblock = jnp.concatenate([hcols.reshape(128, 896), jnp.pad(hd, ((0, 0), (0, 128)))], axis=0)

    edges = jnp.arange(17, dtype=jnp.int32) * 512
    bounds = jnp.sum((routed[0][None, :] < edges[:, None]).astype(jnp.int32), axis=1)
    dp = lax.axis_index("dp")
    pair = jnp.where(me < 12, me // 2, 5)
    meta = jnp.concatenate(
        [
            bounds,
            jnp.stack(
                [
                    lengths[0, 0] // 8, 128 * pair, jnp.where(me < 12, me % 2, 2),
                    me, dp // 2, dp % 2, lengths[0, 0],
                ]
            ),
        ]
    )

    def swap(rows):
        return lax.all_to_all(rows, "fsdp", split_axis=0, concat_axis=0, tiled=True)

    slots, st = call(
        slots_kernel,
        [((128, 1536), BF), ((512, 128), BF)],
        (meta, routed, tokens, cotangent),
        in_specs=[SMEM, VMEM, VMEM, VMEM],
        name="slots",
    )
    own, many, kmask = call(
        entries_kernel,
        [((64, 1536), BF), ((16, 64, 1536), BF), ((1024, 256), F32)],
        (meta, swap(slots.reshape(16, 8, 1536)).reshape(128, 1536)),
        in_specs=[SMEM, VMEM],
        name="entries",
    )
    right = [(i, i + 1) for i in range(15)]
    left = [(i + 1, i) for i in range(15)]
    xl = lax.ppermute(tokens[448:512], "fsdp", right)
    xr = lax.ppermute(tokens[0:64], "fsdp", left)

    wall, many, xl, xr, hblock = lax.optimization_barrier((wall, many, xl, xr, hblock))
    hw = lax.all_gather(hblock, "dp", axis=0, tiled=False)
    xg = swap(many).reshape(1024, 1536)
    ffn, cf, grad_ffn, gvec, vrows = run_light_ffn(tokens, cotangent, wall)
    rs_ffn = lax.psum_scatter(grad_ffn, "dp", scatter_dimension=0, tiled=True)
    lmeta = jnp.stack([lengths[0, 0], me * 512, jnp.int32(8192)])
    lo, dxg, halo, rest, gvec = run_light_attn(
        lmeta, xl, tokens, xr, cotangent, wall, ffn, cf, gvec, vrows
    )
    parts, rest = run_heavy(meta, xg, hw, wall, kmask, gvec, vrows, rest)
    rs_rest = lax.psum_scatter(rest, "dp", scatter_dimension=0, tiled=True)
    hr = lax.ppermute(halo[0:64], "fsdp", left)
    hl = lax.ppermute(halo[64:128], "fsdp", right)
    (send,) = call(
        spread_ffn_kernel,
        [((128, S_ALL), BF)],
        (rs_ffn,),
        [((128, S_REST), BF)],
        out_specs=[HBM],
        sems=(1,),
        name="spread_ffn",
    )
    parts = swap(parts.reshape(16, 64, 1536))
    parts, send, hr, hl = lax.optimization_barrier((parts, send, hr, hl))
    (send,) = call(
        home_kernel,
        [((128, S_ALL), BF)],
        (meta, parts, own, send),
        [((128, 1536), BF), ((64, 1536), BF)],
        [SMEM, VMEM, HBM, HBM],
        [HBM],
        sems=(2,),
        name="home",
        aliases={3: 0},
    )
    send, g_hd = call(
        spread_rest_kernel,
        [((128, S_ALL), BF), ((32, 768), BF)],
        (rs_rest, send),
        [((128, S_BACK - S_REST), BF)],
        [VMEM, HBM],
        [HBM, VMEM],
        sems=(1,),
        name="spread_rest",
        aliases={1: 0},
    )
    g_hd = lax.ppermute(g_hd, ALL, [((d % 8) * 16 + d // 8, d) for d in range(128)])
    got = swap(send.reshape(16, 8, S_ALL))
    six, four, big = ((6, 768), F32), ((6, 1024), F32), ((6, 4096), F32)
    (
        output, grad_tokens, g_q, g_k, g_v, g_o, g_gate, g_up, g_down,
        g_hq, g_hk, g_hv, g_ho, g_hgate, g_hup, *g_vecs,
    ) = call(
        last_kernel,
        [((512, 768), BF), ((512, 768), BF)] + [six] * 4 + [four, four, ((8, 768), F32)]
        + [six] * 4 + [big, big] + [((1, 6), F32)] * 4,
        (got, st, lo, dxg, hl, hr),
        name="last",
    )
    return (
        output, grad_tokens,
        *[v.reshape(6) for v in g_vecs],
        g_q, g_k, g_v, g_o, g_gate, g_up, g_down,
        g_hq, g_hk, g_hv, g_ho, g_hgate, g_hup, g_hd.astype(F32),
    )


def solution(mesh):
    rows = P(ALL, None)
    flat = P(ALL)
    in_specs = (rows, P("dp", None), P("dp", None), rows) + (flat,) * 4 + (rows,) * 14
    out_specs = (rows, rows) + (flat,) * 4 + (rows,) * 14
    return jax.shard_map(body, mesh=mesh, in_specs=in_specs, out_specs=out_specs, check_vma=False)
```

profile of v0, /device:TPU:3, one launch (start us, length us, event | category | flops | bytes accessed | tf_op | source)
XLA Modules:
  0.0 272.5 jit_solution(595166042629616436)
XLA Ops:
  7.2 0.0 all-gather.4.cloned.1.call-start
  7.3 2.0 prep.1
  9.3 0.0 all-gather.4.cloned.1.call-update
  9.3 6.9 %all-to-all-start.1 = ((bf16[16,8,896]{2,1,0:T(8,128)(2,1)}), bf16[16,8,896]{2,1,0:T(8,128)(2,1)S(1)}, u32[]{:S(2)}, u32[]{:S(2)}) async-start(bf16[16,8,896]{2,1,0:T(8,128)(2,1)} %get-tuple-element.73), calls=%async_computation.1 | async-start | bytes 458752 | tf_op jit(solution)/shard_map/all_to_all | solution.py:737
  18.9 0.9 convert_reduce_fusion
  19.8 1.3 concatenate.6.meta
  21.0 3.0 %slots.1 = (bf16[128,1536]{1,0:T(8,128)(2,1)}, bf16[512,128]{1,0:T(8,128)(2,1)}) custom-call(s32[24]{0:T(128)} %concatenate.6.meta, s32[1,1024]{1,0:T(1,128)} %routed.1, bf16[512,768]{1,0:T(8,128)(2,1)} %x_in.3, bf16[512,768]{1,0:T(8,128)(2,1)} %g_in.3), custom_call_target="tpu_custom_call" | custom-call | flops 50000000 | bytes 150000 | tf_op jit(solution)/shard_map/slots/pallas_call | solution.py:639
  24.1 6.7 %all-to-all-start = ((bf16[16,8,1536]{2,1,0:T(8,128)(2,1)}), bf16[16,8,1536]{2,1,0:T(8,128)(2,1)S(1)}, u32[]{:S(2)}, u32[]{:S(2)}) async-start(bf16[16,8,1536]{2,1,0:T(8,128)(2,1)} %bitcast.30), calls=%async_computation | async-start | bytes 786432 | tf_op jit(solution)/shard_map/all_to_all | solution.py:758
  30.7 0.0 all-gather.6.cloned.1.call-start
  30.8 1.0 fusion.2
  31.7 4.3 %collective-permute-start.1 = (bf16[64,768]{1,0:T(8,128)(2,1)S(1)}, bf16[64,768]{1,0:T(8,128)(2,1)S(1)}, u32[]{:S(2)}, u32[]{:S(2)}) collective-permute-start(bf16[64,768]{1,0:T(8,128)(2,1)S(1)} %get-tuple-element.120), channel_id=1, source_target_pairs={{1,0},{2,1},{3,2},{4,3},{5,4},{6,5},{7,6},{8,7},{9,8},{10,9},{11,1... | collective-permute-start | bytes 294920 | tf_op jit(solution)/shard_map/ppermute | solution.py:777
  36.0 1.9 collective-permute-start
  38.0 9.2 %collective-permute-start.2 = (bf16[32,768]{1,0:T(8,128)(2,1)S(1)}, bf16[32,768]{1,0:T(8,128)(2,1)S(1)}, u32[]{:S(2)}, u32[]{:S(2)}) collective-permute-start(bf16[32,768]{1,0:T(8,128)(2,1)S(1)} %copy-done.9), channel_id=1, source_target_pairs={{0,0},{1,16},{2,32},{3,48},{4,64},{5,80},{6,96},{7,112},{8,1},{9,1... | collective-permute-start | bytes 147464 | tf_op jit(solution)/shard_map/ppermute | solution.py:738
  47.2 0.6 pad_add_fusion.meta
  47.8 0.5 collective-permute-done.2
  48.4 0.7 fusion.1
  49.1 0.7 copy-done.2
  49.8 3.8 %entries.1 = (bf16[64,1536]{1,0:T(8,128)(2,1)}, bf16[16,64,1536]{2,1,0:T(8,128)(2,1)}, f32[1024,256]{1,0:T(8,128)}) custom-call(s32[24]{0:T(128)} %concatenate.6.meta, bf16[128,1536]{1,0:T(8,128)(2,1)} %bitcast.28), custom_call_target="tpu_custom_call" | custom-call | flops 50000000 | bytes 150000 | tf_op jit(solution)/shard_map/entries/pallas_call | solution.py:639
  53.7 0.0 copy-start.5
  53.7 38.6 %all-gather.4.cloned.1.call-done.wall = bf16[1024,6784]{1,0:T(8,128)(2,1)} async-done(((bf16[8,6784]{1,0:T(8,128)(2,1)}), bf16[1024,6784]{1,0:T(8,128)(2,1)}) %all-gather.4.cloned.1.call-update) | async-done | bytes 13893648 | tf_op jit(solution)/shard_map/all_gather | solution.py:735
  92.2 0.0 all-gather.6.cloned.1.call-update
  92.3 6.7 %all-to-all-start.2 = ((bf16[16,64,1536]{2,1,0:T(8,128)(2,1)}), bf16[16,64,1536]{2,1,0:T(8,128)(2,1)}, u32[]{:S(2)}, u32[]{:S(2)}) async-start(bf16[16,64,1536]{2,1,0:T(8,128)(2,1)} %get-tuple-element.75), calls=%async_computation.2 | async-start | bytes 6291456 | tf_op jit(solution)/shard_map/all_to_all | solution.py:758
  99.0 0.0 reduce-scatter.5.cloned.1.call-start
  99.1 14.3 %light_ffn.1 = (f32[512,768]{1,0:T(8,128)}, f32[512,768]{1,0:T(8,128)}, bf16[768,3072]{1,0:T(8,128)(2,1)}, f32[8,768]{1,0:T(8,128)}, f32[8,768]{1,0:T(8,128)}) custom-call(bf16[512,768]{1,0:T(8,128)(2,1)} %x_in.3, bf16[512,768]{1,0:T(8,128)(2,1)} %g_in.3, bf16[1024,6784]{1,0:T(8,128)(2,1)} %all-gather.4.cloned.1.call-done.wall), custom_call_target="tpu_custom_call" | custom-call | flops 199999995904 | bytes 600000000 | tf_op jit(solution)/shard_map/light_ffn/pallas_call | solution.py:639
  113.3 0.0 reduce-scatter.5.cloned.1.call-update
  113.4 0.2 reduce-scatter.3.cloned.1.call-start
  113.6 26.6 %light_attn.1 = (f32[512,768]{1,0:T(8,128)}, f32[512,768]{1,0:T(8,128)}, bf16[128,768]{1,0:T(8,128)(2,1)}, bf16[768,5120]{1,0:T(8,128)(2,1)}, f32[8,768]{1,0:T(8,128)}) custom-call(s32[3]{0:T(128)} %pad_add_fusion.meta, bf16[64,768]{1,0:T(8,128)(2,1)} %copy-done.5, bf16[512,768]{1,0:T(8,128)(2,1)} %x_in.3, bf16[64,768]{1,0:T(8,128)(2,1)} %copy-done.4, ...), custom_call_target="tpu_custom_call" | custom-call | flops 2000000000 | bytes 6000000 | tf_op jit(solution)/shard_map/light_attn/pallas_call | solution.py:639
  140.2 0.0 all-gather.6.cloned.1.call-done
  140.3 23.3 %heavy.1 = (bf16[1024,1536]{1,0:T(8,128)(2,1)}, bf16[768,5120]{1,0:T(8,128)(2,1)}) custom-call(s32[24]{0:T(128)} %concatenate.6.meta, bf16[1024,1536]{1,0:T(8,128)(2,1)} %bitcast.16.xg_in, bf16[8,160,896]{2,1,0:T(8,128)(2,1)} %bitcast.42, bf16[1024,6784]{1,0:T(8,128)(2,1)} %all-gather.4.cloned.1.call-done.wall, ...), custom_call_target="tpu_custom_call", output_to_operand_aliasing={{1}: (7, {})} | custom-call | flops 199999995904 | bytes 600000000 | tf_op jit(solution)/shard_map/heavy/pallas_call | solution.py:639
  163.6 0.0 reduce-scatter.3.cloned.1.call-update
  163.6 0.0 copy-start.3
  163.6 11.0 %all-to-all-start.3 = ((bf16[16,64,1536]{2,1,0:T(8,128)(2,1)}), bf16[16,64,1536]{2,1,0:T(8,128)(2,1)S(1)}, u32[]{:S(2)}, u32[]{:S(2)}) async-start(bf16[16,64,1536]{2,1,0:T(8,128)(2,1)} %bitcast.27), calls=%async_computation.4 | async-start | bytes 6291456 | tf_op jit(solution)/shard_map/all_to_all | solution.py:758
  174.7 3.1 %collective-permute-start.4 = (bf16[64,768]{1,0:T(8,128)(2,1)S(1)}, bf16[64,768]{1,0:T(8,128)(2,1)S(1)}, u32[]{:S(2)}, u32[]{:S(2)}) collective-permute-start(bf16[64,768]{1,0:T(8,128)(2,1)S(1)} %get-tuple-element.122), channel_id=1, source_target_pairs={{0,1},{1,2},{2,3},{3,4},{4,5},{5,6},{6,7},{7,8},{8,9},{9,10},{10,1... | collective-permute-start | bytes 294920 | tf_op jit(solution)/shard_map/ppermute | solution.py:791
  177.8 4.3 %collective-permute-start.3 = (bf16[64,768]{1,0:T(8,128)(2,1)S(1)}, bf16[64,768]{1,0:T(8,128)(2,1)S(1)}, u32[]{:S(2)}, u32[]{:S(2)}) collective-permute-start(bf16[64,768]{1,0:T(8,128)(2,1)S(1)} %get-tuple-element.123), channel_id=1, source_target_pairs={{1,0},{2,1},{3,2},{4,3},{5,4},{6,5},{7,6},{8,7},{9,8},{10,9},{11,1... | collective-permute-start | bytes 294920 | tf_op jit(solution)/shard_map/ppermute | solution.py:790
  182.1 0.0 reduce-scatter.5.cloned.1.call-done.r
  182.1 2.3 spread_ffn.1.send_in
  184.4 27.8 %collective-permute-done.4.hl = bf16[64,768]{1,0:T(8,128)(2,1)S(1)} collective-permute-done((bf16[64,768]{1,0:T(8,128)(2,1)S(1)}, bf16[64,768]{1,0:T(8,128)(2,1)S(1)}, u32[]{:S(2)}, u32[]{:S(2)}) %collective-permute-start.4) | collective-permute-done | bytes 98336 | tf_op jit(solution)/shard_map/ppermute | solution.py:791
  212.2 1.6 copy-done
  213.9 4.1 %home.1.send_in = bf16[128,7680]{1,0:T(8,128)(2,1)} custom-call(s32[24]{0:T(128)} %concatenate.6.meta, bf16[16,64,1536]{2,1,0:T(8,128)(2,1)} %copy-done, bf16[64,1536]{1,0:T(8,128)(2,1)} %get-tuple-element.92.own_in, bf16[128,7680]{1,0:T(8,128)(2,1)} %spread_ffn.1.send_in), custom_call_target="tpu_custom_call", output_to_operand_aliasing={{}: (3, {})} | custom-call | flops 50000000 | bytes 150000 | tf_op jit(solution)/shard_map/home/pallas_call | solution.py:639
  218.0 0.0 reduce-scatter.3.cloned.1.call-done.r
  218.0 3.5 %spread_rest.1 = (bf16[128,7680]{1,0:T(8,128)(2,1)}, bf16[32,768]{1,0:T(8,128)(2,1)}) custom-call(bf16[96,5120]{1,0:T(8,128)(2,1)} %reduce-scatter.3.cloned.1.call-done.r, bf16[128,7680]{1,0:T(8,128)(2,1)} %home.1.send_in), custom_call_target="tpu_custom_call", output_to_operand_aliasing={{0}: (1, {})} | custom-call | flops 50000000 | bytes 150000 | tf_op jit(solution)/shard_map/spread_rest/pallas_call | solution.py:639
  221.5 0.0 copy-start.10
  221.5 9.3 %all-to-all-start.4 = ((bf16[16,8,7680]{2,1,0:T(8,128)(2,1)}), bf16[16,8,7680]{2,1,0:T(8,128)(2,1)S(1)}, u32[]{:S(2)}, u32[]{:S(2)}) async-start(bf16[16,8,7680]{2,1,0:T(8,128)(2,1)} %bitcast.26), calls=%async_computation.6 | async-start | bytes 3932160 | tf_op jit(solution)/shard_map/all_to_all | solution.py:758
  230.8 5.9 %collective-permute-start.5 = (bf16[32,768]{1,0:T(8,128)(2,1)S(1)}, bf16[32,768]{1,0:T(8,128)(2,1)S(1)}, u32[]{:S(2)}, u32[]{:S(2)}) collective-permute-start(bf16[32,768]{1,0:T(8,128)(2,1)S(1)} %copy-done.10), channel_id=1, source_target_pairs={{0,0},{16,1},{32,2},{48,3},{64,4},{80,5},{96,6},{112,7},{1,8},{17,... | collective-permute-start | bytes 147464 | tf_op jit(solution)/shard_map/ppermute | solution.py:825
  236.8 22.9 %collective-permute-done.5 = bf16[32,768]{1,0:T(8,128)(2,1)S(1)} collective-permute-done((bf16[32,768]{1,0:T(8,128)(2,1)S(1)}, bf16[32,768]{1,0:T(8,128)(2,1)S(1)}, u32[]{:S(2)}, u32[]{:S(2)}) %collective-permute-start.5) | collective-permute-done | bytes 49184 | tf_op jit(solution)/shard_map/ppermute | solution.py:825
  259.6 0.6 convert_element_type.9
  260.3 1.3 copy-done.1
  261.6 4.4 %last.1 = (bf16[512,768]{1,0:T(8,128)(2,1)}, bf16[512,768]{1,0:T(8,128)(2,1)}, f32[6,768]{1,0:T(8,128)}, f32[6,768]{1,0:T(8,128)}, f32[6,768]{1,0:T(8,128)}, /*i...) custom-call(bf16[16,8,7680]{2,1,0:T(8,128)(2,1)} %copy-done.1, ...), custom_call_target="tpu_custom_call" | custom-call | flops 50000000 | bytes 150000 | tf_op jit(solution)/shard_map/last/pallas_call | solution.py:639
  (26 shorter events, 0.1 us)
Async XLA Ops:
  7.2 40.0 %copy-start.8 = (s32[1,2]{1,0:T(1,128)S(1)}, s32[1,2]{1,0:T(1,128)}, u32[]{:S(2)}) copy-start(s32[1,2]{1,0:T(1,128)} %param.23) | copy-start | bytes 28
  7.2 85.0 %all-gather.4.cloned.1.call-start = ((), (), s32[]{:S(2)}) async-start(), calls=%async_computation.7 | async-start | bytes 14002176 | tf_op jit(solution)/shard_map/all_gather | solution.py:735
  9.3 28.7 %copy-start.9 = (bf16[32,768]{1,0:T(8,128)(2,1)S(1)}, bf16[32,768]{1,0:T(8,128)(2,1)}, u32[]{:S(2)}) copy-start(bf16[32,768]{1,0:T(8,128)(2,1)} %get-tuple-element.74) | copy-start | bytes 147460
  9.3 14.7 %all-to-all-start.1 = ((bf16[16,8,896]{2,1,0:T(8,128)(2,1)}), bf16[16,8,896]{2,1,0:T(8,128)(2,1)S(1)}, u32[]{:S(2)}, u32[]{:S(2)}) async-start(bf16[16,8,896]{2,1,0:T(8,128)(2,1)} %get-tuple-element.73), calls=%async_computation.1 | async-start | bytes 458752 | tf_op jit(solution)/shard_map/all_to_all | solution.py:737
  24.1 25.0 %all-to-all-start = ((bf16[16,8,1536]{2,1,0:T(8,128)(2,1)}), bf16[16,8,1536]{2,1,0:T(8,128)(2,1)S(1)}, u32[]{:S(2)}, u32[]{:S(2)}) async-start(bf16[16,8,1536]{2,1,0:T(8,128)(2,1)} %bitcast.30), calls=%async_computation | async-start | bytes 786432 | tf_op jit(solution)/shard_map/all_to_all | solution.py:758
  30.7 109.5 %all-gather.6.cloned.1.call-start = ((), (), s32[]{:S(2)}) async-start(), calls=%async_computation.10 | async-start | bytes 2580480 | tf_op jit(solution)/shard_map/all_gather | solution.py:780
  31.7 21.9 %collective-permute-start.1 = (bf16[64,768]{1,0:T(8,128)(2,1)S(1)}, bf16[64,768]{1,0:T(8,128)(2,1)S(1)}, u32[]{:S(2)}, u32[]{:S(2)}) collective-permute-start(bf16[64,768]{1,0:T(8,128)(2,1)S(1)} %get-tuple-element.120), channel_id=1, source_target_pairs={{1,0},{2,1},{3,2},{4,3},{5,4},{6,5},{7,6},{8,7},{9,8},{10,9},{11,1... | collective-permute-start | bytes 294920 | tf_op jit(solution)/shard_map/ppermute | solution.py:777
  36.0 17.6 %collective-permute-start = (bf16[64,768]{1,0:T(8,128)(2,1)S(1)}, bf16[64,768]{1,0:T(8,128)(2,1)S(1)}, u32[]{:S(2)}, u32[]{:S(2)}) collective-permute-start(bf16[64,768]{1,0:T(8,128)(2,1)S(1)} %get-tuple-element.121), channel_id=1, source_target_pairs={{0,1},{1,2},{2,3},{3,4},{4,5},{5,6},{6,7},{7,8},{8,9},{9,10},{10,1... | collective-permute-start | bytes 294920 | tf_op jit(solution)/shard_map/ppermute | solution.py:776
  38.0 10.4 %collective-permute-start.2 = (bf16[32,768]{1,0:T(8,128)(2,1)S(1)}, bf16[32,768]{1,0:T(8,128)(2,1)S(1)}, u32[]{:S(2)}, u32[]{:S(2)}) collective-permute-start(bf16[32,768]{1,0:T(8,128)(2,1)S(1)} %copy-done.9), channel_id=1, source_target_pairs={{0,0},{1,16},{2,32},{3,48},{4,64},{5,80},{6,96},{7,112},{8,1},{9,1... | collective-permute-start | bytes 147464 | tf_op jit(solution)/shard_map/ppermute | solution.py:738
  49.1 0.7 copy-start.2
  53.6 38.6 %copy-start.4 = (bf16[64,768]{1,0:T(8,128)(2,1)}, bf16[64,768]{1,0:T(8,128)(2,1)S(1)}, u32[]{:S(2)}) copy-start(bf16[64,768]{1,0:T(8,128)(2,1)S(1)} %collective-permute-done.1.xr) | copy-start | bytes 294916
  53.7 38.6 %copy-start.5 = (bf16[64,768]{1,0:T(8,128)(2,1)}, bf16[64,768]{1,0:T(8,128)(2,1)S(1)}, u32[]{:S(2)}) copy-start(bf16[64,768]{1,0:T(8,128)(2,1)S(1)} %collective-permute-done.xl) | copy-start | bytes 294916
  92.3 47.9 %all-to-all-start.2 = ((bf16[16,64,1536]{2,1,0:T(8,128)(2,1)}), bf16[16,64,1536]{2,1,0:T(8,128)(2,1)}, u32[]{:S(2)}, u32[]{:S(2)}) async-start(bf16[16,64,1536]{2,1,0:T(8,128)(2,1)} %get-tuple-element.75), calls=%async_computation.2 | async-start | bytes 6291456 | tf_op jit(solution)/shard_map/all_to_all | solution.py:758
  99.0 83.1 %reduce-scatter.5.cloned.1.call-start = ((), (), s32[]{:S(2)}) async-start(), calls=%async_computation.9 | async-start | bytes 5308416 | tf_op jit(solution)/shard_map/reduce_scatter | solution.py:783
  113.4 104.6 %reduce-scatter.3.cloned.1.call-start = ((), (), s32[]{:S(2)}) async-start(), calls=%async_computation.8 | async-start | bytes 8847360 | tf_op jit(solution)/shard_map/reduce_scatter | solution.py:789
  163.6 11.0 %copy-start.3 = (bf16[128,768]{1,0:T(8,128)(2,1)S(1)}, bf16[128,768]{1,0:T(8,128)(2,1)}, u32[]{:S(2)}) copy-start(bf16[128,768]{1,0:T(8,128)(2,1)} %get-tuple-element.90) | copy-start | bytes 589828
  163.6 48.6 %all-to-all-start.3 = ((bf16[16,64,1536]{2,1,0:T(8,128)(2,1)}), bf16[16,64,1536]{2,1,0:T(8,128)(2,1)S(1)}, u32[]{:S(2)}, u32[]{:S(2)}) async-start(bf16[16,64,1536]{2,1,0:T(8,128)(2,1)} %bitcast.27), calls=%async_computation.4 | async-start | bytes 6291456 | tf_op jit(solution)/shard_map/all_to_all | solution.py:758
  174.7 37.5 %collective-permute-start.4 = (bf16[64,768]{1,0:T(8,128)(2,1)S(1)}, bf16[64,768]{1,0:T(8,128)(2,1)S(1)}, u32[]{:S(2)}, u32[]{:S(2)}) collective-permute-start(bf16[64,768]{1,0:T(8,128)(2,1)S(1)} %get-tuple-element.122), channel_id=1, source_target_pairs={{0,1},{1,2},{2,3},{3,4},{4,5},{5,6},{6,7},{7,8},{8,9},{9,10},{10,1... | collective-permute-start | bytes 294920 | tf_op jit(solution)/shard_map/ppermute | solution.py:791
  177.8 34.4 %collective-permute-start.3 = (bf16[64,768]{1,0:T(8,128)(2,1)S(1)}, bf16[64,768]{1,0:T(8,128)(2,1)S(1)}, u32[]{:S(2)}, u32[]{:S(2)}) collective-permute-start(bf16[64,768]{1,0:T(8,128)(2,1)S(1)} %get-tuple-element.123), channel_id=1, source_target_pairs={{1,0},{2,1},{3,2},{4,3},{5,4},{6,5},{7,6},{8,7},{9,8},{10,9},{11,1... | collective-permute-start | bytes 294920 | tf_op jit(solution)/shard_map/ppermute | solution.py:790
  212.2 9.3 %copy-start.6 = (bf16[64,768]{1,0:T(8,128)(2,1)}, bf16[64,768]{1,0:T(8,128)(2,1)S(1)}, u32[]{:S(2)}) copy-start(bf16[64,768]{1,0:T(8,128)(2,1)S(1)} %collective-permute-done.4.hl) | copy-start | bytes 294916
  212.2 9.3 %copy-start.7 = (bf16[64,768]{1,0:T(8,128)(2,1)}, bf16[64,768]{1,0:T(8,128)(2,1)S(1)}, u32[]{:S(2)}) copy-start(bf16[64,768]{1,0:T(8,128)(2,1)S(1)} %collective-permute-done.3.hr) | copy-start | bytes 294916
  212.2 1.7 copy-start
  221.5 9.4 %copy-start.10 = (bf16[32,768]{1,0:T(8,128)(2,1)S(1)}, bf16[32,768]{1,0:T(8,128)(2,1)}, u32[]{:S(2)}) copy-start(bf16[32,768]{1,0:T(8,128)(2,1)} %get-tuple-element.119) | copy-start | bytes 147460
  221.5 38.8 %all-to-all-start.4 = ((bf16[16,8,7680]{2,1,0:T(8,128)(2,1)}), bf16[16,8,7680]{2,1,0:T(8,128)(2,1)S(1)}, u32[]{:S(2)}, u32[]{:S(2)}) async-start(bf16[16,8,7680]{2,1,0:T(8,128)(2,1)} %bitcast.26), calls=%async_computation.6 | async-start | bytes 3932160 | tf_op jit(solution)/shard_map/all_to_all | solution.py:758
  230.8 28.8 %collective-permute-start.5 = (bf16[32,768]{1,0:T(8,128)(2,1)S(1)}, bf16[32,768]{1,0:T(8,128)(2,1)S(1)}, u32[]{:S(2)}, u32[]{:S(2)}) collective-permute-start(bf16[32,768]{1,0:T(8,128)(2,1)S(1)} %copy-done.10), channel_id=1, source_target_pairs={{0,0},{16,1},{32,2},{48,3},{64,4},{80,5},{96,6},{112,7},{1,8},{17,... | collective-permute-start | bytes 147464 | tf_op jit(solution)/shard_map/ppermute | solution.py:825
  260.3 1.3 copy-start.1
Sparse Core Ops, SparseCore 0:
  11.6 80.5 all-gather.3
  94.5 25.1 all-gather.5
  122.1 36.6 reduce-scatter.4
  163.7 53.7 reduce-scatter.2
where the time goes:
time: 275 us; the launch traced here: 273 us
  waiting for transfers between devices  89.9 us (33%)
  Pallas kernels  87.3 us (32%)
  starting transfers between devices  69.8 us (25%)
  between operations  16.7 us (6%)
  local copies, waits for them, and re-layouts  5.98 us (2%)
  other arithmetic  2.88 us (1%)
    pallas_call x10, Pallas kernels, call(): pl.pallas_call(kernel, out_shape=[jax.ShapeDtypeStruct(s, t) for s, t in...  87.3 us
    all_gather x1, waiting for transfers between devices, body(): wall = lax.all_gather(pack, ALL, axis=0, tiled=True)  38.6 us
    all_to_all x4, starting transfers between devices, swap(): return lax.all_to_all(rows, 'fsdp', split_axis=0, concat_axis=0, tiled=True)  33.7 us
    ppermute x1, waiting for transfers between devices, body(): hl = lax.ppermute(halo[64:128], 'fsdp', right)  27.8 us
    ppermute x1, waiting for transfers between devices, body(): lax.ppermute(g_hd, ALL, [(d % 8 * 16 + d // 8, d) for d in range(128)])  22.9 us
    ppermute x1, starting transfers between devices, body(): hd = lax.ppermute(hd, ALL, [(d, d % 8 * 16 + d // 8) for d in range(128)])  9.21 us
    all_to_all x1, starting transfers between devices, body(): lax.all_to_all(hsend, 'fsdp', split_axis=0, concat_axis=0, tiled=True)  6.93 us
    ppermute x1, starting transfers between devices, body(): lax.ppermute(g_hd, ALL, [(d % 8 * 16 + d // 8, d) for d in range(128)])  5.92 us
  transfers between devices with their start and end apart: 15, of which 4 were waited for; matrix products, arithmetic and copies ran while one was open for 2% of the time, Pallas kernels for 28%

commit v1 on v0

--- a/solution.py
+++ b/solution.py
@@ -18,7 +18,7 @@
 VMEM = pl.BlockSpec(memory_space=pltpu.VMEM)
 HBM = pl.BlockSpec(memory_space=pl.ANY)
 
-C_QKVO, C_VEC, C_DOWN, C_HO, C_ALL = 2048, 5120, 5248, 6016, 6784
+C_QKVO, C_VEC, C_DOWN, C_ALL = 2048, 5120, 5248, 5504
 F_DOWN, F_ALL = 2048, 3072
 R_HEAVY, R_HO, R_VEC, R_DOWN, R_ALL = 3072, 3968, 4736, 4864, 5120
 S_DOWN, S_REST, S_BACK, S_ALL = 1536, 2304, 6144, 7680
@@ -87,28 +87,35 @@
 
 
 def prep_kernel(
-    q, k, v, o, gate, up, down, hq, hk, hv, ho, hgate, hup, hdown, ga, gf, ra, rf, pack, hsend, hd, scr, rows
+    q, k, v, o, gate, up, down, hq, hk, hv, ho, hgate, hup, hdown, ga, gf, ra, rf, pack, hsend, hd, scr, rows, wide
 ):
     scr[...] = jnp.zeros_like(scr)
     zero128 = jnp.zeros((8, 128), BF)
-
-    def padded(ref):
-        cols = ref.shape[1]
-        scr[0:6, 0:cols] = ref[...]
-        return scr[:, 0:cols].astype(BF)
-
-    gp, upp = padded(gate), padded(up)
     for c in range(4):
-        pack[:, 512 * c : 512 * c + 256] = gp[:, 256 * c : 256 * c + 256]
-        pack[:, 512 * c + 256 : 512 * c + 512] = upp[:, 256 * c : 256 * c + 256]
+        cols = slice(256 * c, 256 * c + 256)
+        scr[0:6, 512 * c : 512 * c + 256] = gate[:, cols]
+        scr[0:6, 512 * c + 256 : 512 * c + 512] = up[:, cols]
     for n, ref in enumerate((q, k, v, o)):
-        pack[:, C_QKVO + 768 * n : C_QKVO + 768 * n + 768] = padded(ref)
+        scr[0:6, C_QKVO + 768 * n : C_QKVO + 768 * n + 768] = ref[...]
+    for a in range(2):
+        for b in range(4):
+            scr[6 + a : 7 + a, 512 * b : 512 * b + 512] = down[4 * a + b : 4 * a + b + 1, 0:512]
+        for b in range(3):
+            at = C_QKVO + 768 * b
+            scr[6 + a : 7 + a, at : at + 768] = ho[3 * a + b : 3 * a + b + 1, :]
+    scr[:, C_DOWN:C_ALL] = down[:, 512:768]
     rows[...] = jnp.zeros_like(rows)
     for n, ref in enumerate((ga, gf, ra, rf)):
         rows[n : n + 1, 0:6] = ref[...]
-    pack[:, C_VEC : C_VEC + 128] = rows[...].T[0:8, :].astype(BF)
-    pack[:, C_DOWN : C_DOWN + 768] = down[...].astype(BF)
-    pack[:, C_HO : C_HO + 768] = padded(ho)
+    scr[:, C_VEC : C_VEC + 128] = rows[...].T[0:8, :]
+    pack[...] = scr[...].astype(BF)
+    wide[...] = jnp.zeros_like(wide)
+
+    def padded(ref):
+        cols = ref.shape[1]
+        wide[0:6, 0:cols] = ref[...]
+        return wide[:, 0:cols].astype(BF)
+
     wq, wk, wv = padded(hq), padded(hk), padded(hv)
     wg, wu = padded(hgate), padded(hup)
     for j in range(16):
@@ -122,7 +129,7 @@
 
 
 def light_ffn_kernel(
-    x_in, g_in, wall, ffn, cf, light, gvec, vrows, x, g, gu, fin, fin_t, gbuf, gu_pad, down, vec, in_sems, out_sems
+    x_in, g_in, wall, ffn, cf, light, gvec, vrows, x, g, gu, fin, fin_t, gbuf, gu_pad, down, vec, wd, in_sems, out_sems
 ):
     def wide(c, at=0):
         return pl.ds(pl.multiple_of(at + 512 * c, 128), 512)
@@ -131,7 +138,7 @@
         rows = pl.ds(pl.multiple_of(256 * c, 256), 256)
         yield pltpu.make_async_copy(wall.at[:, wide(c)], gu_pad.at[:, wide(c)], in_sems.at[2 * c])
         yield pltpu.make_async_copy(
-            wall.at[rows, C_DOWN : C_DOWN + 768], down.at[rows, :], in_sems.at[2 * c + 1]
+            wall.at[rows, C_DOWN:C_ALL], down.at[rows, :], in_sems.at[2 * c + 1]
         )
 
     def stores(c):
@@ -161,22 +168,33 @@
     cf[...] = jnp.zeros_like(cf)
     got_g.wait()
 
+    for c in range(4):
+        for copy in loads(c):
+            copy.wait()
+    out_row = lax.broadcasted_iota(jnp.int32, (256, 256), 0)
+    in_row = lax.broadcasted_iota(jnp.int32, (256, 256), 1)
+    spare = (out_row & ~7) + 6 + ((out_row >> 2) & 1) == in_row
+    spread = [(spare & ((out_row & 3) == b)).astype(F32).astype(BF) for b in range(4)]
+
     @pl.loop(0, 4)
     def _(c):
-        for copy in loads(c):
-            copy.wait()
         for b in range(8):
             block = dot(pick, gu_pad[128 * b : 128 * b + 128, wide(c)])
             gu[96 * b : 96 * b + 96, :] = block.astype(BF)
         w = gu[...]
-        wd = down[pl.ds(pl.multiple_of(256 * c, 256), 256), :]
+        rows = pl.ds(pl.multiple_of(256 * c, 256), 256)
+        left = dot(spread[0], gu_pad[rows, 0:512])
+        for b in range(1, 4):
+            left = left + dot(spread[b], gu_pad[rows, 512 * b : 512 * b + 512])
+        wd[:, 0:512] = left.astype(BF)
+        wd[:, 512:768] = down[rows, :]
         both = dot(fin[...], w)
         act, slope = gelu_parts(both[:, 0:256])
         up = both[:, 256:512]
         hidden = (act * up).astype(BF)
-        dh = dot_nt(g[...], wd)
+        dh = dot_nt(g[...], wd[...])
         dgu = jnp.concatenate([(dh * up * slope).astype(BF), (dh * act).astype(BF)], axis=1)
-        ffn[...] += dot(hidden, wd)
+        ffn[...] += dot(hidden, wd[...])
         cf[...] += dot_nt(dgu, w)
         gbuf[:, wide(c)] = dot(fin_t[...], dgu).astype(BF)
         gd = dot_tn(hidden, g[...]).astype(BF)
@@ -203,7 +221,7 @@
 
 def light_attn_kernel(
     meta, xl, x_in, xr, g_in, wall, ffn_in, cf_in, gin, vrows,
-    lo, dxg, halo, rest, gvec,
+    lo, dxg, halo, rest, gvec, heavy_wo,
     w, xs, a, a_t, qkv, o, do, dqkv, dk, dv, mask, w_pad, g, ffn, cf, lo_buf, d_a, gbuf, in_sems, out_sems,
 ):
     def wide(n, at=0):
@@ -262,6 +280,16 @@
     got_g.wait()
     do[...] = dot_nt(g[...], w[:, 2304:3072]).astype(BF)
 
+    row = lax.broadcasted_iota(jnp.int32, (128, 1024), 0)
+    col = lax.broadcasted_iota(jnp.int32, (128, 1024), 1)
+    entry = 6 * (col >> 3) + 3 * ((col & 7) - 6)
+    keep = ((col & 7) >= 6) & ((row >> 6) == meta[4])
+    wo = jnp.zeros((128, 768), F32)
+    for b in range(3):
+        take = (keep & (entry + b == row + meta[3])).astype(F32).astype(BF)
+        wo = wo + dot(take, w_pad[:, 768 * b : 768 * b + 768])
+    heavy_wo[...] = wo.astype(BF)
+
     lane = lax.broadcasted_iota(jnp.int32, (128, 256), 1)
 
     def pair(b, group, second):
@@ -387,17 +415,20 @@
         many[t] = rows
 
 
-def home_kernel(meta, parts, own_in, send_in, send, back, own, sems):
+def home_kernel(meta, parts_in, own_in, send_in, send, back, own, parts, sems):
     copies = Copies(sems)
+    got = [copies.start(parts_in.at[4 * n : 4 * n + 4], parts.at[4 * n : 4 * n + 4]) for n in range(4)]
     got_own = copies.start(own_in, own)
-    total = parts[0].astype(F32)
-    for t in range(1, 16):
-        total = total + parts[t].astype(F32)
+    onehot = entry_slots(meta)
+    total = jnp.zeros((64, 1536), F32)
+    for n in range(4):
+        got[n].wait()
+        for t in range(4 * n, 4 * n + 4):
+            total = total + parts[t].astype(F32)
     got_own.wait()
     u, scale = unit(own[:, 0:768].astype(F32))
     c = total[:, 768:1536]
     dxr = scale * (c - u * jnp.mean(u * c, axis=-1, keepdims=True))
-    onehot = entry_slots(meta)
     back[:, 0:768] = dot_tn(onehot, total[:, 0:768].astype(BF)).astype(BF)
     back[:, 768:1536] = dot_tn(onehot, dxr.astype(BF)).astype(BF)
     copies.start(back, send.at[:, S_BACK:S_ALL]).wait()
@@ -408,14 +439,13 @@
 
 
 def heavy_kernel(
-    meta, xg_in, hw_in, wall, kmask_in, gin, vrows, rest_in,
+    meta, xg_in, hw_in, wo, kmask_in, gin, vrows, rest_in,
     parts, rest,
-    xg, w, wd, wo, ar, fr, q, k, v, o, do, dqkv, dk, dv, kmask, da, dgu, hid, sa, sf, la,
-    hw, wo_pad, pbuf, gbuf, gvec, in_sems, out_sems,
+    xg, w, wd, ar, fr, q, k, v, o, do, dqkv, dk, dv, kmask, da, dgu, hid, sa, sf, la,
+    hw, pbuf, gbuf, gvec, in_sems, out_sems,
 ):
     loads, stores = Copies(in_sems), Copies(out_sems)
     got_hw = loads.start(hw_in, hw)
-    got_wo = loads.start(wall.at[:, C_HO : C_HO + 768], wo_pad)
     got_xg = loads.start(xg_in, xg)
     got_kmask = loads.start(kmask_in, kmask)
     pick = pick6(96, 128)
@@ -424,11 +454,7 @@
     for b in range(8):
         w[96 * b : 96 * b + 96, :] = dot(pick, hw[b, 0:128, :]).astype(BF)
         wd[32 * b : 32 * b + 32, :] = hw[b, 128:160, 0:768]
-    got_wo.wait()
     low, head = meta[18], meta[19]
-    head_row = lax.broadcasted_iota(jnp.int32, (128, 1024), 0) >> 6
-    mine = jnp.where(head_row == head, pick6(128, 1024, low).astype(F32), 0.0).astype(BF)
-    wo[...] = dot(mine, wo_pad[...]).astype(BF)
     on = (lax.broadcasted_iota(jnp.int32, (256, 128), 1) >> 6) == head
     got_xg.wait()
 
@@ -627,12 +653,24 @@
 
 
 def last_kernel(
-    got, st, lo, dxg, hl, hr,
-    out, grad, q, k, v, o, gate, up, down, hq, hk, hv, ho, hgate, hup, *vecs,
+    got_in, st, lo_in, dxg_in, hl, hr,
+    out, grad, q, k, v, o, gate, up, down, hq, hk, hv, ho, hgate, hup, *rest,
 ):
+    *vecs, got, lo, dxg, sems = rest
+    copies = Copies(sems)
+    pieces = [
+        copies.start(got_in.at[:, :, a:b], got.at[:, :, a:b])
+        for a, b in ((0, S_REST), (S_REST, S_BACK), (S_BACK, S_ALL))
+    ]
+    got_lo, got_dxg = copies.start(lo_in, lo), copies.start(dxg_in, dxg)
+    pieces[0].wait()
+    sum_ffn_kernel(got, gate, up, down)
+    pieces[1].wait()
+    sum_rest_kernel(got, q, k, v, o, hq, hk, hv, ho, hgate, hup, vecs)
+    pieces[2].wait()
+    got_lo.wait()
+    got_dxg.wait()
     tokens_kernel(got, st, lo, dxg, hl, hr, out, grad)
-    sum_ffn_kernel(got, gate, up, down)
-    sum_rest_kernel(got, q, k, v, o, hq, hk, hv, ho, hgate, hup, vecs)
 
 
 def call(kernel, outs, args, scratch=(), in_specs=None, out_specs=None, sems=(), name=None, us=0.05, aliases={}):
@@ -660,7 +698,7 @@
         [
             ((512, 768), BF), ((512, 768), BF),
             ((768, 512), BF), ((512, 768), BF), ((768, 512), BF), ((768, 3072), BF),
-            ((1024, 2048), BF), ((1024, 768), BF), ((1024, 128), BF),
+            ((1024, 2048), BF), ((1024, 256), BF), ((1024, 128), BF), ((256, 768), BF),
         ],
         [HBM, HBM, HBM],
         [VMEM, VMEM, HBM, VMEM, VMEM],
@@ -675,6 +713,7 @@
         light_attn_kernel,
         [
             ((512, 768), F32), ((512, 768), F32), ((128, 768), BF), ((768, R_ALL), BF), ((8, 768), F32),
+            ((128, 768), BF),
         ],
         (meta, xl, tokens, xr, cotangent, wall, ffn, cf, gvec, vrows),
         [
@@ -685,30 +724,30 @@
             ((512, 768), F32), ((640, 768), F32), ((768, 3072), BF),
         ],
         [SMEM, VMEM, HBM, VMEM, HBM] + [HBM] * 3 + [VMEM, VMEM],
-        [HBM, VMEM, VMEM, HBM, VMEM],
+        [HBM, VMEM, VMEM, HBM, VMEM, VMEM],
         sems=(8, 5),
         name="light_attn",
         us=2,
     )
 
 
-def run_heavy(meta, xg, hw, wall, kmask, gvec, vrows, rest):
+def run_heavy(meta, xg, hw, wo, kmask, gvec, vrows, rest):
     col = ((1024, 1), F32)
     rows, narrow = ((1024, 768), BF), ((1024, 128), BF)
     return call(
         heavy_kernel,
         [((1024, 1536), BF), ((768, R_ALL), BF)],
-        (meta, xg, hw, wall, kmask, gvec, vrows, rest),
+        (meta, xg, hw, wo, kmask, gvec, vrows, rest),
         [
-            ((1024, 1536), BF), ((768, 896), BF), ((256, 768), BF), ((128, 768), BF), rows, rows,
+            ((1024, 1536), BF), ((768, 896), BF), ((256, 768), BF), rows, rows,
             narrow, narrow, narrow, narrow, narrow, ((1024, 384), BF),
             ((1024, 128), F32), ((1024, 128), F32), ((1024, 256), F32),
             rows, ((1024, 512), BF), ((1024, 256), BF), col, col, col,
-            ((8, 160, 896), BF), rows, ((1024, 1536), BF), ((768, R_ALL - R_HEAVY), BF), ((8, 768), F32),
+            ((8, 160, 896), BF), ((1024, 1536), BF), ((768, R_ALL - R_HEAVY), BF), ((8, 768), F32),
         ],
-        [SMEM, HBM, HBM, HBM, HBM, VMEM, VMEM, HBM],
+        [SMEM, HBM, HBM, VMEM, HBM, VMEM, VMEM, HBM],
         [HBM, HBM],
-        sems=(4, 7),
+        sems=(3, 7),
         aliases={7: 1},
         name="heavy",
         us=200,
@@ -729,7 +768,7 @@
             light_q, light_k, light_v, light_o, light_gate, light_up, light_down,
             heavy_q, heavy_k, heavy_v, heavy_o, heavy_gate, heavy_up, heavy_down, *vectors,
         ),
-        [((8, 4096), F32), ((128, 128), F32)],
+        [((8, C_ALL), F32), ((128, 128), F32), ((8, 4096), F32)],
         name="prep",
     )
     wall = lax.all_gather(pack, ALL, axis=0, tiled=True)
@@ -781,11 +820,11 @@
     xg = swap(many).reshape(1024, 1536)
     ffn, cf, grad_ffn, gvec, vrows = run_light_ffn(tokens, cotangent, wall)
     rs_ffn = lax.psum_scatter(grad_ffn, "dp", scatter_dimension=0, tiled=True)
-    lmeta = jnp.stack([lengths[0, 0], me * 512, jnp.int32(8192)])
-    lo, dxg, halo, rest, gvec = run_light_attn(
+    lmeta = jnp.concatenate([jnp.stack([lengths[0, 0], me * 512, jnp.int32(8192)]), meta[18:20]])
+    lo, dxg, halo, rest, gvec, heavy_wo = run_light_attn(
         lmeta, xl, tokens, xr, cotangent, wall, ffn, cf, gvec, vrows
     )
-    parts, rest = run_heavy(meta, xg, hw, wall, kmask, gvec, vrows, rest)
+    parts, rest = run_heavy(meta, xg, hw, heavy_wo, kmask, gvec, vrows, rest)
     rs_rest = lax.psum_scatter(rest, "dp", scatter_dimension=0, tiled=True)
     hr = lax.ppermute(halo[0:64], "fsdp", left)
     hl = lax.ppermute(halo[64:128], "fsdp", right)
@@ -804,10 +843,10 @@
         home_kernel,
         [((128, S_ALL), BF)],
         (meta, parts, own, send),
-        [((128, 1536), BF), ((64, 1536), BF)],
-        [SMEM, VMEM, HBM, HBM],
+        [((128, 1536), BF), ((64, 1536), BF), ((16, 64, 1536), BF)],
+        [SMEM, HBM, HBM, HBM],
         [HBM],
-        sems=(2,),
+        sems=(6,),
         name="home",
         aliases={3: 0},
     )
@@ -833,6 +872,9 @@
         [((512, 768), BF), ((512, 768), BF)] + [six] * 4 + [four, four, ((8, 768), F32)]
         + [six] * 4 + [big, big] + [((1, 6), F32)] * 4,
         (got, st, lo, dxg, hl, hr),
+        [((16, 8, S_ALL), BF), ((512, 768), F32), ((512, 768), F32)],
+        [HBM, VMEM, HBM, HBM, VMEM, VMEM],
+        sems=(5,),
         name="last",
     )
     return (

time: 275 us -> 270 us (0.982)
  starting transfers between devices: 69.8 us -> 64 us
  Pallas kernels: 87.3 us -> 90.2 us
    ppermute x1, waiting for transfers between devices: 0.01 us -> 27.8 us  [body(): hr = lax.ppermute(halo[0:64], 'fsdp', left)]
    ppermute x1, waiting for transfers between devices: 27.8 us -> 1.14 us  [body(): hl = lax.ppermute(halo[64:128], 'fsdp', right)]
    all_to_all x4, starting transfers between devices: 33.7 us -> 27.7 us  [swap(): return lax.all_to_all(rows, 'fsdp', split_axis=0, concat_axis=0, tiled=True)]
    all_gather x1, waiting for transfers between devices: 38.6 us -> 32.5 us  [body(): wall = lax.all_gather(pack, ALL, axis=0, tiled=True)]
    pallas_call x10, Pallas kernels: 87.3 us -> 90.2 us  [call(): pl.pallas_call(kernel, out_shape=[jax.ShapeDtypeStruct(s, t) for s, t in...]
  transfers between devices with their start and end apart: 15 -> 15, of which waited for: 4 -> 5; matrix products, arithmetic and copies ran while one was open for 2% -> 2% of each run, Pallas kernels for 28% -> 30%
where the time goes in v1:
time: 270 us; the launch traced here: 268 us
  Pallas kernels  90.2 us (33%)
  waiting for transfers between devices  88.3 us (33%)
  starting transfers between devices  64 us (24%)
  between operations  16.7 us (6%)
  local copies, waits for them, and re-layouts  6.62 us (2%)
    pallas_call x10, Pallas kernels, call(): pl.pallas_call(kernel, out_shape=[jax.ShapeDtypeStruct(s, t) for s, t in...  90.2 us
    all_gather x1, waiting for transfers between devices, body(): wall = lax.all_gather(pack, ALL, axis=0, tiled=True)  32.5 us
    ppermute x1, waiting for transfers between devices, body(): hr = lax.ppermute(halo[0:64], 'fsdp', left)  27.8 us
    all_to_all x4, starting transfers between devices, swap(): return lax.all_to_all(rows, 'fsdp', split_axis=0, concat_axis=0, tiled=True)  27.7 us
    ppermute x1, waiting for transfers between devices, body(): lax.ppermute(g_hd, ALL, [(d % 8 * 16 + d // 8, d) for d in range(128)])  23.3 us
    ppermute x1, starting transfers between devices, body(): hd = lax.ppermute(hd, ALL, [(d, d % 8 * 16 + d // 8) for d in range(128)])  9.59 us
    all_to_all x1, starting transfers between devices, body(): lax.all_to_all(hsend, 'fsdp', split_axis=0, concat_axis=0, tiled=True)  6.93 us
    ppermute x1, starting transfers between devices, body(): lax.ppermute(g_hd, ALL, [(d % 8 * 16 + d // 8, d) for d in range(128)])  5.85 us
  transfers between devices with their start and end apart: 15, of which 5 were waited for; matrix products, arithmetic and copies ran while one was open for 2% of the time, Pallas kernels for 30%

profile of v1, /device:TPU:3, one launch (start us, length us, event | category | flops | bytes accessed | tf_op | source)
XLA Modules:
  0.0 268.0 jit_solution(6073327794383779429)
XLA Ops:
  7.2 0.0 copy-start.8
  7.2 0.0 all-gather.4.cloned.1.call-start
  7.3 2.0 prep.1
  9.3 0.0 all-gather.4.cloned.1.call-update
  9.3 6.9 %all-to-all-start.1 = ((bf16[16,8,896]{2,1,0:T(8,128)(2,1)}), bf16[16,8,896]{2,1,0:T(8,128)(2,1)S(1)}, u32[]{:S(2)}, u32[]{:S(2)}) async-start(bf16[16,8,896]{2,1,0:T(8,128)(2,1)} %get-tuple-element.74), calls=%async_computation.1 | async-start | bytes 458752 | tf_op jit(solution)/shard_map/all_to_all | solution.py:776
  18.9 0.9 convert_reduce_fusion
  19.7 1.3 concatenate.12.meta
  21.0 3.0 %slots.1 = (bf16[128,1536]{1,0:T(8,128)(2,1)}, bf16[512,128]{1,0:T(8,128)(2,1)}) custom-call(s32[24]{0:T(128)} %concatenate.12.meta, s32[1,1024]{1,0:T(1,128)} %routed.1, bf16[512,768]{1,0:T(8,128)(2,1)} %x_in.3, bf16[512,768]{1,0:T(8,128)(2,1)} %g_in.3), custom_call_target="tpu_custom_call" | custom-call | flops 50000000 | bytes 150000 | tf_op jit(solution)/shard_map/slots/pallas_call | solution.py:677
  24.0 6.7 %all-to-all-start = ((bf16[16,8,1536]{2,1,0:T(8,128)(2,1)}), bf16[16,8,1536]{2,1,0:T(8,128)(2,1)S(1)}, u32[]{:S(2)}, u32[]{:S(2)}) async-start(bf16[16,8,1536]{2,1,0:T(8,128)(2,1)} %bitcast.30), calls=%async_computation | async-start | bytes 786432 | tf_op jit(solution)/shard_map/all_to_all | solution.py:797
  30.7 9.6 %collective-permute-start.2 = (bf16[32,768]{1,0:T(8,128)(2,1)S(1)}, bf16[32,768]{1,0:T(8,128)(2,1)S(1)}, u32[]{:S(2)}, u32[]{:S(2)}) collective-permute-start(bf16[32,768]{1,0:T(8,128)(2,1)S(1)} %copy-done.9), channel_id=1, source_target_pairs={{0,0},{1,16},{2,32},{3,48},{4,64},{5,80},{6,96},{7,112},{8,1},{9,1... | collective-permute-start | bytes 147464 | tf_op jit(solution)/shard_map/ppermute | solution.py:777
  40.3 1.0 fusion.2
  41.3 1.9 collective-permute-start
  43.2 5.5 %collective-permute-start.1 = (bf16[64,768]{1,0:T(8,128)(2,1)S(1)}, bf16[64,768]{1,0:T(8,128)(2,1)S(1)}, u32[]{:S(2)}, u32[]{:S(2)}) collective-permute-start(bf16[64,768]{1,0:T(8,128)(2,1)S(1)} %get-tuple-element.122), channel_id=1, source_target_pairs={{1,0},{2,1},{3,2},{4,3},{5,4},{6,5},{7,6},{8,7},{9,8},{10,9},{11,1... | collective-permute-start | bytes 294920 | tf_op jit(solution)/shard_map/ppermute | solution.py:816
  48.7 0.6 concatenate.14.meta
  49.3 0.7 fusion.1
  50.1 0.7 copy-done.2
  50.8 3.8 %entries.1 = (bf16[64,1536]{1,0:T(8,128)(2,1)}, bf16[16,64,1536]{2,1,0:T(8,128)(2,1)}, f32[1024,256]{1,0:T(8,128)}) custom-call(s32[24]{0:T(128)} %concatenate.12.meta, bf16[128,1536]{1,0:T(8,128)(2,1)} %bitcast.28), custom_call_target="tpu_custom_call" | custom-call | flops 50000000 | bytes 150000 | tf_op jit(solution)/shard_map/entries/pallas_call | solution.py:677
  54.6 0.0 copy-start.5
  54.6 32.5 %all-gather.4.cloned.1.call-done.wall = bf16[1024,5504]{1,0:T(8,128)(2,1)} async-done(((bf16[8,5504]{1,0:T(8,128)(2,1)}), bf16[1024,5504]{1,0:T(8,128)(2,1)}) %all-gather.4.cloned.1.call-update) | async-done | bytes 11272208 | tf_op jit(solution)/shard_map/all_gather | solution.py:774
  87.2 6.5 %all-to-all-start.2 = ((bf16[16,64,1536]{2,1,0:T(8,128)(2,1)}), bf16[16,64,1536]{2,1,0:T(8,128)(2,1)}, u32[]{:S(2)}, u32[]{:S(2)}) async-start(bf16[16,64,1536]{2,1,0:T(8,128)(2,1)} %get-tuple-element.76), calls=%async_computation.2 | async-start | bytes 6291456 | tf_op jit(solution)/shard_map/all_to_all | solution.py:797
  93.7 0.0 all-gather.6.cloned.1.call-start
  93.7 0.7 all-gather.6.cloned.1.call-update
  94.4 0.0 reduce-scatter.5.cloned.1.call-start
  94.5 16.2 %light_ffn.1 = (f32[512,768]{1,0:T(8,128)}, f32[512,768]{1,0:T(8,128)}, bf16[768,3072]{1,0:T(8,128)(2,1)}, f32[8,768]{1,0:T(8,128)}, f32[8,768]{1,0:T(8,128)}) custom-call(bf16[512,768]{1,0:T(8,128)(2,1)} %x_in.3, bf16[512,768]{1,0:T(8,128)(2,1)} %g_in.3, bf16[1024,5504]{1,0:T(8,128)(2,1)} %all-gather.4.cloned.1.call-done.wall), custom_call_target="tpu_custom_call" | custom-call | flops 199999995904 | bytes 600000000 | tf_op jit(solution)/shard_map/light_ffn/pallas_call | solution.py:677
  110.7 0.0 reduce-scatter.5.cloned.1.call-update
  110.7 0.2 reduce-scatter.3.cloned.1.call-start
  110.9 27.3 %light_attn.1 = (f32[512,768]{1,0:T(8,128)}, f32[512,768]{1,0:T(8,128)}, bf16[128,768]{1,0:T(8,128)(2,1)}, bf16[768,5120]{1,0:T(8,128)(2,1)}, f32[8,768]{1,0:T(8,128)}, /*index=5*/bf16[128,768]{1,0:T(8,128)(2,1)}) custom-call(s32[5]{0:T(128)} %concatenate.14.meta, bf16[64,768]{1,0:T(8,128)(2,1)} %copy-done.4, bf16[512,768]{1,0:T(8,128)(2,1)} %x_in.3, ...), custom_call_target="tpu_custom_call" | custom-call | flops 2000000000 | bytes 6000000 | tf_op jit(solution)/shard_map/light_attn/pallas_call | solution.py:677
  138.3 0.0 all-gather.6.cloned.1.call-done
  138.3 23.0 %heavy.1 = (bf16[1024,1536]{1,0:T(8,128)(2,1)}, bf16[768,5120]{1,0:T(8,128)(2,1)}) custom-call(s32[24]{0:T(128)} %concatenate.12.meta, bf16[1024,1536]{1,0:T(8,128)(2,1)} %bitcast.16.xg_in, bf16[8,160,896]{2,1,0:T(8,128)(2,1)} %bitcast.42, bf16[128,768]{1,0:T(8,128)(2,1)} %get-tuple-element.85.wo, ...), custom_call_target="tpu_custom_call", output_to_operand_aliasing={{1}: (7, {})} | custom-call | flops 199999995904 | bytes 600000000 | tf_op jit(solution)/shard_map/heavy/pallas_call | solution.py:677
  161.4 0.0 reduce-scatter.3.cloned.1.call-update
  161.4 7.6 %all-to-all-start.3 = ((bf16[16,64,1536]{2,1,0:T(8,128)(2,1)}), bf16[16,64,1536]{2,1,0:T(8,128)(2,1)S(1)}, u32[]{:S(2)}, u32[]{:S(2)}) async-start(bf16[16,64,1536]{2,1,0:T(8,128)(2,1)} %bitcast.27), calls=%async_computation.4 | async-start | bytes 6291456 | tf_op jit(solution)/shard_map/all_to_all | solution.py:797
  169.1 4.3 %collective-permute-start.3 = (bf16[64,768]{1,0:T(8,128)(2,1)S(1)}, bf16[64,768]{1,0:T(8,128)(2,1)S(1)}, u32[]{:S(2)}, u32[]{:S(2)}) collective-permute-start(bf16[64,768]{1,0:T(8,128)(2,1)S(1)} %get-tuple-element.125), channel_id=1, source_target_pairs={{1,0},{2,1},{3,2},{4,3},{5,4},{6,5},{7,6},{8,7},{9,8},{10,9},{11,1... | collective-permute-start | bytes 294920 | tf_op jit(solution)/shard_map/ppermute | solution.py:829
  173.4 1.9 collective-permute-start.4
  175.3 0.0 reduce-scatter.5.cloned.1.call-done.r
  175.3 2.3 spread_ffn.1.send_in
  177.6 27.8 %collective-permute-done.3.hr = bf16[64,768]{1,0:T(8,128)(2,1)S(1)} collective-permute-done((bf16[64,768]{1,0:T(8,128)(2,1)S(1)}, bf16[64,768]{1,0:T(8,128)(2,1)S(1)}, u32[]{:S(2)}, u32[]{:S(2)}) %collective-permute-start.3) | collective-permute-done | bytes 98336 | tf_op jit(solution)/shard_map/ppermute | solution.py:829
  205.4 1.1 collective-permute-done.4.hl
  206.6 1.7 copy-done
  208.2 3.9 %home.1.send_in = bf16[128,7680]{1,0:T(8,128)(2,1)} custom-call(s32[24]{0:T(128)} %concatenate.12.meta, bf16[16,64,1536]{2,1,0:T(8,128)(2,1)} %copy-done, bf16[64,1536]{1,0:T(8,128)(2,1)} %get-tuple-element.94.own_in, bf16[128,7680]{1,0:T(8,128)(2,1)} %spread_ffn.1.send_in), custom_call_target="tpu_custom_call", output_to_operand_aliasing={{}: (3, {})} | custom-call | flops 50000000 | bytes 150000 | tf_op jit(solution)/shard_map/home/pallas_call | solution.py:677
  212.2 2.7 %reduce-scatter.3.cloned.1.call-done.r = bf16[96,5120]{1,0:T(8,128)(2,1)} async-done(((bf16[768,5120]{1,0:T(8,128)(2,1)}), bf16[96,5120]{1,0:T(8,128)(2,1)}) %reduce-scatter.3.cloned.1.call-update) | async-done | bytes 983056 | tf_op jit(solution)/shard_map/reduce_scatter | solution.py:828
  214.9 3.4 %spread_rest.1 = (bf16[128,7680]{1,0:T(8,128)(2,1)}, bf16[32,768]{1,0:T(8,128)(2,1)}) custom-call(bf16[96,5120]{1,0:T(8,128)(2,1)} %reduce-scatter.3.cloned.1.call-done.r, bf16[128,7680]{1,0:T(8,128)(2,1)} %home.1.send_in), custom_call_target="tpu_custom_call", output_to_operand_aliasing={{0}: (1, {})} | custom-call | flops 50000000 | bytes 150000 | tf_op jit(solution)/shard_map/spread_rest/pallas_call | solution.py:677
  218.3 0.0 copy-start.10
  218.4 6.8 %all-to-all-start.4 = ((bf16[16,8,7680]{2,1,0:T(8,128)(2,1)}), bf16[16,8,7680]{2,1,0:T(8,128)(2,1)S(1)}, u32[]{:S(2)}, u32[]{:S(2)}) async-start(bf16[16,8,7680]{2,1,0:T(8,128)(2,1)} %bitcast.26), calls=%async_computation.6 | async-start | bytes 3932160 | tf_op jit(solution)/shard_map/all_to_all | solution.py:797
  225.2 5.9 %collective-permute-start.5 = (bf16[32,768]{1,0:T(8,128)(2,1)S(1)}, bf16[32,768]{1,0:T(8,128)(2,1)S(1)}, u32[]{:S(2)}, u32[]{:S(2)}) collective-permute-start(bf16[32,768]{1,0:T(8,128)(2,1)S(1)} %copy-done.10), channel_id=1, source_target_pairs={{0,0},{16,1},{32,2},{48,3},{64,4},{80,5},{96,6},{112,7},{1,8},{17,... | collective-permute-start | bytes 147464 | tf_op jit(solution)/shard_map/ppermute | solution.py:864
  231.1 23.3 %collective-permute-done.5 = bf16[32,768]{1,0:T(8,128)(2,1)S(1)} collective-permute-done((bf16[32,768]{1,0:T(8,128)(2,1)S(1)}, bf16[32,768]{1,0:T(8,128)(2,1)S(1)}, u32[]{:S(2)}, u32[]{:S(2)}) %collective-permute-start.5) | collective-permute-done | bytes 49184 | tf_op jit(solution)/shard_map/ppermute | solution.py:864
  254.4 0.6 convert_element_type.9
  255.0 1.3 copy-done.1
  256.3 5.2 %last.1 = (bf16[512,768]{1,0:T(8,128)(2,1)}, bf16[512,768]{1,0:T(8,128)(2,1)}, f32[6,768]{1,0:T(8,128)}, f32[6,768]{1,0:T(8,128)}, f32[6,768]{1,0:T(8,128)}, /*i...) custom-call(bf16[16,8,7680]{2,1,0:T(8,128)(2,1)} %copy-done.1, ...), custom_call_target="tpu_custom_call" | custom-call | flops 50000000 | bytes 150000 | tf_op jit(solution)/shard_map/last/pallas_call | solution.py:677
  (26 shorter events, 0.1 us)
Async XLA Ops:
  7.2 41.5 %copy-start.8 = (s32[1,2]{1,0:T(1,128)S(1)}, s32[1,2]{1,0:T(1,128)}, u32[]{:S(2)}) copy-start(s32[1,2]{1,0:T(1,128)} %param.23) | copy-start | bytes 28
  7.2 79.9 %all-gather.4.cloned.1.call-start = ((), (), s32[]{:S(2)}) async-start(), calls=%async_computation.7 | async-start | bytes 11360256 | tf_op jit(solution)/shard_map/all_gather | solution.py:774
  9.3 21.4 %copy-start.9 = (bf16[32,768]{1,0:T(8,128)(2,1)S(1)}, bf16[32,768]{1,0:T(8,128)(2,1)}, u32[]{:S(2)}) copy-start(bf16[32,768]{1,0:T(8,128)(2,1)} %get-tuple-element.75) | copy-start | bytes 147460
  9.3 14.7 %all-to-all-start.1 = ((bf16[16,8,896]{2,1,0:T(8,128)(2,1)}), bf16[16,8,896]{2,1,0:T(8,128)(2,1)S(1)}, u32[]{:S(2)}, u32[]{:S(2)}) async-start(bf16[16,8,896]{2,1,0:T(8,128)(2,1)} %get-tuple-element.74), calls=%async_computation.1 | async-start | bytes 458752 | tf_op jit(solution)/shard_map/all_to_all | solution.py:776
  24.0 26.0 %all-to-all-start = ((bf16[16,8,1536]{2,1,0:T(8,128)(2,1)}), bf16[16,8,1536]{2,1,0:T(8,128)(2,1)S(1)}, u32[]{:S(2)}, u32[]{:S(2)}) async-start(bf16[16,8,1536]{2,1,0:T(8,128)(2,1)} %bitcast.30), calls=%async_computation | async-start | bytes 786432 | tf_op jit(solution)/shard_map/all_to_all | solution.py:797
  30.7 18.6 %collective-permute-start.2 = (bf16[32,768]{1,0:T(8,128)(2,1)S(1)}, bf16[32,768]{1,0:T(8,128)(2,1)S(1)}, u32[]{:S(2)}, u32[]{:S(2)}) collective-permute-start(bf16[32,768]{1,0:T(8,128)(2,1)S(1)} %copy-done.9), channel_id=1, source_target_pairs={{0,0},{1,16},{2,32},{3,48},{4,64},{5,80},{6,96},{7,112},{8,1},{9,1... | collective-permute-start | bytes 147464 | tf_op jit(solution)/shard_map/ppermute | solution.py:777
  41.3 13.4 %collective-permute-start = (bf16[64,768]{1,0:T(8,128)(2,1)S(1)}, bf16[64,768]{1,0:T(8,128)(2,1)S(1)}, u32[]{:S(2)}, u32[]{:S(2)}) collective-permute-start(bf16[64,768]{1,0:T(8,128)(2,1)S(1)} %get-tuple-element.123), channel_id=1, source_target_pairs={{0,1},{1,2},{2,3},{3,4},{4,5},{5,6},{6,7},{7,8},{8,9},{9,10},{10,1... | collective-permute-start | bytes 294920 | tf_op jit(solution)/shard_map/ppermute | solution.py:815
  43.2 11.4 %collective-permute-start.1 = (bf16[64,768]{1,0:T(8,128)(2,1)S(1)}, bf16[64,768]{1,0:T(8,128)(2,1)S(1)}, u32[]{:S(2)}, u32[]{:S(2)}) collective-permute-start(bf16[64,768]{1,0:T(8,128)(2,1)S(1)} %get-tuple-element.122), channel_id=1, source_target_pairs={{1,0},{2,1},{3,2},{4,3},{5,4},{6,5},{7,6},{8,7},{9,8},{10,9},{11,1... | collective-permute-start | bytes 294920 | tf_op jit(solution)/shard_map/ppermute | solution.py:816
  50.1 0.7 copy-start.2
  54.6 32.5 %copy-start.4 = (bf16[64,768]{1,0:T(8,128)(2,1)}, bf16[64,768]{1,0:T(8,128)(2,1)S(1)}, u32[]{:S(2)}) copy-start(bf16[64,768]{1,0:T(8,128)(2,1)S(1)} %collective-permute-done.xl) | copy-start | bytes 294916
  54.6 32.5 %copy-start.5 = (bf16[64,768]{1,0:T(8,128)(2,1)}, bf16[64,768]{1,0:T(8,128)(2,1)S(1)}, u32[]{:S(2)}) copy-start(bf16[64,768]{1,0:T(8,128)(2,1)S(1)} %collective-permute-done.1.xr) | copy-start | bytes 294916
  87.2 51.1 %all-to-all-start.2 = ((bf16[16,64,1536]{2,1,0:T(8,128)(2,1)}), bf16[16,64,1536]{2,1,0:T(8,128)(2,1)}, u32[]{:S(2)}, u32[]{:S(2)}) async-start(bf16[16,64,1536]{2,1,0:T(8,128)(2,1)} %get-tuple-element.76), calls=%async_computation.2 | async-start | bytes 6291456 | tf_op jit(solution)/shard_map/all_to_all | solution.py:797
  93.7 44.6 %all-gather.6.cloned.1.call-start = ((), (), s32[]{:S(2)}) async-start(), calls=%async_computation.10 | async-start | bytes 2580480 | tf_op jit(solution)/shard_map/all_gather | solution.py:819
  94.4 80.9 %reduce-scatter.5.cloned.1.call-start = ((), (), s32[]{:S(2)}) async-start(), calls=%async_computation.9 | async-start | bytes 5308416 | tf_op jit(solution)/shard_map/reduce_scatter | solution.py:822
  110.7 104.2 %reduce-scatter.3.cloned.1.call-start = ((), (), s32[]{:S(2)}) async-start(), calls=%async_computation.8 | async-start | bytes 8847360 | tf_op jit(solution)/shard_map/reduce_scatter | solution.py:828
  161.4 7.7 %copy-start.3 = (bf16[128,768]{1,0:T(8,128)(2,1)S(1)}, bf16[128,768]{1,0:T(8,128)(2,1)}, u32[]{:S(2)}) copy-start(bf16[128,768]{1,0:T(8,128)(2,1)} %get-tuple-element.92) | copy-start | bytes 589828
  161.4 45.2 %all-to-all-start.3 = ((bf16[16,64,1536]{2,1,0:T(8,128)(2,1)}), bf16[16,64,1536]{2,1,0:T(8,128)(2,1)S(1)}, u32[]{:S(2)}, u32[]{:S(2)}) async-start(bf16[16,64,1536]{2,1,0:T(8,128)(2,1)} %bitcast.27), calls=%async_computation.4 | async-start | bytes 6291456 | tf_op jit(solution)/shard_map/all_to_all | solution.py:797
  169.1 36.4 %collective-permute-start.3 = (bf16[64,768]{1,0:T(8,128)(2,1)S(1)}, bf16[64,768]{1,0:T(8,128)(2,1)S(1)}, u32[]{:S(2)}, u32[]{:S(2)}) collective-permute-start(bf16[64,768]{1,0:T(8,128)(2,1)S(1)} %get-tuple-element.125), channel_id=1, source_target_pairs={{1,0},{2,1},{3,2},{4,3},{5,4},{6,5},{7,6},{8,7},{9,8},{10,9},{11,1... | collective-permute-start | bytes 294920 | tf_op jit(solution)/shard_map/ppermute | solution.py:829
  173.4 33.2 %collective-permute-start.4 = (bf16[64,768]{1,0:T(8,128)(2,1)S(1)}, bf16[64,768]{1,0:T(8,128)(2,1)S(1)}, u32[]{:S(2)}, u32[]{:S(2)}) collective-permute-start(bf16[64,768]{1,0:T(8,128)(2,1)S(1)} %get-tuple-element.124), channel_id=1, source_target_pairs={{0,1},{1,2},{2,3},{3,4},{4,5},{5,6},{6,7},{7,8},{8,9},{9,10},{10,1... | collective-permute-start | bytes 294920 | tf_op jit(solution)/shard_map/ppermute | solution.py:830
  205.4 12.9 %copy-start.6 = (bf16[64,768]{1,0:T(8,128)(2,1)}, bf16[64,768]{1,0:T(8,128)(2,1)S(1)}, u32[]{:S(2)}) copy-start(bf16[64,768]{1,0:T(8,128)(2,1)S(1)} %collective-permute-done.3.hr) | copy-start | bytes 294916
  206.6 11.8 %copy-start.7 = (bf16[64,768]{1,0:T(8,128)(2,1)}, bf16[64,768]{1,0:T(8,128)(2,1)S(1)}, u32[]{:S(2)}) copy-start(bf16[64,768]{1,0:T(8,128)(2,1)S(1)} %collective-permute-done.4.hl) | copy-start | bytes 294916
  206.6 1.7 copy-start
  218.3 6.9 %copy-start.10 = (bf16[32,768]{1,0:T(8,128)(2,1)S(1)}, bf16[32,768]{1,0:T(8,128)(2,1)}, u32[]{:S(2)}) copy-start(bf16[32,768]{1,0:T(8,128)(2,1)} %get-tuple-element.121) | copy-start | bytes 147460
  218.4 36.7 %all-to-all-start.4 = ((bf16[16,8,7680]{2,1,0:T(8,128)(2,1)}), bf16[16,8,7680]{2,1,0:T(8,128)(2,1)S(1)}, u32[]{:S(2)}, u32[]{:S(2)}) async-start(bf16[16,8,7680]{2,1,0:T(8,128)(2,1)} %bitcast.26), calls=%async_computation.6 | async-start | bytes 3932160 | tf_op jit(solution)/shard_map/all_to_all | solution.py:797
  225.2 29.2 %collective-permute-start.5 = (bf16[32,768]{1,0:T(8,128)(2,1)S(1)}, bf16[32,768]{1,0:T(8,128)(2,1)S(1)}, u32[]{:S(2)}, u32[]{:S(2)}) collective-permute-start(bf16[32,768]{1,0:T(8,128)(2,1)S(1)} %copy-done.10), channel_id=1, source_target_pairs={{0,0},{16,1},{32,2},{48,3},{64,4},{80,5},{96,6},{112,7},{1,8},{17,... | collective-permute-start | bytes 147464 | tf_op jit(solution)/shard_map/ppermute | solution.py:864
  255.0 1.3 copy-start.1
Sparse Core Ops, SparseCore 0:
  11.7 75.3 all-gather.3
  96.8 25.7 all-gather.5
  125.0 36.2 reduce-scatter.4
  163.5 51.2 reduce-scatter.2

commit v2 on v1

--- a/solution.py
+++ b/solution.py
@@ -21,7 +21,8 @@
 C_QKVO, C_VEC, C_DOWN, C_ALL = 2048, 5120, 5248, 5504
 F_DOWN, F_ALL = 2048, 3072
 R_HEAVY, R_HO, R_VEC, R_DOWN, R_ALL = 3072, 3968, 4736, 4864, 5120
-S_DOWN, S_REST, S_BACK, S_ALL = 1536, 2304, 6144, 7680
+S_DOWN, S_FFN = 1536, 2304
+S_BACK, S_ALL = 3840, 5376
 
 def dot(a, b):
     return jnp.dot(a, b, preferred_element_type=F32)
@@ -415,23 +416,29 @@
         many[t] = rows
 
 
-def home_kernel(meta, parts_in, own_in, send_in, send, back, own, parts, sems):
-    copies = Copies(sems)
-    got = [copies.start(parts_in.at[4 * n : 4 * n + 4], parts.at[4 * n : 4 * n + 4]) for n in range(4)]
-    got_own = copies.start(own_in, own)
+def first_sum_kernel(meta, y0, y1, y2, y3, c0, c1, c2, c3, *outs):
+    for n in range(4):
+        for here, parts, out in (
+            (meta[20] & 3, (y0, y1, y2, y3), outs[n]), (meta[20] >> 2, (c0, c1, c2, c3), outs[4 + n])
+        ):
+            rows = pl.ds(pl.multiple_of(64 * ((here + n) & 3), 64), 64)
+            total = parts[0][rows, :].astype(F32)
+            for part in parts[1:]:
+                total = total + part[rows, :].astype(F32)
+            out[...] = total.astype(BF)
+
+
+def home_kernel(meta, y0, y1, y2, y3, c0, c1, c2, c3, own, send, back, sems):
+    y, c = (
+        a[...].astype(F32) + b[...].astype(F32) + d[...].astype(F32) + e[...].astype(F32)
+        for a, b, d, e in ((y0, y1, y2, y3), (c0, c1, c2, c3))
+    )
     onehot = entry_slots(meta)
-    total = jnp.zeros((64, 1536), F32)
-    for n in range(4):
-        got[n].wait()
-        for t in range(4 * n, 4 * n + 4):
-            total = total + parts[t].astype(F32)
-    got_own.wait()
     u, scale = unit(own[:, 0:768].astype(F32))
-    c = total[:, 768:1536]
     dxr = scale * (c - u * jnp.mean(u * c, axis=-1, keepdims=True))
-    back[:, 0:768] = dot_tn(onehot, total[:, 0:768].astype(BF)).astype(BF)
+    back[:, 0:768] = dot_tn(onehot, y.astype(BF)).astype(BF)
     back[:, 768:1536] = dot_tn(onehot, dxr.astype(BF)).astype(BF)
-    copies.start(back, send.at[:, S_BACK:S_ALL]).wait()
+    Copies(sems).start(back, send.at[:, S_BACK:S_ALL]).wait()
 
 
 def entry_of(row):
@@ -440,9 +447,9 @@
 
 def heavy_kernel(
     meta, xg_in, hw_in, wo, kmask_in, gin, vrows, rest_in,
-    parts, rest,
+    y0, y1, y2, y3, c0, c1, c2, c3, rest,
     xg, w, wd, ar, fr, q, k, v, o, do, dqkv, dk, dv, kmask, da, dgu, hid, sa, sf, la,
-    hw, pbuf, gbuf, gvec, in_sems, out_sems,
+    hw, ybuf, cbuf, gbuf, gvec, in_sems, out_sems,
 ):
     loads, stores = Copies(in_sems), Copies(out_sems)
     got_hw = loads.start(hw_in, hw)
@@ -515,10 +522,6 @@
     stores.send(gbuf.at[:, 512 : R_VEC - at], rest.at[:, at + 512 : R_VEC])
     gvec[...] = gin[...]
 
-    def send_parts(b):
-        rows = pl.ds(pl.multiple_of(256 * b, 256), 256)
-        return pltpu.make_async_copy(pbuf.at[rows, :], parts.at[rows, :], out_sems.at[3 + b])
-
     @pl.loop(0, 4, unroll=2)
     def _(b):
         rows = pl.ds(pl.multiple_of(256 * b, 256), 256)
@@ -544,9 +547,16 @@
         gvec[2:3, :] += jnp.sum(lab * ar[rows, :].astype(F32), axis=0, keepdims=True)
         gvec[3:4, :] += jnp.sum(lfb * frb.astype(F32), axis=0, keepdims=True)
         da[rows, :] = dfb
-        pbuf[rows, 0:768] = y.astype(BF)
-        pbuf[rows, 768:1536] = (d_a * gain_a + d_f * gain_f).astype(BF)
-        send_parts(b).start()
+        ybuf[rows, :] = y.astype(BF)
+        c = (d_a * gain_a + d_f * gain_f).astype(BF)
+        for t in range(4):
+            cbuf[pl.ds(pl.multiple_of(256 * t + 64 * b, 64), 64), :] = c[64 * t : 64 * t + 64]
+
+    for n, (yk, ck) in enumerate(((y0, c0), (y1, c1), (y2, c2), (y3, c3))):
+        to_x = ((meta[20] >> 2) + n) & 3
+        to_y = ((meta[20] & 3) + n) & 3
+        stores.send(ybuf.at[pl.ds(pl.multiple_of(256 * to_x, 256), 256), :], yk)
+        stores.send(cbuf.at[pl.ds(pl.multiple_of(256 * to_y, 256), 256), :], ck)
 
     gbuf[:, 0:512] = dot_tn(fr[...], dgu[...]).astype(BF)
     stores.send(gbuf.at[:, 0:512], rest.at[:, at : at + 512])
@@ -560,8 +570,6 @@
             ]
     stores.send(gbuf.at[:, R_VEC - at : R_ALL - at], rest.at[:, R_VEC:R_ALL])
     stores.finish()
-    for b in range(4):
-        send_parts(b).wait()
 
 
 def tokens_kernel(got, st, lo, dxg, hl, hr, out, grad):
@@ -599,15 +607,14 @@
     )
 
 
-def spread_ffn_kernel(r, send, rows, sems):
-    rows[:, 0:S_DOWN] = owner_rows(r, F_DOWN)
-    rows[:, S_DOWN:S_REST] = tail_rows(r[...], F_DOWN)
-    Copies(sems).start(rows, send.at[:, 0:S_REST]).wait()
+def spread_ffn_kernel(r, send):
+    send[:, 0:S_DOWN] = owner_rows(r, F_DOWN)
+    send[:, S_DOWN:S_FFN] = tail_rows(r[...], F_DOWN)
 
 
 def spread_rest_kernel(r, send_in, send, hd, rows, sems):
     rows[...] = owner_rows(r, R_ALL)
-    copy = Copies(sems).start(rows, send.at[:, S_REST:S_BACK])
+    copy = Copies(sems).start(rows, send.at[:, 0:S_BACK])
     hd[...] = jnp.concatenate([r[32 * t : 32 * t + 32, R_DOWN:R_ALL] for t in range(3)], axis=1)
     copy.wait()
 
@@ -627,11 +634,11 @@
     both = tail_of(both)
     gate[:, 768:1024] = both[:, 0:256]
     up[:, 768:1024] = both[:, 256:512]
-    down[...] = sum_parts(got, S_DOWN, S_REST)
+    down[...] = sum_parts(got, S_DOWN, S_FFN)
 
 
 def sum_rest_kernel(got, q, k, v, o, hq, hk, hv, ho, hgate, hup, vecs):
-    total = sum_parts(got, S_REST, S_BACK)
+    total = sum_parts(got, 0, S_BACK)
     for n, ref in enumerate((q, k, v, o)):
         ref[...] = total[0:6, 768 * n : 768 * n + 768]
     rest = tail_of(total)
@@ -639,13 +646,13 @@
     rows = jnp.concatenate([rest[:, 896:1024], jnp.zeros((122, 128), F32)], axis=0).T
     for n, ref in enumerate(vecs):
         ref[...] = rows[n : n + 1, 0:6]
-    at = S_REST + R_HEAVY
+    at = R_HEAVY
     for j in range(16):
         hgate[:, 256 * j : 256 * j + 256] = got[j, :, at : at + 256].astype(F32)[0:6]
         hup[:, 256 * j : 256 * j + 256] = got[j, :, at + 256 : at + 512].astype(F32)[0:6]
     at = at + 512
     for p in range(6):
-        two = [got[2 * p + n, :, S_REST:S_BACK].astype(F32) for n in range(2)]
+        two = [got[2 * p + n, :, 0:S_BACK].astype(F32) for n in range(2)]
         pair = two[0][:, R_HEAVY + 512 : R_HEAVY + 768] + two[1][:, R_HEAVY + 512 : R_HEAVY + 768]
         hq[:, 128 * p : 128 * p + 128] = pair[0:6, 0:128]
         hk[:, 128 * p : 128 * p + 128] = pair[0:6, 128:256]
@@ -654,20 +661,17 @@
 
 def last_kernel(
     got_in, st, lo_in, dxg_in, hl, hr,
-    out, grad, q, k, v, o, gate, up, down, hq, hk, hv, ho, hgate, hup, *rest,
+    out, grad, q, k, v, o, hq, hk, hv, ho, hgate, hup, *rest,
 ):
     *vecs, got, lo, dxg, sems = rest
     copies = Copies(sems)
     pieces = [
-        copies.start(got_in.at[:, :, a:b], got.at[:, :, a:b])
-        for a, b in ((0, S_REST), (S_REST, S_BACK), (S_BACK, S_ALL))
+        copies.start(got_in.at[:, :, a:b], got.at[:, :, a:b]) for a, b in ((0, S_BACK), (S_BACK, S_ALL))
     ]
     got_lo, got_dxg = copies.start(lo_in, lo), copies.start(dxg_in, dxg)
     pieces[0].wait()
-    sum_ffn_kernel(got, gate, up, down)
+    sum_rest_kernel(got, q, k, v, o, hq, hk, hv, ho, hgate, hup, vecs)
     pieces[1].wait()
-    sum_rest_kernel(got, q, k, v, o, hq, hk, hv, ho, hgate, hup, vecs)
-    pieces[2].wait()
     got_lo.wait()
     got_dxg.wait()
     tokens_kernel(got, st, lo, dxg, hl, hr, out, grad)
@@ -736,19 +740,19 @@
     rows, narrow = ((1024, 768), BF), ((1024, 128), BF)
     return call(
         heavy_kernel,
-        [((1024, 1536), BF), ((768, R_ALL), BF)],
+        [((256, 768), BF)] * 8 + [((768, R_ALL), BF)],
         (meta, xg, hw, wo, kmask, gvec, vrows, rest),
         [
             ((1024, 1536), BF), ((768, 896), BF), ((256, 768), BF), rows, rows,
             narrow, narrow, narrow, narrow, narrow, ((1024, 384), BF),
             ((1024, 128), F32), ((1024, 128), F32), ((1024, 256), F32),
             rows, ((1024, 512), BF), ((1024, 256), BF), col, col, col,
-            ((8, 160, 896), BF), ((1024, 1536), BF), ((768, R_ALL - R_HEAVY), BF), ((8, 768), F32),
+            ((8, 160, 896), BF), rows, rows, ((768, R_ALL - R_HEAVY), BF), ((8, 768), F32),
         ],
         [SMEM, HBM, HBM, VMEM, HBM, VMEM, VMEM, HBM],
-        [HBM, HBM],
-        sems=(3, 7),
-        aliases={7: 1},
+        [HBM] * 9,
+        sems=(3, 11),
+        aliases={7: 8},
         name="heavy",
         us=200,
     )
@@ -824,37 +828,46 @@
     lo, dxg, halo, rest, gvec, heavy_wo = run_light_attn(
         lmeta, xl, tokens, xr, cotangent, wall, ffn, cf, gvec, vrows
     )
-    parts, rest = run_heavy(meta, xg, hw, heavy_wo, kmask, gvec, vrows, rest)
+    *partial, rest = run_heavy(meta, xg, hw, heavy_wo, kmask, gvec, vrows, rest)
     rs_rest = lax.psum_scatter(rest, "dp", scatter_dimension=0, tiled=True)
+
+    def along(blocks, x, y):
+        moved = [
+            lax.ppermute(
+                block, "fsdp", [(i, (i // 4 + n * x) % 4 * 4 + (i % 4 + n * y) % 4) for i in range(16)]
+            )
+            for n, block in enumerate(blocks[1:], 1)
+        ]
+        return [blocks[0]] + moved
+
+    blocks = call(
+        first_sum_kernel,
+        [((64, 768), BF)] * 8,
+        (meta, *along(partial[0:4], 1, 0), *along(partial[4:8], 0, 1)),
+        in_specs=[SMEM] + [VMEM] * 8,
+        name="first_sum",
+    )
+    blocks = along(blocks[0:4], 0, 1) + along(blocks[4:8], 1, 0)
     hr = lax.ppermute(halo[0:64], "fsdp", left)
     hl = lax.ppermute(halo[64:128], "fsdp", right)
-    (send,) = call(
-        spread_ffn_kernel,
-        [((128, S_ALL), BF)],
-        (rs_ffn,),
-        [((128, S_REST), BF)],
-        out_specs=[HBM],
-        sems=(1,),
-        name="spread_ffn",
-    )
-    parts = swap(parts.reshape(16, 64, 1536))
-    parts, send, hr, hl = lax.optimization_barrier((parts, send, hr, hl))
+    (send_ffn,) = call(spread_ffn_kernel, [((128, S_FFN), BF)], (rs_ffn,), name="spread_ffn")
+    got_ffn = swap(send_ffn.reshape(16, 8, S_FFN))
+    *blocks, got_ffn, hr, hl = lax.optimization_barrier((*blocks, got_ffn, hr, hl))
     (send,) = call(
         home_kernel,
         [((128, S_ALL), BF)],
-        (meta, parts, own, send),
-        [((128, 1536), BF), ((64, 1536), BF), ((16, 64, 1536), BF)],
-        [SMEM, HBM, HBM, HBM],
+        (meta, *blocks, own),
+        [((128, 1536), BF)],
+        [SMEM] + [VMEM] * 9,
         [HBM],
-        sems=(6,),
+        sems=(1,),
         name="home",
-        aliases={3: 0},
     )
     send, g_hd = call(
         spread_rest_kernel,
         [((128, S_ALL), BF), ((32, 768), BF)],
         (rs_rest, send),
-        [((128, S_BACK - S_REST), BF)],
+        [((128, S_BACK), BF)],
         [VMEM, HBM],
         [HBM, VMEM],
         sems=(1,),
@@ -864,17 +877,16 @@
     g_hd = lax.ppermute(g_hd, ALL, [((d % 8) * 16 + d // 8, d) for d in range(128)])
     got = swap(send.reshape(16, 8, S_ALL))
     six, four, big = ((6, 768), F32), ((6, 1024), F32), ((6, 4096), F32)
-    (
-        output, grad_tokens, g_q, g_k, g_v, g_o, g_gate, g_up, g_down,
-        g_hq, g_hk, g_hv, g_ho, g_hgate, g_hup, *g_vecs,
-    ) = call(
+    g_gate, g_up, g_down = call(
+        sum_ffn_kernel, [four, four, ((8, 768), F32)], (got_ffn,), name="sum_ffn"
+    )
+    output, grad_tokens, g_q, g_k, g_v, g_o, g_hq, g_hk, g_hv, g_ho, g_hgate, g_hup, *g_vecs = call(
         last_kernel,
-        [((512, 768), BF), ((512, 768), BF)] + [six] * 4 + [four, four, ((8, 768), F32)]
-        + [six] * 4 + [big, big] + [((1, 6), F32)] * 4,
+        [((512, 768), BF), ((512, 768), BF)] + [six] * 8 + [big, big] + [((1, 6), F32)] * 4,
         (got, st, lo, dxg, hl, hr),
         [((16, 8, S_ALL), BF), ((512, 768), F32), ((512, 768), F32)],
         [HBM, VMEM, HBM, HBM, VMEM, VMEM],
-        sems=(5,),
+        sems=(4,),
         name="last",
     )
     return (

time: 270 us -> 264 us (0.978)
  waiting for transfers between devices: 88.3 us -> 58.4 us
  starting transfers between devices: 64 us -> 84 us
  Pallas kernels: 90.2 us -> 93.5 us
    ppermute x1, waiting for transfers between devices: 27.8 us -> 0.01 us  [body(): hr = lax.ppermute(halo[0:64], 'fsdp', left)]
    ppermute x0 -> x12, starting transfers between devices: none -> 19.8 us  [along(): lax.ppermute(block, 'fsdp', [(i, (i // 4 + n * x) % 4 * 4 + (i % 4 + n *...]
    ppermute x1, waiting for transfers between devices: 23.3 us -> 13.8 us  [body(): lax.ppermute(g_hd, ALL, [(d % 8 * 16 + d // 8, d) for d in range(128)])]
    ppermute x0 -> x12, waiting for transfers between devices: none -> 7.59 us  [along(): lax.ppermute(block, 'fsdp', [(i, (i // 4 + n * x) % 4 * 4 + (i % 4 + n *...]
    pallas_call x10 -> x12, Pallas kernels: 90.2 us -> 93.5 us  [call(): pl.pallas_call(kernel, out_shape=[jax.ShapeDtypeStruct(s, t) for s, t in...]
  transfers between devices with their start and end apart: 15 -> 27, of which waited for: 5 -> 8; matrix products, arithmetic and copies ran while one was open for 2% -> 2% of each run, Pallas kernels for 30% -> 32%
where the time goes in v2:
time: 264 us; the launch traced here: 262 us
  Pallas kernels  93.5 us (35%)
  starting transfers between devices  84 us (32%)
  waiting for transfers between devices  58.4 us (22%)
  between operations  16.9 us (6%)
  local copies, waits for them, and re-layouts  7.31 us (3%)
    pallas_call x12, Pallas kernels, call(): pl.pallas_call(kernel, out_shape=[jax.ShapeDtypeStruct(s, t) for s, t in...  93.5 us
    all_gather x1, waiting for transfers between devices, body(): wall = lax.all_gather(pack, ALL, axis=0, tiled=True)  32.5 us
    all_to_all x4, starting transfers between devices, swap(): return lax.all_to_all(rows, 'fsdp', split_axis=0, concat_axis=0, tiled=True)  25 us
    ppermute x12, starting transfers between devices, along(): lax.ppermute(block, 'fsdp', [(i, (i // 4 + n * x) % 4 * 4 + (i % 4 + n *...  19.8 us
    ppermute x1, waiting for transfers between devices, body(): lax.ppermute(g_hd, ALL, [(d % 8 * 16 + d // 8, d) for d in range(128)])  13.8 us
    ppermute x1, starting transfers between devices, body(): hd = lax.ppermute(hd, ALL, [(d, d % 8 * 16 + d // 8) for d in range(128)])  9.59 us
    ppermute x1, starting transfers between devices, body(): lax.ppermute(g_hd, ALL, [(d % 8 * 16 + d // 8, d) for d in range(128)])  8.16 us
    ppermute x12, waiting for transfers between devices, along(): lax.ppermute(block, 'fsdp', [(i, (i // 4 + n * x) % 4 * 4 + (i % 4 + n *...  7.59 us
  transfers between devices with their start and end apart: 27, of which 8 were waited for; matrix products, arithmetic and copies ran while one was open for 2% of the time, Pallas kernels for 32%

profile of v2, /device:TPU:3, one launch (start us, length us, event | category | flops | bytes accessed | tf_op | source)
XLA Modules:
  0.0 262.3 jit_solution(17289225567934585875)
XLA Ops:
  7.3 2.0 prep.1
  9.3 6.9 %all-to-all-start.1 = ((bf16[16,8,896]{2,1,0:T(8,128)(2,1)}), bf16[16,8,896]{2,1,0:T(8,128)(2,1)S(1)}, u32[]{:S(2)}, u32[]{:S(2)}) async-start(bf16[16,8,896]{2,1,0:T(8,128)(2,1)} %get-tuple-element.96), calls=%async_computation.1 | async-start | bytes 458752 | tf_op jit(solution)/shard_map/all_to_all | solution.py:780
  18.9 0.9 convert_reduce_fusion
  19.7 1.3 concatenate.12.meta
  21.0 3.0 %slots.1 = (bf16[128,1536]{1,0:T(8,128)(2,1)}, bf16[512,128]{1,0:T(8,128)(2,1)}) custom-call(s32[24]{0:T(128)} %concatenate.12.meta, s32[1,1024]{1,0:T(1,128)} %routed.1, bf16[512,768]{1,0:T(8,128)(2,1)} %x_in.3, bf16[512,768]{1,0:T(8,128)(2,1)} %g_in.3), custom_call_target="tpu_custom_call" | custom-call | flops 50000000 | bytes 150000 | tf_op jit(solution)/shard_map/slots/pallas_call | solution.py:681
  24.0 6.7 %all-to-all-start = ((bf16[16,8,1536]{2,1,0:T(8,128)(2,1)}), bf16[16,8,1536]{2,1,0:T(8,128)(2,1)S(1)}, u32[]{:S(2)}, u32[]{:S(2)}) async-start(bf16[16,8,1536]{2,1,0:T(8,128)(2,1)} %bitcast.30), calls=%async_computation | async-start | bytes 786432 | tf_op jit(solution)/shard_map/all_to_all | solution.py:801
  30.7 9.6 %collective-permute-start.2 = (bf16[32,768]{1,0:T(8,128)(2,1)S(1)}, bf16[32,768]{1,0:T(8,128)(2,1)S(1)}, u32[]{:S(2)}, u32[]{:S(2)}) collective-permute-start(bf16[32,768]{1,0:T(8,128)(2,1)S(1)} %copy-done.23), channel_id=1, source_target_pairs={{0,0},{1,16},{2,32},{3,48},{4,64},{5,80},{6,96},{7,112},{8,1},{9,1... | collective-permute-start | bytes 147464 | tf_op jit(solution)/shard_map/ppermute | solution.py:781
  40.3 1.0 fusion.2
  41.3 1.9 collective-permute-start
  43.2 5.5 %collective-permute-start.1 = (bf16[64,768]{1,0:T(8,128)(2,1)S(1)}, bf16[64,768]{1,0:T(8,128)(2,1)S(1)}, u32[]{:S(2)}, u32[]{:S(2)}) collective-permute-start(bf16[64,768]{1,0:T(8,128)(2,1)S(1)} %get-tuple-element.166), channel_id=1, source_target_pairs={{1,0},{2,1},{3,2},{4,3},{5,4},{6,5},{7,6},{8,7},{9,8},{10,9},{11,1... | collective-permute-start | bytes 294920 | tf_op jit(solution)/shard_map/ppermute | solution.py:820
  49.3 0.7 fusion.1
  50.1 0.7 copy-done.2
  50.8 3.8 %entries.1 = (bf16[64,1536]{1,0:T(8,128)(2,1)}, bf16[16,64,1536]{2,1,0:T(8,128)(2,1)}, f32[1024,256]{1,0:T(8,128)}) custom-call(s32[24]{0:T(128)} %concatenate.12.meta, bf16[128,1536]{1,0:T(8,128)(2,1)} %bitcast.28), custom_call_target="tpu_custom_call" | custom-call | flops 50000000 | bytes 150000 | tf_op jit(solution)/shard_map/entries/pallas_call | solution.py:681
  54.7 32.5 %all-gather.4.cloned.1.call-done.wall = bf16[1024,5504]{1,0:T(8,128)(2,1)} async-done(((bf16[8,5504]{1,0:T(8,128)(2,1)}), bf16[1024,5504]{1,0:T(8,128)(2,1)}) %all-gather.4.cloned.1.call-update) | async-done | bytes 11272208 | tf_op jit(solution)/shard_map/all_gather | solution.py:778
  87.2 6.5 %all-to-all-start.2 = ((bf16[16,64,1536]{2,1,0:T(8,128)(2,1)}), bf16[16,64,1536]{2,1,0:T(8,128)(2,1)}, u32[]{:S(2)}, u32[]{:S(2)}) async-start(bf16[16,64,1536]{2,1,0:T(8,128)(2,1)} %get-tuple-element.98), calls=%async_computation.2 | async-start | bytes 6291456 | tf_op jit(solution)/shard_map/all_to_all | solution.py:801
  94.5 16.1 %light_ffn.1 = (f32[512,768]{1,0:T(8,128)}, f32[512,768]{1,0:T(8,128)}, bf16[768,3072]{1,0:T(8,128)(2,1)}, f32[8,768]{1,0:T(8,128)}, f32[8,768]{1,0:T(8,128)}) custom-call(bf16[512,768]{1,0:T(8,128)(2,1)} %x_in.3, bf16[512,768]{1,0:T(8,128)(2,1)} %g_in.3, bf16[1024,5504]{1,0:T(8,128)(2,1)} %all-gather.4.cloned.1.call-done.wall), custom_call_target="tpu_custom_call" | custom-call | flops 199999995904 | bytes 600000000 | tf_op jit(solution)/shard_map/light_ffn/pallas_call | solution.py:681
  110.9 27.4 %light_attn.1 = (f32[512,768]{1,0:T(8,128)}, f32[512,768]{1,0:T(8,128)}, bf16[128,768]{1,0:T(8,128)(2,1)}, bf16[768,5120]{1,0:T(8,128)(2,1)}, f32[8,768]{1,0:T(8,128)}, /*index=5*/bf16[128,768]{1,0:T(8,128)(2,1)}) custom-call(s32[5]{0:T(128)} %concatenate.14.meta, bf16[64,768]{1,0:T(8,128)(2,1)} %copy-done.10, bf16[512,768]{1,0:T(8,128)(2,1)} %x_in.3, ...), custom_call_target="tpu_custom_call" | custom-call | flops 2000000000 | bytes 6000000 | tf_op jit(solution)/shard_map/light_attn/pallas_call | solution.py:681
  138.3 23.0 %heavy.1 = (bf16[256,768]{1,0:T(8,128)(2,1)}, bf16[256,768]{1,0:T(8,128)(2,1)}, bf16[256,768]{1,0:T(8,128)(2,1)}, bf16[256,768]{1,0:T(8,128)(2,1)}, bf16[256,768...) custom-call(s32[24]{0:T(128)} %concatenate.12.meta, ...), custom_call_target="tpu_custom_call", output_to_operand_aliasing={{8}: (7, {})} | custom-call | flops 199999995904 | bytes 600000000 | tf_op jit(solution)/shard_map/heavy/pallas_call | solution.py:681
  161.4 0.9 copy-done.22
  162.4 1.2 collective-permute-start.3
  163.6 0.7 collective-permute-start.4
  164.3 1.9 collective-permute-start.5
  166.2 1.2 collective-permute-start.6
  167.4 2.4 collective-permute-start.7
  169.9 2.3 collective-permute-done.3.y1
  172.2 2.4 collective-permute-start.8
  174.6 2.3 spread_ffn.1
  176.9 4.9 %all-to-all-start.3 = ((bf16[16,8,2304]{2,1,0:T(8,128)(2,1)}), bf16[16,8,2304]{2,1,0:T(8,128)(2,1)S(1)}, u32[]{:S(2)}, u32[]{:S(2)}) async-start(bf16[16,8,2304]{2,1,0:T(8,128)(2,1)} %bitcast.27), calls=%async_computation.5 | async-start | bytes 1179648 | tf_op jit(solution)/shard_map/all_to_all | solution.py:801
  181.9 4.8 %collective-permute-start.15 = (bf16[64,768]{1,0:T(8,128)(2,1)S(1)}, bf16[64,768]{1,0:T(8,128)(2,1)S(1)}, u32[]{:S(2)}, u32[]{:S(2)}) collective-permute-start(bf16[64,768]{1,0:T(8,128)(2,1)S(1)} %get-tuple-element.169), channel_id=1, source_target_pairs={{1,0},{2,1},{3,2},{4,3},{5,4},{6,5},{7,6},{8,7},{9,8},{10,9},{11,1... | collective-permute-start | bytes 294920 | tf_op jit(solution)/shard_map/ppermute | solution.py:851
  186.8 1.9 collective-permute-start.16
  188.8 0.7 copy-done.6
  189.8 3.1 %first_sum.1 = (bf16[64,768]{1,0:T(8,128)(2,1)}, bf16[64,768]{1,0:T(8,128)(2,1)}, bf16[64,768]{1,0:T(8,128)(2,1)}, bf16[64,768]{1,0:T(8,128)(2,1)}, bf16[64,768]...) custom-call(s32[24]{0:T(128)} %concatenate.12.meta, ...), custom_call_target="tpu_custom_call" | custom-call | flops 50000000 | bytes 150000 | tf_op jit(solution)/shard_map/first_sum/pallas_call | solution.py:681
  192.8 1.2 collective-permute-start.10
  194.1 2.2 collective-permute-start.11
  196.3 1.2 collective-permute-start.12
  197.4 5.3 %collective-permute-start.13 = (bf16[64,768]{1,0:T(8,128)(2,1)}, bf16[64,768]{1,0:T(8,128)(2,1)S(1)}, u32[]{:S(2)}, u32[]{:S(2)}) collective-permute-start(bf16[64,768]{1,0:T(8,128)(2,1)} %get-tuple-element.126), channel_id=1, source_target_pairs={{0,8},{1,9},{2,10},{3,11},{4,12},{5,13},{6,14},{7,15},{8,0},{9,1},... | collective-permute-start | bytes 294920 | tf_op jit(solution)/shard_map/ppermute | solution.py:836
  203.5 1.8 collective-permute-done.13.c2
  205.3 1.5 collective-permute-done.14.c3
  206.8 1.3 collective-permute-done.9.y1
  208.7 2.5 home.1.send_in
  211.2 3.7 %reduce-scatter.3.cloned.1.call-done.r = bf16[96,5120]{1,0:T(8,128)(2,1)} async-done(((bf16[768,5120]{1,0:T(8,128)(2,1)}), bf16[96,5120]{1,0:T(8,128)(2,1)}) %reduce-scatter.3.cloned.1.call-update) | async-done | bytes 983056 | tf_op jit(solution)/shard_map/reduce_scatter | solution.py:832
  214.9 3.5 %spread_rest.1 = (bf16[128,5376]{1,0:T(8,128)(2,1)}, bf16[32,768]{1,0:T(8,128)(2,1)}) custom-call(bf16[96,5120]{1,0:T(8,128)(2,1)} %reduce-scatter.3.cloned.1.call-done.r, bf16[128,5376]{1,0:T(8,128)(2,1)} %home.1.send_in), custom_call_target="tpu_custom_call", output_to_operand_aliasing={{0}: (1, {})} | custom-call | flops 50000000 | bytes 150000 | tf_op jit(solution)/shard_map/spread_rest/pallas_call | solution.py:681
  218.4 6.9 %all-to-all-start.4 = ((bf16[16,8,5376]{2,1,0:T(8,128)(2,1)}), bf16[16,8,5376]{2,1,0:T(8,128)(2,1)S(1)}, u32[]{:S(2)}, u32[]{:S(2)}) async-start(bf16[16,8,5376]{2,1,0:T(8,128)(2,1)} %bitcast.26), calls=%async_computation.6 | async-start | bytes 2752512 | tf_op jit(solution)/shard_map/all_to_all | solution.py:801
  225.3 8.2 %collective-permute-start.17 = (bf16[32,768]{1,0:T(8,128)(2,1)S(1)}, bf16[32,768]{1,0:T(8,128)(2,1)S(1)}, u32[]{:S(2)}, u32[]{:S(2)}) collective-permute-start(bf16[32,768]{1,0:T(8,128)(2,1)S(1)} %copy-done.24), channel_id=1, source_target_pairs={{0,0},{16,1},{32,2},{48,3},{64,4},{80,5},{96,6},{112,7},{1,8},{17,... | collective-permute-start | bytes 147464 | tf_op jit(solution)/shard_map/ppermute | solution.py:877
  233.4 1.8 sum_ffn.1
  235.2 13.8 %collective-permute-done.17 = bf16[32,768]{1,0:T(8,128)(2,1)S(1)} collective-permute-done((bf16[32,768]{1,0:T(8,128)(2,1)S(1)}, bf16[32,768]{1,0:T(8,128)(2,1)S(1)}, u32[]{:S(2)}, u32[]{:S(2)}) %collective-permute-start.17) | collective-permute-done | bytes 49184 | tf_op jit(solution)/shard_map/ppermute | solution.py:877
  249.7 1.1 copy-done
  250.8 4.9 %last.1 = (bf16[512,768]{1,0:T(8,128)(2,1)}, bf16[512,768]{1,0:T(8,128)(2,1)}, f32[6,768]{1,0:T(8,128)}, f32[6,768]{1,0:T(8,128)}, f32[6,768]{1,0:T(8,128)}, /*i...) custom-call(bf16[16,8,5376]{2,1,0:T(8,128)(2,1)} %copy-done, ...), custom_call_target="tpu_custom_call" | custom-call | flops 50000000 | bytes 150000 | tf_op jit(solution)/shard_map/last/pallas_call | solution.py:681
  (80 shorter events, 4.2 us)
Async XLA Ops:
  7.2 41.5 %copy-start.20 = (s32[1,2]{1,0:T(1,128)S(1)}, s32[1,2]{1,0:T(1,128)}, u32[]{:S(2)}) copy-start(s32[1,2]{1,0:T(1,128)} %param.23) | copy-start | bytes 28
  7.2 79.9 %all-gather.4.cloned.1.call-start = ((), (), s32[]{:S(2)}) async-start(), calls=%async_computation.7 | async-start | bytes 11360256 | tf_op jit(solution)/shard_map/all_gather | solution.py:778
  9.3 21.4 %copy-start.23 = (bf16[32,768]{1,0:T(8,128)(2,1)S(1)}, bf16[32,768]{1,0:T(8,128)(2,1)}, u32[]{:S(2)}) copy-start(bf16[32,768]{1,0:T(8,128)(2,1)} %get-tuple-element.97) | copy-start | bytes 147460
  9.3 14.7 %all-to-all-start.1 = ((bf16[16,8,896]{2,1,0:T(8,128)(2,1)}), bf16[16,8,896]{2,1,0:T(8,128)(2,1)S(1)}, u32[]{:S(2)}, u32[]{:S(2)}) async-start(bf16[16,8,896]{2,1,0:T(8,128)(2,1)} %get-tuple-element.96), calls=%async_computation.1 | async-start | bytes 458752 | tf_op jit(solution)/shard_map/all_to_all | solution.py:780
  24.0 26.0 %all-to-all-start = ((bf16[16,8,1536]{2,1,0:T(8,128)(2,1)}), bf16[16,8,1536]{2,1,0:T(8,128)(2,1)S(1)}, u32[]{:S(2)}, u32[]{:S(2)}) async-start(bf16[16,8,1536]{2,1,0:T(8,128)(2,1)} %bitcast.30), calls=%async_computation | async-start | bytes 786432 | tf_op jit(solution)/shard_map/all_to_all | solution.py:801
  30.7 18.6 %collective-permute-start.2 = (bf16[32,768]{1,0:T(8,128)(2,1)S(1)}, bf16[32,768]{1,0:T(8,128)(2,1)S(1)}, u32[]{:S(2)}, u32[]{:S(2)}) collective-permute-start(bf16[32,768]{1,0:T(8,128)(2,1)S(1)} %copy-done.23), channel_id=1, source_target_pairs={{0,0},{1,16},{2,32},{3,48},{4,64},{5,80},{6,96},{7,112},{8,1},{9,1... | collective-permute-start | bytes 147464 | tf_op jit(solution)/shard_map/ppermute | solution.py:781
  41.3 13.4 %collective-permute-start = (bf16[64,768]{1,0:T(8,128)(2,1)S(1)}, bf16[64,768]{1,0:T(8,128)(2,1)S(1)}, u32[]{:S(2)}, u32[]{:S(2)}) collective-permute-start(bf16[64,768]{1,0:T(8,128)(2,1)S(1)} %get-tuple-element.167), channel_id=1, source_target_pairs={{0,1},{1,2},{2,3},{3,4},{4,5},{5,6},{6,7},{7,8},{8,9},{9,10},{10,1... | collective-permute-start | bytes 294920 | tf_op jit(solution)/shard_map/ppermute | solution.py:819
  43.2 11.5 %collective-permute-start.1 = (bf16[64,768]{1,0:T(8,128)(2,1)S(1)}, bf16[64,768]{1,0:T(8,128)(2,1)S(1)}, u32[]{:S(2)}, u32[]{:S(2)}) collective-permute-start(bf16[64,768]{1,0:T(8,128)(2,1)S(1)} %get-tuple-element.166), channel_id=1, source_target_pairs={{1,0},{2,1},{3,2},{4,3},{5,4},{6,5},{7,6},{8,7},{9,8},{10,9},{11,1... | collective-permute-start | bytes 294920 | tf_op jit(solution)/shard_map/ppermute | solution.py:820
  54.6 32.5 %copy-start.10 = (bf16[64,768]{1,0:T(8,128)(2,1)}, bf16[64,768]{1,0:T(8,128)(2,1)S(1)}, u32[]{:S(2)}) copy-start(bf16[64,768]{1,0:T(8,128)(2,1)S(1)} %collective-permute-done.xl) | copy-start | bytes 294916
  54.7 32.5 %copy-start.11 = (bf16[64,768]{1,0:T(8,128)(2,1)}, bf16[64,768]{1,0:T(8,128)(2,1)S(1)}, u32[]{:S(2)}) copy-start(bf16[64,768]{1,0:T(8,128)(2,1)S(1)} %collective-permute-done.1.xr) | copy-start | bytes 294916
  87.2 51.1 %all-to-all-start.2 = ((bf16[16,64,1536]{2,1,0:T(8,128)(2,1)}), bf16[16,64,1536]{2,1,0:T(8,128)(2,1)}, u32[]{:S(2)}, u32[]{:S(2)}) async-start(bf16[16,64,1536]{2,1,0:T(8,128)(2,1)} %get-tuple-element.98), calls=%async_computation.2 | async-start | bytes 6291456 | tf_op jit(solution)/shard_map/all_to_all | solution.py:801
  93.7 44.6 %all-gather.6.cloned.1.call-start = ((), (), s32[]{:S(2)}) async-start(), calls=%async_computation.10 | async-start | bytes 2580480 | tf_op jit(solution)/shard_map/all_gather | solution.py:823
  94.4 80.2 %reduce-scatter.5.cloned.1.call-start = ((), (), s32[]{:S(2)}) async-start(), calls=%async_computation.9 | async-start | bytes 5308416 | tf_op jit(solution)/shard_map/reduce_scatter | solution.py:826
  110.7 104.2 %reduce-scatter.3.cloned.1.call-start = ((), (), s32[]{:S(2)}) async-start(), calls=%async_computation.8 | async-start | bytes 8847360 | tf_op jit(solution)/shard_map/reduce_scatter | solution.py:832
  161.4 1.0 copy-start.22
  161.4 10.8 %copy-start.21 = (bf16[256,768]{1,0:T(8,128)(2,1)S(1)}, bf16[256,768]{1,0:T(8,128)(2,1)}, u32[]{:S(2)}) copy-start(bf16[256,768]{1,0:T(8,128)(2,1)} %get-tuple-element.119) | copy-start | bytes 1179652
  161.4 20.4 %copy-start.9 = (bf16[128,768]{1,0:T(8,128)(2,1)S(1)}, bf16[128,768]{1,0:T(8,128)(2,1)}, u32[]{:S(2)}) copy-start(bf16[128,768]{1,0:T(8,128)(2,1)} %get-tuple-element.129) | copy-start | bytes 589828
  162.4 9.8 %collective-permute-start.3 = (bf16[256,768]{1,0:T(8,128)(2,1)S(1)}, bf16[256,768]{1,0:T(8,128)(2,1)S(1)}, u32[]{:S(2)}, u32[]{:S(2)}) collective-permute-start(bf16[256,768]{1,0:T(8,128)(2,1)S(1)} %copy-done.22), channel_id=1, source_target_pairs={{0,4},{1,5},{2,6},{3,7},{4,8},{5,9},{6,10},{7,11},{8,12},{9,13},{1... | collective-permute-start | bytes 1179656 | tf_op jit(solution)/shard_map/ppermute | solution.py:836
  163.6 18.3 %collective-permute-start.4 = (bf16[256,768]{1,0:T(8,128)(2,1)}, bf16[256,768]{1,0:T(8,128)(2,1)S(1)}, u32[]{:S(2)}, u32[]{:S(2)}) collective-permute-start(bf16[256,768]{1,0:T(8,128)(2,1)} %get-tuple-element.114), channel_id=1, source_target_pairs={{0,8},{1,9},{2,10},{3,11},{4,12},{5,13},{6,14},{7,15},{8,0},{9,1},... | collective-permute-start | bytes 1179656 | tf_op jit(solution)/shard_map/ppermute | solution.py:836
  164.3 22.5 %collective-permute-start.5 = (bf16[256,768]{1,0:T(8,128)(2,1)}, bf16[256,768]{1,0:T(8,128)(2,1)S(1)}, u32[]{:S(2)}, u32[]{:S(2)}) collective-permute-start(bf16[256,768]{1,0:T(8,128)(2,1)} %get-tuple-element.115), channel_id=1, source_target_pairs={{0,12},{1,13},{2,14},{3,15},{4,0},{5,1},{6,2},{7,3},{8,4},{9,5},{1... | collective-permute-start | bytes 1179656 | tf_op jit(solution)/shard_map/ppermute | solution.py:836
  166.2 22.5 %collective-permute-start.6 = (bf16[256,768]{1,0:T(8,128)(2,1)}, bf16[256,768]{1,0:T(8,128)(2,1)S(1)}, u32[]{:S(2)}, u32[]{:S(2)}) collective-permute-start(bf16[256,768]{1,0:T(8,128)(2,1)} %get-tuple-element.117), channel_id=1, source_target_pairs={{0,1},{1,2},{2,3},{3,0},{4,5},{5,6},{6,7},{7,4},{8,9},{9,10},{10,1... | collective-permute-start | bytes 1179656 | tf_op jit(solution)/shard_map/ppermute | solution.py:836
  167.4 21.3 %collective-permute-start.7 = (bf16[256,768]{1,0:T(8,128)(2,1)}, bf16[256,768]{1,0:T(8,128)(2,1)S(1)}, u32[]{:S(2)}, u32[]{:S(2)}) collective-permute-start(bf16[256,768]{1,0:T(8,128)(2,1)} %get-tuple-element.118), channel_id=1, source_target_pairs={{0,2},{1,3},{2,0},{3,1},{4,6},{5,7},{6,4},{7,5},{8,10},{9,11},{10,... | collective-permute-start | bytes 1179656 | tf_op jit(solution)/shard_map/ppermute | solution.py:836
  172.2 16.5 %copy-start.3 = (bf16[256,768]{1,0:T(8,128)(2,1)}, bf16[256,768]{1,0:T(8,128)(2,1)S(1)}, u32[]{:S(2)}) copy-start(bf16[256,768]{1,0:T(8,128)(2,1)S(1)} %collective-permute-done.3.y1) | copy-start | bytes 1179652
  172.2 16.5 %collective-permute-start.8 = (bf16[256,768]{1,0:T(8,128)(2,1)S(1)}, bf16[256,768]{1,0:T(8,128)(2,1)S(1)}, u32[]{:S(2)}, u32[]{:S(2)}) collective-permute-start(bf16[256,768]{1,0:T(8,128)(2,1)S(1)} %copy-done.21), channel_id=1, source_target_pairs={{0,3},{1,0},{2,1},{3,2},{4,7},{5,4},{6,5},{7,6},{8,11},{9,8},{10,9... | collective-permute-start | bytes 1179656 | tf_op jit(solution)/shard_map/ppermute | solution.py:836
  176.9 31.2 %all-to-all-start.3 = ((bf16[16,8,2304]{2,1,0:T(8,128)(2,1)}), bf16[16,8,2304]{2,1,0:T(8,128)(2,1)S(1)}, u32[]{:S(2)}, u32[]{:S(2)}) async-start(bf16[16,8,2304]{2,1,0:T(8,128)(2,1)} %bitcast.27), calls=%async_computation.5 | async-start | bytes 1179648 | tf_op jit(solution)/shard_map/all_to_all | solution.py:801
  181.9 6.9 %copy-start.4 = (bf16[256,768]{1,0:T(8,128)(2,1)}, bf16[256,768]{1,0:T(8,128)(2,1)S(1)}, u32[]{:S(2)}) copy-start(bf16[256,768]{1,0:T(8,128)(2,1)S(1)} %collective-permute-done.4.y2) | copy-start | bytes 1179652
  181.9 15.5 %collective-permute-start.15 = (bf16[64,768]{1,0:T(8,128)(2,1)S(1)}, bf16[64,768]{1,0:T(8,128)(2,1)S(1)}, u32[]{:S(2)}, u32[]{:S(2)}) collective-permute-start(bf16[64,768]{1,0:T(8,128)(2,1)S(1)} %get-tuple-element.169), channel_id=1, source_target_pairs={{1,0},{2,1},{3,2},{4,3},{5,4},{6,5},{7,6},{8,7},{9,8},{10,9},{11,1... | collective-permute-start | bytes 294920 | tf_op jit(solution)/shard_map/ppermute | solution.py:851
  186.8 2.0 copy-start.5
  186.8 15.9 %collective-permute-start.16 = (bf16[64,768]{1,0:T(8,128)(2,1)S(1)}, bf16[64,768]{1,0:T(8,128)(2,1)S(1)}, u32[]{:S(2)}, u32[]{:S(2)}) collective-permute-start(bf16[64,768]{1,0:T(8,128)(2,1)S(1)} %get-tuple-element.168), channel_id=1, source_target_pairs={{0,1},{1,2},{2,3},{3,4},{4,5},{5,6},{6,7},{7,8},{8,9},{9,10},{10,1... | collective-permute-start | bytes 294920 | tf_op jit(solution)/shard_map/ppermute | solution.py:852
  188.8 1.0 copy-start.8
  192.8 9.9 %collective-permute-start.10 = (bf16[64,768]{1,0:T(8,128)(2,1)}, bf16[64,768]{1,0:T(8,128)(2,1)S(1)}, u32[]{:S(2)}, u32[]{:S(2)}) collective-permute-start(bf16[64,768]{1,0:T(8,128)(2,1)} %get-tuple-element.122), channel_id=1, source_target_pairs={{0,2},{1,3},{2,0},{3,1},{4,6},{5,7},{6,4},{7,5},{8,10},{9,11},{10,... | collective-permute-start | bytes 294920 | tf_op jit(solution)/shard_map/ppermute | solution.py:836
  194.1 8.7 %collective-permute-start.11 = (bf16[64,768]{1,0:T(8,128)(2,1)}, bf16[64,768]{1,0:T(8,128)(2,1)S(1)}, u32[]{:S(2)}, u32[]{:S(2)}) collective-permute-start(bf16[64,768]{1,0:T(8,128)(2,1)} %get-tuple-element.123), channel_id=1, source_target_pairs={{0,3},{1,0},{2,1},{3,2},{4,7},{5,4},{6,5},{7,6},{8,11},{9,8},{10,9... | collective-permute-start | bytes 294920 | tf_op jit(solution)/shard_map/ppermute | solution.py:836
  196.3 7.3 %collective-permute-start.12 = (bf16[64,768]{1,0:T(8,128)(2,1)}, bf16[64,768]{1,0:T(8,128)(2,1)S(1)}, u32[]{:S(2)}, u32[]{:S(2)}) collective-permute-start(bf16[64,768]{1,0:T(8,128)(2,1)} %get-tuple-element.125), channel_id=1, source_target_pairs={{0,4},{1,5},{2,6},{3,7},{4,8},{5,9},{6,10},{7,11},{8,12},{9,13},{1... | collective-permute-start | bytes 294920 | tf_op jit(solution)/shard_map/ppermute | solution.py:836
  197.4 52.3 %copy-start.18 = (bf16[64,768]{1,0:T(8,128)(2,1)}, bf16[64,768]{1,0:T(8,128)(2,1)S(1)}, u32[]{:S(2)}) copy-start(bf16[64,768]{1,0:T(8,128)(2,1)S(1)} %collective-permute-done.15.hr) | copy-start | bytes 294916
  197.4 7.9 %collective-permute-start.13 = (bf16[64,768]{1,0:T(8,128)(2,1)}, bf16[64,768]{1,0:T(8,128)(2,1)S(1)}, u32[]{:S(2)}, u32[]{:S(2)}) collective-permute-start(bf16[64,768]{1,0:T(8,128)(2,1)} %get-tuple-element.126), channel_id=1, source_target_pairs={{0,8},{1,9},{2,10},{3,11},{4,12},{5,13},{6,14},{7,15},{8,0},{9,1},... | collective-permute-start | bytes 294920 | tf_op jit(solution)/shard_map/ppermute | solution.py:836
  202.7 47.0 %copy-start.19 = (bf16[64,768]{1,0:T(8,128)(2,1)}, bf16[64,768]{1,0:T(8,128)(2,1)S(1)}, u32[]{:S(2)}) copy-start(bf16[64,768]{1,0:T(8,128)(2,1)S(1)} %collective-permute-done.16.hl) | copy-start | bytes 294916
  202.7 4.1 %collective-permute-start.14 = (bf16[64,768]{1,0:T(8,128)(2,1)}, bf16[64,768]{1,0:T(8,128)(2,1)S(1)}, u32[]{:S(2)}, u32[]{:S(2)}) collective-permute-start(bf16[64,768]{1,0:T(8,128)(2,1)} %get-tuple-element.127), channel_id=1, source_target_pairs={{0,12},{1,13},{2,14},{3,15},{4,0},{5,1},{6,2},{7,3},{8,4},{9,5},{1... | collective-permute-start | bytes 294920 | tf_op jit(solution)/shard_map/ppermute | solution.py:836
  202.7 5.4 %copy-start.12 = (bf16[64,768]{1,0:T(8,128)(2,1)}, bf16[64,768]{1,0:T(8,128)(2,1)S(1)}, u32[]{:S(2)}) copy-start(bf16[64,768]{1,0:T(8,128)(2,1)S(1)} %collective-permute-done.10.y2) | copy-start | bytes 294916
  202.7 5.4 %collective-permute-start.9 = (bf16[64,768]{1,0:T(8,128)(2,1)}, bf16[64,768]{1,0:T(8,128)(2,1)S(1)}, u32[]{:S(2)}, u32[]{:S(2)}) collective-permute-start(bf16[64,768]{1,0:T(8,128)(2,1)} %get-tuple-element.121), channel_id=1, source_target_pairs={{0,1},{1,2},{2,3},{3,0},{4,5},{5,6},{6,7},{7,4},{8,9},{9,10},{10,1... | collective-permute-start | bytes 294920 | tf_op jit(solution)/shard_map/ppermute | solution.py:836
  202.8 5.3 %copy-start.13 = (bf16[64,768]{1,0:T(8,128)(2,1)}, bf16[64,768]{1,0:T(8,128)(2,1)S(1)}, u32[]{:S(2)}) copy-start(bf16[64,768]{1,0:T(8,128)(2,1)S(1)} %collective-permute-done.11.y3) | copy-start | bytes 294916
  203.5 4.6 %copy-start.14 = (bf16[64,768]{1,0:T(8,128)(2,1)}, bf16[64,768]{1,0:T(8,128)(2,1)S(1)}, u32[]{:S(2)}) copy-start(bf16[64,768]{1,0:T(8,128)(2,1)S(1)} %collective-permute-done.12.c1) | copy-start | bytes 294916
  205.3 2.8 %copy-start.15 = (bf16[64,768]{1,0:T(8,128)(2,1)}, bf16[64,768]{1,0:T(8,128)(2,1)S(1)}, u32[]{:S(2)}) copy-start(bf16[64,768]{1,0:T(8,128)(2,1)S(1)} %collective-permute-done.13.c2) | copy-start | bytes 294916
  206.8 1.4 copy-start.16
  208.1 10.3 %copy-start.1 = (bf16[16,8,2304]{2,1,0:T(8,128)(2,1)}, bf16[16,8,2304]{2,1,0:T(8,128)(2,1)S(1)}, u32[]{:S(2)}) copy-start(bf16[16,8,2304]{2,1,0:T(8,128)(2,1)S(1)} %all-to-all-done.3.got) | copy-start | bytes 1769476
  218.4 6.9 %copy-start.24 = (bf16[32,768]{1,0:T(8,128)(2,1)S(1)}, bf16[32,768]{1,0:T(8,128)(2,1)}, u32[]{:S(2)}) copy-start(bf16[32,768]{1,0:T(8,128)(2,1)} %get-tuple-element.165) | copy-start | bytes 147460
  218.4 31.3 %all-to-all-start.4 = ((bf16[16,8,5376]{2,1,0:T(8,128)(2,1)}), bf16[16,8,5376]{2,1,0:T(8,128)(2,1)S(1)}, u32[]{:S(2)}, u32[]{:S(2)}) async-start(bf16[16,8,5376]{2,1,0:T(8,128)(2,1)} %bitcast.26), calls=%async_computation.6 | async-start | bytes 2752512 | tf_op jit(solution)/shard_map/all_to_all | solution.py:801
  225.3 23.8 %collective-permute-start.17 = (bf16[32,768]{1,0:T(8,128)(2,1)S(1)}, bf16[32,768]{1,0:T(8,128)(2,1)S(1)}, u32[]{:S(2)}, u32[]{:S(2)}) collective-permute-start(bf16[32,768]{1,0:T(8,128)(2,1)S(1)} %copy-done.24), channel_id=1, source_target_pairs={{0,0},{16,1},{32,2},{48,3},{64,4},{80,5},{96,6},{112,7},{1,8},{17,... | collective-permute-start | bytes 147464 | tf_op jit(solution)/shard_map/ppermute | solution.py:877
  249.7 1.1 copy-start
  (4 other events, 3.1 us)
Sparse Core Ops, SparseCore 0:
  11.7 75.3 all-gather.3
  96.8 25.7 all-gather.5
  125.0 36.2 reduce-scatter.4
  163.6 51.3 reduce-scatter.2

commit v3 on v2

--- a/solution.py
+++ b/solution.py
@@ -13,7 +13,7 @@
 CAP = 96
 LIGHT_SCALE = 96**-0.5
 HEAVY_SCALE = 64**-0.5
-PARAMS = pltpu.CompilerParams(vmem_limit_bytes=60 * 1024 * 1024)
+PARAMS = pltpu.CompilerParams(vmem_limit_bytes=63 * 1024 * 1024)
 SMEM = pl.BlockSpec(memory_space=pltpu.SMEM)
 VMEM = pl.BlockSpec(memory_space=pltpu.VMEM)
 HBM = pl.BlockSpec(memory_space=pl.ANY)
@@ -222,7 +222,7 @@
 
 def light_attn_kernel(
     meta, xl, x_in, xr, g_in, wall, ffn_in, cf_in, gin, vrows,
-    lo, dxg, halo, rest, gvec, heavy_wo,
+    lo, dxg, to_left, to_right, rest, gvec, heavy_wo,
     w, xs, a, a_t, qkv, o, do, dqkv, dk, dv, mask, w_pad, g, ffn, cf, lo_buf, d_a, gbuf, in_sems, out_sems,
 ):
     def wide(n, at=0):
@@ -369,8 +369,8 @@
 
     own = slice(64, 576)
     dxg[...] = norm_back(c[own] + cf[...], own) + g[...].astype(F32)
-    halo[0:64, :] = norm_back(c[0:64], slice(0, 64)).astype(BF)
-    halo[64:128, :] = norm_back(c[576:640], slice(576, 640)).astype(BF)
+    to_left[...] = norm_back(c[0:64], slice(0, 64)).astype(BF)
+    to_right[...] = norm_back(c[576:640], slice(576, 640)).astype(BF)
     stores.finish()
     for n in range(4):
         store(n).wait()
@@ -475,7 +475,7 @@
         sfb = jax.nn.sigmoid(jnp.sum(frb.astype(F32) * r_f, axis=-1, keepdims=True))
         sa[rows, :], sf[rows, :] = sab, sfb
         qkv = dot(arb, w[:, 512:896])
-        q[rows, :] = jnp.where(on, qkv[:, 0:128], 0.0).astype(BF)
+        q[rows, :] = jnp.where(on, qkv[:, 0:128] * HEAVY_SCALE, 0.0).astype(BF)
         k[rows, :] = qkv[:, 128:256].astype(BF)
         v[rows, :] = jnp.where(on, qkv[:, 256:384], 0.0).astype(BF)
         dab = (sab * xg[rows, 768:1536].astype(F32)).astype(BF)
@@ -498,7 +498,7 @@
             axis=1,
         )
         qb, dob = q[rows, :], do[rows, :]
-        s = dot_nt(k[...], qb) * HEAVY_SCALE + bias
+        s = dot_nt(k[...], qb) + bias
         e = jnp.exp(s - jnp.max(s, axis=0, keepdims=True))
         p = e * (1.0 / jnp.sum(e, axis=0, keepdims=True))
         pb = p.astype(BF)
@@ -510,7 +510,7 @@
         dp = dot_nt(v[...], dob)
         ds = (p * (dp - jnp.sum(p * dp, axis=0, keepdims=True))).astype(BF)
         dqkv[rows, 0:128] = jnp.where(on, dot_tn(ds, k[...]) * HEAVY_SCALE, 0.0).astype(BF)
-        dk[...] += dot(ds, qb) * HEAVY_SCALE
+        dk[...] += dot(ds, qb)
         dv[...] += dot(pb, dob)
 
     dqkv[:, 128:256] = dk[...].astype(BF)
@@ -586,18 +586,19 @@
     return jnp.concatenate([block[:, low : low + 768], last], axis=0)
 
 
-def owner_rows(r, cols):
+def owner_piece(r, cols, t):
     quarter = cols // 4
     row = lax.broadcasted_iota(jnp.int32, (128, 96), 0)
     col = lax.broadcasted_iota(jnp.int32, (128, 96), 1)
     device, low = 6 * (row >> 3), row & 7
     main = ((low < 6) & (col == device + low)).astype(F32).astype(BF)
-    tail = r[:, 3 * quarter : cols]
-    pieces = []
-    for t in range(3):
-        extra = ((low >= 6) & (col == device + 3 * (low - 6) + t)).astype(F32).astype(BF)
-        pieces.append((dot(main, r[:, quarter * t : quarter * t + quarter]) + dot(extra, tail)).astype(BF))
-    return jnp.concatenate(pieces, axis=1)
+    extra = ((low >= 6) & (col == device + 3 * (low - 6) + t)).astype(F32).astype(BF)
+    part = dot(main, r[:, quarter * t : quarter * t + quarter]) + dot(extra, r[:, 3 * quarter : cols])
+    return part.astype(BF)
+
+
+def owner_rows(r, cols):
+    return jnp.concatenate([owner_piece(r, cols, t) for t in range(3)], axis=1)
 
 
 def tail_of(block):
@@ -612,11 +613,21 @@
     send[:, S_DOWN:S_FFN] = tail_rows(r[...], F_DOWN)
 
 
-def spread_rest_kernel(r, send_in, send, hd, rows, sems):
-    rows[...] = owner_rows(r, R_ALL)
-    copy = Copies(sems).start(rows, send.at[:, 0:S_BACK])
+def spread_rest_kernel(r_in, send_in, send, hd, r, rows, in_sems, out_sems):
+    loads, stores = Copies(in_sems), Copies(out_sems)
+    quarter = R_ALL // 4
+    got = [
+        loads.start(r_in.at[:, quarter * t : quarter * t + quarter], r.at[:, quarter * t : quarter * t + quarter])
+        for t in (3, 0, 1, 2)
+    ]
+    got[0].wait()
     hd[...] = jnp.concatenate([r[32 * t : 32 * t + 32, R_DOWN:R_ALL] for t in range(3)], axis=1)
-    copy.wait()
+    for t in range(3):
+        piece = slice(quarter * t, quarter * t + quarter)
+        got[t + 1].wait()
+        rows[:, piece] = owner_piece(r, R_ALL, t)
+        stores.send(rows.at[:, piece], send.at[:, piece])
+    stores.finish()
 
 
 def sum_parts(got, a, b):
@@ -716,7 +727,7 @@
     return call(
         light_attn_kernel,
         [
-            ((512, 768), F32), ((512, 768), F32), ((128, 768), BF), ((768, R_ALL), BF), ((8, 768), F32),
+            ((512, 768), F32), ((512, 768), F32), ((64, 768), BF), ((64, 768), BF), ((768, R_ALL), BF), ((8, 768), F32),
             ((128, 768), BF),
         ],
         (meta, xl, tokens, xr, cotangent, wall, ffn, cf, gvec, vrows),
@@ -728,7 +739,7 @@
             ((512, 768), F32), ((640, 768), F32), ((768, 3072), BF),
         ],
         [SMEM, VMEM, HBM, VMEM, HBM] + [HBM] * 3 + [VMEM, VMEM],
-        [HBM, VMEM, VMEM, HBM, VMEM, VMEM],
+        [HBM, VMEM, VMEM, VMEM, HBM, VMEM, VMEM],
         sems=(8, 5),
         name="light_attn",
         us=2,
@@ -825,7 +836,7 @@
     ffn, cf, grad_ffn, gvec, vrows = run_light_ffn(tokens, cotangent, wall)
     rs_ffn = lax.psum_scatter(grad_ffn, "dp", scatter_dimension=0, tiled=True)
     lmeta = jnp.concatenate([jnp.stack([lengths[0, 0], me * 512, jnp.int32(8192)]), meta[18:20]])
-    lo, dxg, halo, rest, gvec, heavy_wo = run_light_attn(
+    lo, dxg, to_left, to_right, rest, gvec, heavy_wo = run_light_attn(
         lmeta, xl, tokens, xr, cotangent, wall, ffn, cf, gvec, vrows
     )
     *partial, rest = run_heavy(meta, xg, hw, heavy_wo, kmask, gvec, vrows, rest)
@@ -847,9 +858,10 @@
         in_specs=[SMEM] + [VMEM] * 8,
         name="first_sum",
     )
+    *blocks, to_left, to_right = lax.optimization_barrier((*blocks, to_left, to_right))
     blocks = along(blocks[0:4], 0, 1) + along(blocks[4:8], 1, 0)
-    hr = lax.ppermute(halo[0:64], "fsdp", left)
-    hl = lax.ppermute(halo[64:128], "fsdp", right)
+    hr = lax.ppermute(to_left, "fsdp", left)
+    hl = lax.ppermute(to_right, "fsdp", right)
     (send_ffn,) = call(spread_ffn_kernel, [((128, S_FFN), BF)], (rs_ffn,), name="spread_ffn")
     got_ffn = swap(send_ffn.reshape(16, 8, S_FFN))
     *blocks, got_ffn, hr, hl = lax.optimization_barrier((*blocks, got_ffn, hr, hl))
@@ -867,10 +879,10 @@
         spread_rest_kernel,
         [((128, S_ALL), BF), ((32, 768), BF)],
         (rs_rest, send),
-        [((128, S_BACK), BF)],
-        [VMEM, HBM],
+        [((96, R_ALL), BF), ((128, S_BACK), BF)],
+        [HBM, HBM],
         [HBM, VMEM],
-        sems=(1,),
+        sems=(4, 3),
         name="spread_rest",
         aliases={1: 0},
     )

time: 264 us -> 262 us (level)
    ppermute x2, waiting for transfers between devices: 0.01 us -> 5.71 us  [the longest x1 5.1 us: body(): hl = lax.ppermute(to_right, 'fsdp', right)]
    reduce_scatter x1, waiting for transfers between devices: 3.68 us -> 0.02 us  [body(): rs_rest = lax.psum_scatter(rest, 'dp', scatter_dimension=0, tiled=True)]
    ppermute x12, starting transfers between devices: 19.8 us -> 23 us  [along(): lax.ppermute(block, 'fsdp', [(i, (i // 4 + n * x) % 4 * 4 + (i % 4 + n *...]
where the time goes in v3:
time: 262 us; the launch traced here: 261 us
  Pallas kernels  93.7 us (36%)
  starting transfers between devices  84 us (32%)
  waiting for transfers between devices  58.5 us (22%)
  between operations  16.8 us (6%)
  local copies, waits for them, and re-layouts  5.88 us (2%)
    pallas_call x12, Pallas kernels, call(): pl.pallas_call(kernel, out_shape=[jax.ShapeDtypeStruct(s, t) for s, t in...  93.7 us
    all_gather x1, waiting for transfers between devices, body(): wall = lax.all_gather(pack, ALL, axis=0, tiled=True)  31.9 us
    all_to_all x4, starting transfers between devices, swap(): return lax.all_to_all(rows, 'fsdp', split_axis=0, concat_axis=0, tiled=True)  23.2 us
    ppermute x12, starting transfers between devices, along(): lax.ppermute(block, 'fsdp', [(i, (i // 4 + n * x) % 4 * 4 + (i % 4 + n *...  23 us
    ppermute x1, waiting for transfers between devices, body(): lax.ppermute(g_hd, ALL, [(d % 8 * 16 + d // 8, d) for d in range(128)])  13.7 us
    ppermute x1, starting transfers between devices, body(): hd = lax.ppermute(hd, ALL, [(d, d % 8 * 16 + d // 8) for d in range(128)])  9.59 us
    ppermute x1, starting transfers between devices, body(): lax.ppermute(g_hd, ALL, [(d % 8 * 16 + d // 8, d) for d in range(128)])  8.07 us
    all_to_all x1, starting transfers between devices, body(): lax.all_to_all(hsend, 'fsdp', split_axis=0, concat_axis=0, tiled=True)  6.93 us
  transfers between devices with their start and end apart: 27, of which 8 were waited for; matrix products, arithmetic and copies ran while one was open for 2% of the time, Pallas kernels for 32%

profile of v3, /device:TPU:3, one launch (start us, length us, event | category | flops | bytes accessed | tf_op | source)
XLA Modules:
  0.0 261.1 jit_solution(10749254816026545753)
XLA Ops:
  7.3 2.0 prep.1
  9.3 6.9 %all-to-all-start.1 = ((bf16[16,8,896]{2,1,0:T(8,128)(2,1)}), bf16[16,8,896]{2,1,0:T(8,128)(2,1)S(1)}, u32[]{:S(2)}, u32[]{:S(2)}) async-start(bf16[16,8,896]{2,1,0:T(8,128)(2,1)} %get-tuple-element.107), calls=%async_computation.1 | async-start | bytes 458752 | tf_op jit(solution)/shard_map/all_to_all | solution.py:791
  18.9 0.9 convert_reduce_fusion
  19.7 1.3 concatenate.12.meta
  21.0 3.0 %slots.1 = (bf16[128,1536]{1,0:T(8,128)(2,1)}, bf16[512,128]{1,0:T(8,128)(2,1)}) custom-call(s32[24]{0:T(128)} %concatenate.12.meta, s32[1,1024]{1,0:T(1,128)} %routed.1, bf16[512,768]{1,0:T(8,128)(2,1)} %x_in.3, bf16[512,768]{1,0:T(8,128)(2,1)} %g_in.3), custom_call_target="tpu_custom_call" | custom-call | flops 50000000 | bytes 150000 | tf_op jit(solution)/shard_map/slots/pallas_call | solution.py:692
  24.0 6.7 %all-to-all-start = ((bf16[16,8,1536]{2,1,0:T(8,128)(2,1)}), bf16[16,8,1536]{2,1,0:T(8,128)(2,1)S(1)}, u32[]{:S(2)}, u32[]{:S(2)}) async-start(bf16[16,8,1536]{2,1,0:T(8,128)(2,1)} %bitcast.30), calls=%async_computation | async-start | bytes 786432 | tf_op jit(solution)/shard_map/all_to_all | solution.py:812
  30.7 9.6 %collective-permute-start.2 = (bf16[32,768]{1,0:T(8,128)(2,1)S(1)}, bf16[32,768]{1,0:T(8,128)(2,1)S(1)}, u32[]{:S(2)}, u32[]{:S(2)}) collective-permute-start(bf16[32,768]{1,0:T(8,128)(2,1)S(1)} %copy-done.14), channel_id=1, source_target_pairs={{0,0},{1,16},{2,32},{3,48},{4,64},{5,80},{6,96},{7,112},{8,1},{9,1... | collective-permute-start | bytes 147464 | tf_op jit(solution)/shard_map/ppermute | solution.py:792
  40.3 1.6 fusion.2
  41.9 1.9 collective-permute-start
  43.8 5.5 %collective-permute-start.1 = (bf16[64,768]{1,0:T(8,128)(2,1)S(1)}, bf16[64,768]{1,0:T(8,128)(2,1)S(1)}, u32[]{:S(2)}, u32[]{:S(2)}) collective-permute-start(bf16[64,768]{1,0:T(8,128)(2,1)S(1)} %get-tuple-element.188), channel_id=1, source_target_pairs={{1,0},{2,1},{3,2},{4,3},{5,4},{6,5},{7,6},{8,7},{9,8},{10,9},{11,1... | collective-permute-start | bytes 294920 | tf_op jit(solution)/shard_map/ppermute | solution.py:831
  49.3 0.6 concatenate.14.meta
  49.9 0.7 fusion.1
  50.7 0.7 copy-done.1
  51.4 3.8 %entries.1 = (bf16[64,1536]{1,0:T(8,128)(2,1)}, bf16[16,64,1536]{2,1,0:T(8,128)(2,1)}, f32[1024,256]{1,0:T(8,128)}) custom-call(s32[24]{0:T(128)} %concatenate.12.meta, bf16[128,1536]{1,0:T(8,128)(2,1)} %bitcast.28), custom_call_target="tpu_custom_call" | custom-call | flops 50000000 | bytes 150000 | tf_op jit(solution)/shard_map/entries/pallas_call | solution.py:692
  55.3 31.9 %all-gather.4.cloned.1.call-done.wall = bf16[1024,5504]{1,0:T(8,128)(2,1)} async-done(((bf16[8,5504]{1,0:T(8,128)(2,1)}), bf16[1024,5504]{1,0:T(8,128)(2,1)}) %all-gather.4.cloned.1.call-update) | async-done | bytes 11272208 | tf_op jit(solution)/shard_map/all_gather | solution.py:789
  87.2 6.5 %all-to-all-start.2 = ((bf16[16,64,1536]{2,1,0:T(8,128)(2,1)}), bf16[16,64,1536]{2,1,0:T(8,128)(2,1)}, u32[]{:S(2)}, u32[]{:S(2)}) async-start(bf16[16,64,1536]{2,1,0:T(8,128)(2,1)} %get-tuple-element.109), calls=%async_computation.2 | async-start | bytes 6291456 | tf_op jit(solution)/shard_map/all_to_all | solution.py:812
  93.7 0.7 all-gather.6.cloned.1.call-update
  94.5 16.2 %light_ffn.1 = (f32[512,768]{1,0:T(8,128)}, f32[512,768]{1,0:T(8,128)}, bf16[768,3072]{1,0:T(8,128)(2,1)}, f32[8,768]{1,0:T(8,128)}, f32[8,768]{1,0:T(8,128)}) custom-call(bf16[512,768]{1,0:T(8,128)(2,1)} %x_in.3, bf16[512,768]{1,0:T(8,128)(2,1)} %g_in.3, bf16[1024,5504]{1,0:T(8,128)(2,1)} %all-gather.4.cloned.1.call-done.wall), custom_call_target="tpu_custom_call" | custom-call | flops 199999995904 | bytes 600000000 | tf_op jit(solution)/shard_map/light_ffn/pallas_call | solution.py:692
  110.9 27.3 %light_attn.1 = (f32[512,768]{1,0:T(8,128)}, f32[512,768]{1,0:T(8,128)}, bf16[64,768]{1,0:T(8,128)(2,1)}, bf16[64,768]{1,0:T(8,128)(2,1)}, bf16[768,5120]{1,0:T(...) custom-call(s32[5]{0:T(128)} %concatenate.14.meta, bf16[64,768]{1,0:T(8,128)(2,1)} %copy-done.3, ...), custom_call_target="tpu_custom_call" | custom-call | flops 2000000000 | bytes 6000000 | tf_op jit(solution)/shard_map/light_attn/pallas_call | solution.py:692
  138.3 23.0 %heavy.1 = (bf16[256,768]{1,0:T(8,128)(2,1)}, bf16[256,768]{1,0:T(8,128)(2,1)}, bf16[256,768]{1,0:T(8,128)(2,1)}, bf16[256,768]{1,0:T(8,128)(2,1)}, bf16[256,768...) custom-call(s32[24]{0:T(128)} %concatenate.12.meta, ...), custom_call_target="tpu_custom_call", output_to_operand_aliasing={{8}: (7, {})} | custom-call | flops 199999995904 | bytes 600000000 | tf_op jit(solution)/shard_map/heavy/pallas_call | solution.py:692
  161.4 1.0 copy-done.13
  162.3 1.2 collective-permute-start.3
  163.5 0.8 collective-permute-start.4
  164.3 1.9 collective-permute-start.5
  166.2 1.2 collective-permute-start.6
  167.4 2.4 collective-permute-start.7
  169.8 2.4 collective-permute-done.3.y1
  172.2 2.4 collective-permute-start.8
  174.6 2.3 spread_ffn.1
  177.0 4.9 %all-to-all-start.3 = ((bf16[16,8,2304]{2,1,0:T(8,128)(2,1)}), bf16[16,8,2304]{2,1,0:T(8,128)(2,1)S(1)}, u32[]{:S(2)}, u32[]{:S(2)}) async-start(bf16[16,8,2304]{2,1,0:T(8,128)(2,1)} %bitcast.27), calls=%async_computation.5 | async-start | bytes 1179648 | tf_op jit(solution)/shard_map/all_to_all | solution.py:812
  181.9 1.4 collective-permute-done.5.y3
  183.3 2.4 collective-permute-done.7.c2
  185.8 3.1 %first_sum.1 = (bf16[64,768]{1,0:T(8,128)(2,1)}, bf16[64,768]{1,0:T(8,128)(2,1)}, bf16[64,768]{1,0:T(8,128)(2,1)}, bf16[64,768]{1,0:T(8,128)(2,1)}, bf16[64,768]...) custom-call(s32[24]{0:T(128)} %concatenate.12.meta, ...), custom_call_target="tpu_custom_call" | custom-call | flops 50000000 | bytes 150000 | tf_op jit(solution)/shard_map/first_sum/pallas_call | solution.py:692
  188.9 1.3 collective-permute-start.10
  190.1 1.1 collective-permute-start.11
  191.2 10.7 %collective-permute-start.13 = (bf16[64,768]{1,0:T(8,128)(2,1)}, bf16[64,768]{1,0:T(8,128)(2,1)S(1)}, u32[]{:S(2)}, u32[]{:S(2)}) collective-permute-start(bf16[64,768]{1,0:T(8,128)(2,1)} %get-tuple-element.147), channel_id=1, source_target_pairs={{0,8},{1,9},{2,10},{3,11},{4,12},{5,13},{6,14},{7,15},{8,0},{9,1},... | collective-permute-start | bytes 294920 | tf_op jit(solution)/shard_map/ppermute | solution.py:847
  201.9 3.6 %collective-permute-start.15 = (bf16[64,768]{1,0:T(8,128)(2,1)}, bf16[64,768]{1,0:T(8,128)(2,1)S(1)}, u32[]{:S(2)}, u32[]{:S(2)}) collective-permute-start(bf16[64,768]{1,0:T(8,128)(2,1)} %get-tuple-element.150), channel_id=1, source_target_pairs={{1,0},{2,1},{3,2},{4,3},{5,4},{6,5},{7,6},{8,7},{9,8},{10,9},{11,1... | collective-permute-start | bytes 294920 | tf_op jit(solution)/shard_map/ppermute | solution.py:863
  205.5 1.9 collective-permute-start.16
  208.2 5.1 %collective-permute-done.16.hl = bf16[64,768]{1,0:T(8,128)(2,1)S(1)} collective-permute-done((bf16[64,768]{1,0:T(8,128)(2,1)}, bf16[64,768]{1,0:T(8,128)(2,1)S(1)}, u32[]{:S(2)}, u32[]{:S(2)}) %collective-permute-start.16) | collective-permute-done | bytes 98336 | tf_op jit(solution)/shard_map/ppermute | solution.py:864
  213.3 0.6 copy-done.11
  214.0 2.8 %home.1.send_in = bf16[128,5376]{1,0:T(8,128)(2,1)} custom-call(s32[24]{0:T(128)} %concatenate.12.meta, bf16[64,768]{1,0:T(8,128)(2,1)} %get-tuple-element.152.y0, bf16[64,768]{1,0:T(8,128)(2,1)} %collective-permute-done.9.y1, bf16[64,768]{1,0:T(8,128)(2,1)} %copy-done.5, bf16[64,768]{1,0:T(8,128)(2,1)} %copy-done.6, bf16[64,768]{1,0:T(8,128)(2,1)} %get-tuple-element.156.c0, ...), custom_call_target="tpu_custom_call" | custom-call | flops 50000000 | bytes 150000 | tf_op jit(solution)/shard_map/home/pallas_call | solution.py:692
  216.8 3.5 %spread_rest.1 = (bf16[128,5376]{1,0:T(8,128)(2,1)}, bf16[32,768]{1,0:T(8,128)(2,1)}) custom-call(bf16[96,5120]{1,0:T(8,128)(2,1)} %reduce-scatter.3.cloned.1.call-done.r_in, bf16[128,5376]{1,0:T(8,128)(2,1)} %home.1.send_in), custom_call_target="tpu_custom_call", output_to_operand_aliasing={{0}: (1, {})} | custom-call | flops 50000000 | bytes 150000 | tf_op jit(solution)/shard_map/spread_rest/pallas_call | solution.py:692
  220.4 5.0 %all-to-all-start.4 = ((bf16[16,8,5376]{2,1,0:T(8,128)(2,1)}), bf16[16,8,5376]{2,1,0:T(8,128)(2,1)}, u32[]{:S(2)}, u32[]{:S(2)}) async-start(bf16[16,8,5376]{2,1,0:T(8,128)(2,1)} %bitcast.26), calls=%async_computation.6 | async-start | bytes 2752512 | tf_op jit(solution)/shard_map/all_to_all | solution.py:812
  225.4 8.1 %collective-permute-start.17 = (bf16[32,768]{1,0:T(8,128)(2,1)S(1)}, bf16[32,768]{1,0:T(8,128)(2,1)S(1)}, u32[]{:S(2)}, u32[]{:S(2)}) collective-permute-start(bf16[32,768]{1,0:T(8,128)(2,1)S(1)} %copy-done.15), channel_id=1, source_target_pairs={{0,0},{16,1},{32,2},{48,3},{64,4},{80,5},{96,6},{112,7},{1,8},{17,... | collective-permute-start | bytes 147464 | tf_op jit(solution)/shard_map/ppermute | solution.py:889
  233.5 1.8 sum_ffn.1
  235.2 13.7 %collective-permute-done.17 = bf16[32,768]{1,0:T(8,128)(2,1)S(1)} collective-permute-done((bf16[32,768]{1,0:T(8,128)(2,1)S(1)}, bf16[32,768]{1,0:T(8,128)(2,1)S(1)}, u32[]{:S(2)}, u32[]{:S(2)}) %collective-permute-start.17) | collective-permute-done | bytes 49184 | tf_op jit(solution)/shard_map/ppermute | solution.py:889
  249.0 0.6 convert_element_type.9
  249.6 4.9 %last.1 = (bf16[512,768]{1,0:T(8,128)(2,1)}, bf16[512,768]{1,0:T(8,128)(2,1)}, f32[6,768]{1,0:T(8,128)}, f32[6,768]{1,0:T(8,128)}, f32[6,768]{1,0:T(8,128)}, /*i...) custom-call(bf16[16,8,5376]{2,1,0:T(8,128)(2,1)} %all-to-all-done.4., ...), custom_call_target="tpu_custom_call" | custom-call | flops 50000000 | bytes 150000 | tf_op jit(solution)/shard_map/last/pallas_call | solution.py:692
  (61 shorter events, 1.3 us)
Async XLA Ops:
  7.2 42.1 %copy-start.12 = (s32[1,2]{1,0:T(1,128)S(1)}, s32[1,2]{1,0:T(1,128)}, u32[]{:S(2)}) copy-start(s32[1,2]{1,0:T(1,128)} %param.23) | copy-start | bytes 28
  7.2 79.9 %all-gather.4.cloned.1.call-start = ((), (), s32[]{:S(2)}) async-start(), calls=%async_computation.7 | async-start | bytes 11360256 | tf_op jit(solution)/shard_map/all_gather | solution.py:789
  9.3 21.4 %copy-start.14 = (bf16[32,768]{1,0:T(8,128)(2,1)S(1)}, bf16[32,768]{1,0:T(8,128)(2,1)}, u32[]{:S(2)}) copy-start(bf16[32,768]{1,0:T(8,128)(2,1)} %get-tuple-element.108) | copy-start | bytes 147460
  9.3 14.7 %all-to-all-start.1 = ((bf16[16,8,896]{2,1,0:T(8,128)(2,1)}), bf16[16,8,896]{2,1,0:T(8,128)(2,1)S(1)}, u32[]{:S(2)}, u32[]{:S(2)}) async-start(bf16[16,8,896]{2,1,0:T(8,128)(2,1)} %get-tuple-element.107), calls=%async_computation.1 | async-start | bytes 458752 | tf_op jit(solution)/shard_map/all_to_all | solution.py:791
  24.0 26.6 %all-to-all-start = ((bf16[16,8,1536]{2,1,0:T(8,128)(2,1)}), bf16[16,8,1536]{2,1,0:T(8,128)(2,1)S(1)}, u32[]{:S(2)}, u32[]{:S(2)}) async-start(bf16[16,8,1536]{2,1,0:T(8,128)(2,1)} %bitcast.30), calls=%async_computation | async-start | bytes 786432 | tf_op jit(solution)/shard_map/all_to_all | solution.py:812
  30.7 19.2 %collective-permute-start.2 = (bf16[32,768]{1,0:T(8,128)(2,1)S(1)}, bf16[32,768]{1,0:T(8,128)(2,1)S(1)}, u32[]{:S(2)}, u32[]{:S(2)}) collective-permute-start(bf16[32,768]{1,0:T(8,128)(2,1)S(1)} %copy-done.14), channel_id=1, source_target_pairs={{0,0},{1,16},{2,32},{3,48},{4,64},{5,80},{6,96},{7,112},{8,1},{9,1... | collective-permute-start | bytes 147464 | tf_op jit(solution)/shard_map/ppermute | solution.py:792
  41.9 13.4 %collective-permute-start = (bf16[64,768]{1,0:T(8,128)(2,1)}, bf16[64,768]{1,0:T(8,128)(2,1)S(1)}, u32[]{:S(2)}, u32[]{:S(2)}) collective-permute-start(bf16[64,768]{1,0:T(8,128)(2,1)} %get-tuple-element.189), channel_id=1, source_target_pairs={{0,1},{1,2},{2,3},{3,4},{4,5},{5,6},{6,7},{7,8},{8,9},{9,10},{10,1... | collective-permute-start | bytes 294920 | tf_op jit(solution)/shard_map/ppermute | solution.py:830
  43.8 11.5 %collective-permute-start.1 = (bf16[64,768]{1,0:T(8,128)(2,1)S(1)}, bf16[64,768]{1,0:T(8,128)(2,1)S(1)}, u32[]{:S(2)}, u32[]{:S(2)}) collective-permute-start(bf16[64,768]{1,0:T(8,128)(2,1)S(1)} %get-tuple-element.188), channel_id=1, source_target_pairs={{1,0},{2,1},{3,2},{4,3},{5,4},{6,5},{7,6},{8,7},{9,8},{10,9},{11,1... | collective-permute-start | bytes 294920 | tf_op jit(solution)/shard_map/ppermute | solution.py:831
  50.7 0.7 copy-start.1
  55.3 31.9 %copy-start.3 = (bf16[64,768]{1,0:T(8,128)(2,1)}, bf16[64,768]{1,0:T(8,128)(2,1)S(1)}, u32[]{:S(2)}) copy-start(bf16[64,768]{1,0:T(8,128)(2,1)S(1)} %collective-permute-done.xl) | copy-start | bytes 294916
  55.3 31.9 %copy-start.4 = (bf16[64,768]{1,0:T(8,128)(2,1)}, bf16[64,768]{1,0:T(8,128)(2,1)S(1)}, u32[]{:S(2)}) copy-start(bf16[64,768]{1,0:T(8,128)(2,1)S(1)} %collective-permute-done.1.xr) | copy-start | bytes 294916
  87.2 51.1 %all-to-all-start.2 = ((bf16[16,64,1536]{2,1,0:T(8,128)(2,1)}), bf16[16,64,1536]{2,1,0:T(8,128)(2,1)}, u32[]{:S(2)}, u32[]{:S(2)}) async-start(bf16[16,64,1536]{2,1,0:T(8,128)(2,1)} %get-tuple-element.109), calls=%async_computation.2 | async-start | bytes 6291456 | tf_op jit(solution)/shard_map/all_to_all | solution.py:812
  93.7 44.6 %all-gather.6.cloned.1.call-start = ((), (), s32[]{:S(2)}) async-start(), calls=%async_computation.10 | async-start | bytes 2580480 | tf_op jit(solution)/shard_map/all_gather | solution.py:834
  94.4 80.2 %reduce-scatter.5.cloned.1.call-start = ((), (), s32[]{:S(2)}) async-start(), calls=%async_computation.9 | async-start | bytes 5308416 | tf_op jit(solution)/shard_map/reduce_scatter | solution.py:837
  110.7 106.1 %reduce-scatter.3.cloned.1.call-start = ((), (), s32[]{:S(2)}) async-start(), calls=%async_computation.8 | async-start | bytes 8847360 | tf_op jit(solution)/shard_map/reduce_scatter | solution.py:843
  161.3 1.0 copy-start.13
  162.3 9.9 %collective-permute-start.3 = (bf16[256,768]{1,0:T(8,128)(2,1)S(1)}, bf16[256,768]{1,0:T(8,128)(2,1)S(1)}, u32[]{:S(2)}, u32[]{:S(2)}) collective-permute-start(bf16[256,768]{1,0:T(8,128)(2,1)S(1)} %copy-done.13), channel_id=1, source_target_pairs={{0,4},{1,5},{2,6},{3,7},{4,8},{5,9},{6,10},{7,11},{8,12},{9,13},{1... | collective-permute-start | bytes 1179656 | tf_op jit(solution)/shard_map/ppermute | solution.py:847
  163.5 18.4 %collective-permute-start.4 = (bf16[256,768]{1,0:T(8,128)(2,1)}, bf16[256,768]{1,0:T(8,128)(2,1)}, u32[]{:S(2)}, u32[]{:S(2)}) collective-permute-start(bf16[256,768]{1,0:T(8,128)(2,1)} %get-tuple-element.125), channel_id=1, source_target_pairs={{0,8},{1,9},{2,10},{3,11},{4,12},{5,13},{6,14},{7,15},{8,0},{9,1},... | collective-permute-start | bytes 1179656 | tf_op jit(solution)/shard_map/ppermute | solution.py:847
  164.3 19.0 %collective-permute-start.5 = (bf16[256,768]{1,0:T(8,128)(2,1)}, bf16[256,768]{1,0:T(8,128)(2,1)}, u32[]{:S(2)}, u32[]{:S(2)}) collective-permute-start(bf16[256,768]{1,0:T(8,128)(2,1)} %get-tuple-element.126), channel_id=1, source_target_pairs={{0,12},{1,13},{2,14},{3,15},{4,0},{5,1},{6,2},{7,3},{8,4},{9,5},{1... | collective-permute-start | bytes 1179656 | tf_op jit(solution)/shard_map/ppermute | solution.py:847
  166.2 17.1 %collective-permute-start.6 = (bf16[256,768]{1,0:T(8,128)(2,1)}, bf16[256,768]{1,0:T(8,128)(2,1)}, u32[]{:S(2)}, u32[]{:S(2)}) collective-permute-start(bf16[256,768]{1,0:T(8,128)(2,1)} %get-tuple-element.128), channel_id=1, source_target_pairs={{0,1},{1,2},{2,3},{3,0},{4,5},{5,6},{6,7},{7,4},{8,9},{9,10},{10,1... | collective-permute-start | bytes 1179656 | tf_op jit(solution)/shard_map/ppermute | solution.py:847
  167.4 18.3 %collective-permute-start.7 = (bf16[256,768]{1,0:T(8,128)(2,1)}, bf16[256,768]{1,0:T(8,128)(2,1)}, u32[]{:S(2)}, u32[]{:S(2)}) collective-permute-start(bf16[256,768]{1,0:T(8,128)(2,1)} %get-tuple-element.129), channel_id=1, source_target_pairs={{0,2},{1,3},{2,0},{3,1},{4,6},{5,7},{6,4},{7,5},{8,10},{9,11},{10,... | collective-permute-start | bytes 1179656 | tf_op jit(solution)/shard_map/ppermute | solution.py:847
  172.2 13.6 %copy-start.2 = (bf16[256,768]{1,0:T(8,128)(2,1)}, bf16[256,768]{1,0:T(8,128)(2,1)S(1)}, u32[]{:S(2)}) copy-start(bf16[256,768]{1,0:T(8,128)(2,1)S(1)} %collective-permute-done.3.y1) | copy-start | bytes 1179652
  172.2 13.6 %collective-permute-start.8 = (bf16[256,768]{1,0:T(8,128)(2,1)}, bf16[256,768]{1,0:T(8,128)(2,1)}, u32[]{:S(2)}, u32[]{:S(2)}) collective-permute-start(bf16[256,768]{1,0:T(8,128)(2,1)} %get-tuple-element.130), channel_id=1, source_target_pairs={{0,3},{1,0},{2,1},{3,2},{4,7},{5,4},{6,5},{7,6},{8,11},{9,8},{10,9... | collective-permute-start | bytes 1179656 | tf_op jit(solution)/shard_map/ppermute | solution.py:847
  177.0 37.0 %all-to-all-start.3 = ((bf16[16,8,2304]{2,1,0:T(8,128)(2,1)}), bf16[16,8,2304]{2,1,0:T(8,128)(2,1)S(1)}, u32[]{:S(2)}, u32[]{:S(2)}) async-start(bf16[16,8,2304]{2,1,0:T(8,128)(2,1)} %bitcast.27), calls=%async_computation.5 | async-start | bytes 1179648 | tf_op jit(solution)/shard_map/all_to_all | solution.py:812
  188.9 13.0 %collective-permute-start.10 = (bf16[64,768]{1,0:T(8,128)(2,1)}, bf16[64,768]{1,0:T(8,128)(2,1)S(1)}, u32[]{:S(2)}, u32[]{:S(2)}) collective-permute-start(bf16[64,768]{1,0:T(8,128)(2,1)} %get-tuple-element.143), channel_id=1, source_target_pairs={{0,2},{1,3},{2,0},{3,1},{4,6},{5,7},{6,4},{7,5},{8,10},{9,11},{10,... | collective-permute-start | bytes 294920 | tf_op jit(solution)/shard_map/ppermute | solution.py:847
  190.1 15.4 %collective-permute-start.11 = (bf16[64,768]{1,0:T(8,128)(2,1)}, bf16[64,768]{1,0:T(8,128)(2,1)S(1)}, u32[]{:S(2)}, u32[]{:S(2)}) collective-permute-start(bf16[64,768]{1,0:T(8,128)(2,1)} %get-tuple-element.144), channel_id=1, source_target_pairs={{0,3},{1,0},{2,1},{3,2},{4,7},{5,4},{6,5},{7,6},{8,11},{9,8},{10,9... | collective-permute-start | bytes 294920 | tf_op jit(solution)/shard_map/ppermute | solution.py:847
  191.2 16.2 %collective-permute-start.12 = (bf16[64,768]{1,0:T(8,128)(2,1)}, bf16[64,768]{1,0:T(8,128)(2,1)S(1)}, u32[]{:S(2)}, u32[]{:S(2)}) collective-permute-start(bf16[64,768]{1,0:T(8,128)(2,1)} %get-tuple-element.146), channel_id=1, source_target_pairs={{0,4},{1,5},{2,6},{3,7},{4,8},{5,9},{6,10},{7,11},{8,12},{9,13},{1... | collective-permute-start | bytes 294920 | tf_op jit(solution)/shard_map/ppermute | solution.py:847
  191.2 16.3 %collective-permute-start.13 = (bf16[64,768]{1,0:T(8,128)(2,1)}, bf16[64,768]{1,0:T(8,128)(2,1)S(1)}, u32[]{:S(2)}, u32[]{:S(2)}) collective-permute-start(bf16[64,768]{1,0:T(8,128)(2,1)} %get-tuple-element.147), channel_id=1, source_target_pairs={{0,8},{1,9},{2,10},{3,11},{4,12},{5,13},{6,14},{7,15},{8,0},{9,1},... | collective-permute-start | bytes 294920 | tf_op jit(solution)/shard_map/ppermute | solution.py:847
  201.9 5.7 %collective-permute-start.14 = (bf16[64,768]{1,0:T(8,128)(2,1)}, bf16[64,768]{1,0:T(8,128)(2,1)S(1)}, u32[]{:S(2)}, u32[]{:S(2)}) collective-permute-start(bf16[64,768]{1,0:T(8,128)(2,1)} %get-tuple-element.148), channel_id=1, source_target_pairs={{0,12},{1,13},{2,14},{3,15},{4,0},{5,1},{6,2},{7,3},{8,4},{9,5},{1... | collective-permute-start | bytes 294920 | tf_op jit(solution)/shard_map/ppermute | solution.py:847
  201.9 12.1 %copy-start.5 = (bf16[64,768]{1,0:T(8,128)(2,1)}, bf16[64,768]{1,0:T(8,128)(2,1)S(1)}, u32[]{:S(2)}) copy-start(bf16[64,768]{1,0:T(8,128)(2,1)S(1)} %collective-permute-done.10.y2) | copy-start | bytes 294916
  201.9 6.3 %collective-permute-start.15 = (bf16[64,768]{1,0:T(8,128)(2,1)}, bf16[64,768]{1,0:T(8,128)(2,1)S(1)}, u32[]{:S(2)}, u32[]{:S(2)}) collective-permute-start(bf16[64,768]{1,0:T(8,128)(2,1)} %get-tuple-element.150), channel_id=1, source_target_pairs={{1,0},{2,1},{3,2},{4,3},{5,4},{6,5},{7,6},{8,7},{9,8},{10,9},{11,1... | collective-permute-start | bytes 294920 | tf_op jit(solution)/shard_map/ppermute | solution.py:863
  205.5 8.5 %copy-start.6 = (bf16[64,768]{1,0:T(8,128)(2,1)}, bf16[64,768]{1,0:T(8,128)(2,1)S(1)}, u32[]{:S(2)}) copy-start(bf16[64,768]{1,0:T(8,128)(2,1)S(1)} %collective-permute-done.11.y3) | copy-start | bytes 294916
  205.5 7.8 %collective-permute-start.16 = (bf16[64,768]{1,0:T(8,128)(2,1)}, bf16[64,768]{1,0:T(8,128)(2,1)S(1)}, u32[]{:S(2)}, u32[]{:S(2)}) collective-permute-start(bf16[64,768]{1,0:T(8,128)(2,1)} %get-tuple-element.151), channel_id=1, source_target_pairs={{0,1},{1,2},{2,3},{3,4},{4,5},{5,6},{6,7},{7,8},{8,9},{9,10},{10,1... | collective-permute-start | bytes 294920 | tf_op jit(solution)/shard_map/ppermute | solution.py:864
  207.5 6.5 %copy-start.7 = (bf16[64,768]{1,0:T(8,128)(2,1)}, bf16[64,768]{1,0:T(8,128)(2,1)S(1)}, u32[]{:S(2)}) copy-start(bf16[64,768]{1,0:T(8,128)(2,1)S(1)} %collective-permute-done.12.c1) | copy-start | bytes 294916
  207.5 6.5 %collective-permute-start.9 = (bf16[64,768]{1,0:T(8,128)(2,1)}, bf16[64,768]{1,0:T(8,128)(2,1)}, u32[]{:S(2)}, u32[]{:S(2)}) collective-permute-start(bf16[64,768]{1,0:T(8,128)(2,1)} %get-tuple-element.142), channel_id=1, source_target_pairs={{0,1},{1,2},{2,3},{3,0},{4,5},{5,6},{6,7},{7,4},{8,9},{9,10},{10,1... | collective-permute-start | bytes 294920 | tf_op jit(solution)/shard_map/ppermute | solution.py:847
  207.6 6.4 %copy-start.8 = (bf16[64,768]{1,0:T(8,128)(2,1)}, bf16[64,768]{1,0:T(8,128)(2,1)S(1)}, u32[]{:S(2)}) copy-start(bf16[64,768]{1,0:T(8,128)(2,1)S(1)} %collective-permute-done.13.c2) | copy-start | bytes 294916
  207.6 5.7 %copy-start.9 = (bf16[64,768]{1,0:T(8,128)(2,1)}, bf16[64,768]{1,0:T(8,128)(2,1)S(1)}, u32[]{:S(2)}) copy-start(bf16[64,768]{1,0:T(8,128)(2,1)S(1)} %collective-permute-done.14.c3) | copy-start | bytes 294916
  208.2 5.1 %copy-start.10 = (bf16[64,768]{1,0:T(8,128)(2,1)}, bf16[64,768]{1,0:T(8,128)(2,1)S(1)}, u32[]{:S(2)}) copy-start(bf16[64,768]{1,0:T(8,128)(2,1)S(1)} %collective-permute-done.15.hr) | copy-start | bytes 294916
  213.3 0.6 copy-start.11
  214.0 6.4 %copy-start = (bf16[16,8,2304]{2,1,0:T(8,128)(2,1)}, bf16[16,8,2304]{2,1,0:T(8,128)(2,1)S(1)}, u32[]{:S(2)}) copy-start(bf16[16,8,2304]{2,1,0:T(8,128)(2,1)S(1)} %all-to-all-done.3.got) | copy-start | bytes 1769476
  220.3 5.0 %copy-start.15 = (bf16[32,768]{1,0:T(8,128)(2,1)S(1)}, bf16[32,768]{1,0:T(8,128)(2,1)}, u32[]{:S(2)}) copy-start(bf16[32,768]{1,0:T(8,128)(2,1)} %get-tuple-element.187) | copy-start | bytes 147460
  220.4 29.3 %all-to-all-start.4 = ((bf16[16,8,5376]{2,1,0:T(8,128)(2,1)}), bf16[16,8,5376]{2,1,0:T(8,128)(2,1)}, u32[]{:S(2)}, u32[]{:S(2)}) async-start(bf16[16,8,5376]{2,1,0:T(8,128)(2,1)} %bitcast.26), calls=%async_computation.6 | async-start | bytes 2752512 | tf_op jit(solution)/shard_map/all_to_all | solution.py:812
  225.4 23.6 %collective-permute-start.17 = (bf16[32,768]{1,0:T(8,128)(2,1)S(1)}, bf16[32,768]{1,0:T(8,128)(2,1)S(1)}, u32[]{:S(2)}, u32[]{:S(2)}) collective-permute-start(bf16[32,768]{1,0:T(8,128)(2,1)S(1)} %copy-done.15), channel_id=1, source_target_pairs={{0,0},{16,1},{32,2},{48,3},{64,4},{80,5},{96,6},{112,7},{1,8},{17,... | collective-permute-start | bytes 147464 | tf_op jit(solution)/shard_map/ppermute | solution.py:889
Sparse Core Ops, SparseCore 0:
  11.7 75.3 all-gather.3
  96.8 25.7 all-gather.5
  125.0 36.3 reduce-scatter.4
  163.6 51.3 reduce-scatter.2

commit v4 on v3

--- a/solution.py
+++ b/solution.py
@@ -465,7 +465,7 @@
     on = (lax.broadcasted_iota(jnp.int32, (256, 128), 1) >> 6) == head
     got_xg.wait()
 
-    @pl.loop(0, 4)
+    @pl.loop(0, 4, unroll=2)
     def _(b):
         rows = pl.ds(pl.multiple_of(256 * b, 256), 256)
         u, _ = unit(xg[rows, 0:768].astype(F32))

time: 262 us -> 262 us (level)
  no operation moved by 1% of the time
where the time goes in v4:
time: 262 us; the launch traced here: 261 us
  Pallas kernels  93.5 us (36%)
  starting transfers between devices  83.9 us (32%)
  waiting for transfers between devices  58.8 us (22%)
  between operations  16.8 us (6%)
  local copies, waits for them, and re-layouts  5.89 us (2%)
    pallas_call x12, Pallas kernels, call(): pl.pallas_call(kernel, out_shape=[jax.ShapeDtypeStruct(s, t) for s, t in...  93.5 us
    all_gather x1, waiting for transfers between devices, body(): wall = lax.all_gather(pack, ALL, axis=0, tiled=True)  31.9 us
    all_to_all x4, starting transfers between devices, swap(): return lax.all_to_all(rows, 'fsdp', split_axis=0, concat_axis=0, tiled=True)  23.4 us
    ppermute x12, starting transfers between devices, along(): lax.ppermute(block, 'fsdp', [(i, (i // 4 + n * x) % 4 * 4 + (i % 4 + n *...  22.9 us
    ppermute x1, waiting for transfers between devices, body(): lax.ppermute(g_hd, ALL, [(d % 8 * 16 + d // 8, d) for d in range(128)])  14 us
    ppermute x1, starting transfers between devices, body(): hd = lax.ppermute(hd, ALL, [(d, d % 8 * 16 + d // 8) for d in range(128)])  9.59 us
    ppermute x1, starting transfers between devices, body(): lax.ppermute(g_hd, ALL, [(d % 8 * 16 + d // 8, d) for d in range(128)])  7.82 us
    all_to_all x1, starting transfers between devices, body(): lax.all_to_all(hsend, 'fsdp', split_axis=0, concat_axis=0, tiled=True)  6.93 us
  transfers between devices with their start and end apart: 27, of which 8 were waited for; matrix products, arithmetic and copies ran while one was open for 2% of the time, Pallas kernels for 32%

profile of v4, /device:TPU:3, one launch (start us, length us, event | category | flops | bytes accessed | tf_op | source)
XLA Modules:
  0.0 261.1 jit_solution(18246480516397258527)
XLA Ops:
  7.3 2.0 prep.1
  9.3 6.9 %all-to-all-start.1 = ((bf16[16,8,896]{2,1,0:T(8,128)(2,1)}), bf16[16,8,896]{2,1,0:T(8,128)(2,1)S(1)}, u32[]{:S(2)}, u32[]{:S(2)}) async-start(bf16[16,8,896]{2,1,0:T(8,128)(2,1)} %get-tuple-element.107), calls=%async_computation.1 | async-start | bytes 458752 | tf_op jit(solution)/shard_map/all_to_all | solution.py:791
  18.9 0.9 convert_reduce_fusion
  19.7 1.3 concatenate.12.meta
  21.0 3.0 %slots.1 = (bf16[128,1536]{1,0:T(8,128)(2,1)}, bf16[512,128]{1,0:T(8,128)(2,1)}) custom-call(s32[24]{0:T(128)} %concatenate.12.meta, s32[1,1024]{1,0:T(1,128)} %routed.1, bf16[512,768]{1,0:T(8,128)(2,1)} %x_in.3, bf16[512,768]{1,0:T(8,128)(2,1)} %g_in.3), custom_call_target="tpu_custom_call" | custom-call | flops 50000000 | bytes 150000 | tf_op jit(solution)/shard_map/slots/pallas_call | solution.py:692
  24.0 6.7 %all-to-all-start = ((bf16[16,8,1536]{2,1,0:T(8,128)(2,1)}), bf16[16,8,1536]{2,1,0:T(8,128)(2,1)S(1)}, u32[]{:S(2)}, u32[]{:S(2)}) async-start(bf16[16,8,1536]{2,1,0:T(8,128)(2,1)} %bitcast.30), calls=%async_computation | async-start | bytes 786432 | tf_op jit(solution)/shard_map/all_to_all | solution.py:812
  30.7 9.6 %collective-permute-start.2 = (bf16[32,768]{1,0:T(8,128)(2,1)S(1)}, bf16[32,768]{1,0:T(8,128)(2,1)S(1)}, u32[]{:S(2)}, u32[]{:S(2)}) collective-permute-start(bf16[32,768]{1,0:T(8,128)(2,1)S(1)} %copy-done.14), channel_id=1, source_target_pairs={{0,0},{1,16},{2,32},{3,48},{4,64},{5,80},{6,96},{7,112},{8,1},{9,1... | collective-permute-start | bytes 147464 | tf_op jit(solution)/shard_map/ppermute | solution.py:792
  40.3 1.6 fusion.2
  41.9 1.9 collective-permute-start
  43.8 5.5 %collective-permute-start.1 = (bf16[64,768]{1,0:T(8,128)(2,1)S(1)}, bf16[64,768]{1,0:T(8,128)(2,1)S(1)}, u32[]{:S(2)}, u32[]{:S(2)}) collective-permute-start(bf16[64,768]{1,0:T(8,128)(2,1)S(1)} %get-tuple-element.188), channel_id=1, source_target_pairs={{1,0},{2,1},{3,2},{4,3},{5,4},{6,5},{7,6},{8,7},{9,8},{10,9},{11,1... | collective-permute-start | bytes 294920 | tf_op jit(solution)/shard_map/ppermute | solution.py:831
  49.3 0.6 concatenate.14.meta
  49.9 0.7 fusion.1
  50.7 0.7 copy-done.1
  51.4 3.8 %entries.1 = (bf16[64,1536]{1,0:T(8,128)(2,1)}, bf16[16,64,1536]{2,1,0:T(8,128)(2,1)}, f32[1024,256]{1,0:T(8,128)}) custom-call(s32[24]{0:T(128)} %concatenate.12.meta, bf16[128,1536]{1,0:T(8,128)(2,1)} %bitcast.28), custom_call_target="tpu_custom_call" | custom-call | flops 50000000 | bytes 150000 | tf_op jit(solution)/shard_map/entries/pallas_call | solution.py:692
  55.3 31.9 %all-gather.4.cloned.1.call-done.wall = bf16[1024,5504]{1,0:T(8,128)(2,1)} async-done(((bf16[8,5504]{1,0:T(8,128)(2,1)}), bf16[1024,5504]{1,0:T(8,128)(2,1)}) %all-gather.4.cloned.1.call-update) | async-done | bytes 11272208 | tf_op jit(solution)/shard_map/all_gather | solution.py:789
  87.2 6.5 %all-to-all-start.2 = ((bf16[16,64,1536]{2,1,0:T(8,128)(2,1)}), bf16[16,64,1536]{2,1,0:T(8,128)(2,1)}, u32[]{:S(2)}, u32[]{:S(2)}) async-start(bf16[16,64,1536]{2,1,0:T(8,128)(2,1)} %get-tuple-element.109), calls=%async_computation.2 | async-start | bytes 6291456 | tf_op jit(solution)/shard_map/all_to_all | solution.py:812
  93.7 0.7 all-gather.6.cloned.1.call-update
  94.5 16.2 %light_ffn.1 = (f32[512,768]{1,0:T(8,128)}, f32[512,768]{1,0:T(8,128)}, bf16[768,3072]{1,0:T(8,128)(2,1)}, f32[8,768]{1,0:T(8,128)}, f32[8,768]{1,0:T(8,128)}) custom-call(bf16[512,768]{1,0:T(8,128)(2,1)} %x_in.3, bf16[512,768]{1,0:T(8,128)(2,1)} %g_in.3, bf16[1024,5504]{1,0:T(8,128)(2,1)} %all-gather.4.cloned.1.call-done.wall), custom_call_target="tpu_custom_call" | custom-call | flops 199999995904 | bytes 600000000 | tf_op jit(solution)/shard_map/light_ffn/pallas_call | solution.py:692
  110.9 27.3 %light_attn.1 = (f32[512,768]{1,0:T(8,128)}, f32[512,768]{1,0:T(8,128)}, bf16[64,768]{1,0:T(8,128)(2,1)}, bf16[64,768]{1,0:T(8,128)(2,1)}, bf16[768,5120]{1,0:T(...) custom-call(s32[5]{0:T(128)} %concatenate.14.meta, bf16[64,768]{1,0:T(8,128)(2,1)} %copy-done.3, ...), custom_call_target="tpu_custom_call" | custom-call | flops 2000000000 | bytes 6000000 | tf_op jit(solution)/shard_map/light_attn/pallas_call | solution.py:692
  138.3 22.7 %heavy.1 = (bf16[256,768]{1,0:T(8,128)(2,1)}, bf16[256,768]{1,0:T(8,128)(2,1)}, bf16[256,768]{1,0:T(8,128)(2,1)}, bf16[256,768]{1,0:T(8,128)(2,1)}, bf16[256,768...) custom-call(s32[24]{0:T(128)} %concatenate.12.meta, ...), custom_call_target="tpu_custom_call", output_to_operand_aliasing={{8}: (7, {})} | custom-call | flops 199999995904 | bytes 600000000 | tf_op jit(solution)/shard_map/heavy/pallas_call | solution.py:692
  161.1 1.0 copy-done.13
  162.1 1.2 collective-permute-start.3
  163.3 0.8 collective-permute-start.4
  164.1 1.9 collective-permute-start.5
  166.0 1.2 collective-permute-start.6
  167.2 2.4 collective-permute-start.7
  169.6 2.4 collective-permute-done.3.y1
  172.0 2.4 collective-permute-start.8
  174.4 2.3 spread_ffn.1
  176.8 4.9 %all-to-all-start.3 = ((bf16[16,8,2304]{2,1,0:T(8,128)(2,1)}), bf16[16,8,2304]{2,1,0:T(8,128)(2,1)S(1)}, u32[]{:S(2)}, u32[]{:S(2)}) async-start(bf16[16,8,2304]{2,1,0:T(8,128)(2,1)} %bitcast.27), calls=%async_computation.5 | async-start | bytes 1179648 | tf_op jit(solution)/shard_map/all_to_all | solution.py:812
  181.7 1.4 collective-permute-done.5.y3
  183.0 2.4 collective-permute-done.7.c2
  185.6 3.1 %first_sum.1 = (bf16[64,768]{1,0:T(8,128)(2,1)}, bf16[64,768]{1,0:T(8,128)(2,1)}, bf16[64,768]{1,0:T(8,128)(2,1)}, bf16[64,768]{1,0:T(8,128)(2,1)}, bf16[64,768]...) custom-call(s32[24]{0:T(128)} %concatenate.12.meta, ...), custom_call_target="tpu_custom_call" | custom-call | flops 50000000 | bytes 150000 | tf_op jit(solution)/shard_map/first_sum/pallas_call | solution.py:692
  188.7 1.3 collective-permute-start.10
  189.9 1.1 collective-permute-start.11
  191.0 10.6 %collective-permute-start.13 = (bf16[64,768]{1,0:T(8,128)(2,1)}, bf16[64,768]{1,0:T(8,128)(2,1)S(1)}, u32[]{:S(2)}, u32[]{:S(2)}) collective-permute-start(bf16[64,768]{1,0:T(8,128)(2,1)} %get-tuple-element.147), channel_id=1, source_target_pairs={{0,8},{1,9},{2,10},{3,11},{4,12},{5,13},{6,14},{7,15},{8,0},{9,1},... | collective-permute-start | bytes 294920 | tf_op jit(solution)/shard_map/ppermute | solution.py:847
  201.6 3.6 %collective-permute-start.15 = (bf16[64,768]{1,0:T(8,128)(2,1)}, bf16[64,768]{1,0:T(8,128)(2,1)S(1)}, u32[]{:S(2)}, u32[]{:S(2)}) collective-permute-start(bf16[64,768]{1,0:T(8,128)(2,1)} %get-tuple-element.150), channel_id=1, source_target_pairs={{1,0},{2,1},{3,2},{4,3},{5,4},{6,5},{7,6},{8,7},{9,8},{10,9},{11,1... | collective-permute-start | bytes 294920 | tf_op jit(solution)/shard_map/ppermute | solution.py:863
  205.3 1.9 collective-permute-start.16
  207.9 5.1 %collective-permute-done.16.hl = bf16[64,768]{1,0:T(8,128)(2,1)S(1)} collective-permute-done((bf16[64,768]{1,0:T(8,128)(2,1)}, bf16[64,768]{1,0:T(8,128)(2,1)S(1)}, u32[]{:S(2)}, u32[]{:S(2)}) %collective-permute-start.16) | collective-permute-done | bytes 98336 | tf_op jit(solution)/shard_map/ppermute | solution.py:864
  213.1 0.6 copy-done.11
  213.7 2.8 %home.1.send_in = bf16[128,5376]{1,0:T(8,128)(2,1)} custom-call(s32[24]{0:T(128)} %concatenate.12.meta, bf16[64,768]{1,0:T(8,128)(2,1)} %get-tuple-element.152.y0, bf16[64,768]{1,0:T(8,128)(2,1)} %collective-permute-done.9.y1, bf16[64,768]{1,0:T(8,128)(2,1)} %copy-done.5, bf16[64,768]{1,0:T(8,128)(2,1)} %copy-done.6, bf16[64,768]{1,0:T(8,128)(2,1)} %get-tuple-element.156.c0, ...), custom_call_target="tpu_custom_call" | custom-call | flops 50000000 | bytes 150000 | tf_op jit(solution)/shard_map/home/pallas_call | solution.py:692
  216.5 3.5 %spread_rest.1 = (bf16[128,5376]{1,0:T(8,128)(2,1)}, bf16[32,768]{1,0:T(8,128)(2,1)}) custom-call(bf16[96,5120]{1,0:T(8,128)(2,1)} %reduce-scatter.3.cloned.1.call-done.r_in, bf16[128,5376]{1,0:T(8,128)(2,1)} %home.1.send_in), custom_call_target="tpu_custom_call", output_to_operand_aliasing={{0}: (1, {})} | custom-call | flops 50000000 | bytes 150000 | tf_op jit(solution)/shard_map/spread_rest/pallas_call | solution.py:692
  220.1 5.3 %all-to-all-start.4 = ((bf16[16,8,5376]{2,1,0:T(8,128)(2,1)}), bf16[16,8,5376]{2,1,0:T(8,128)(2,1)}, u32[]{:S(2)}, u32[]{:S(2)}) async-start(bf16[16,8,5376]{2,1,0:T(8,128)(2,1)} %bitcast.26), calls=%async_computation.6 | async-start | bytes 2752512 | tf_op jit(solution)/shard_map/all_to_all | solution.py:812
  225.4 7.8 %collective-permute-start.17 = (bf16[32,768]{1,0:T(8,128)(2,1)S(1)}, bf16[32,768]{1,0:T(8,128)(2,1)S(1)}, u32[]{:S(2)}, u32[]{:S(2)}) collective-permute-start(bf16[32,768]{1,0:T(8,128)(2,1)S(1)} %copy-done.15), channel_id=1, source_target_pairs={{0,0},{16,1},{32,2},{48,3},{64,4},{80,5},{96,6},{112,7},{1,8},{17,... | collective-permute-start | bytes 147464 | tf_op jit(solution)/shard_map/ppermute | solution.py:889
  233.2 1.8 sum_ffn.1
  235.0 14.0 %collective-permute-done.17 = bf16[32,768]{1,0:T(8,128)(2,1)S(1)} collective-permute-done((bf16[32,768]{1,0:T(8,128)(2,1)S(1)}, bf16[32,768]{1,0:T(8,128)(2,1)S(1)}, u32[]{:S(2)}, u32[]{:S(2)}) %collective-permute-start.17) | collective-permute-done | bytes 49184 | tf_op jit(solution)/shard_map/ppermute | solution.py:889
  249.0 0.6 convert_element_type.9
  249.6 4.9 %last.1 = (bf16[512,768]{1,0:T(8,128)(2,1)}, bf16[512,768]{1,0:T(8,128)(2,1)}, f32[6,768]{1,0:T(8,128)}, f32[6,768]{1,0:T(8,128)}, f32[6,768]{1,0:T(8,128)}, /*i...) custom-call(bf16[16,8,5376]{2,1,0:T(8,128)(2,1)} %all-to-all-done.4., ...), custom_call_target="tpu_custom_call" | custom-call | flops 50000000 | bytes 150000 | tf_op jit(solution)/shard_map/last/pallas_call | solution.py:692
  (61 shorter events, 1.3 us)
Async XLA Ops:
  7.2 42.1 %copy-start.12 = (s32[1,2]{1,0:T(1,128)S(1)}, s32[1,2]{1,0:T(1,128)}, u32[]{:S(2)}) copy-start(s32[1,2]{1,0:T(1,128)} %param.23) | copy-start | bytes 28
  7.2 79.9 %all-gather.4.cloned.1.call-start = ((), (), s32[]{:S(2)}) async-start(), calls=%async_computation.7 | async-start | bytes 11360256 | tf_op jit(solution)/shard_map/all_gather | solution.py:789
  9.3 21.4 %copy-start.14 = (bf16[32,768]{1,0:T(8,128)(2,1)S(1)}, bf16[32,768]{1,0:T(8,128)(2,1)}, u32[]{:S(2)}) copy-start(bf16[32,768]{1,0:T(8,128)(2,1)} %get-tuple-element.108) | copy-start | bytes 147460
  9.3 14.7 %all-to-all-start.1 = ((bf16[16,8,896]{2,1,0:T(8,128)(2,1)}), bf16[16,8,896]{2,1,0:T(8,128)(2,1)S(1)}, u32[]{:S(2)}, u32[]{:S(2)}) async-start(bf16[16,8,896]{2,1,0:T(8,128)(2,1)} %get-tuple-element.107), calls=%async_computation.1 | async-start | bytes 458752 | tf_op jit(solution)/shard_map/all_to_all | solution.py:791
  24.0 26.6 %all-to-all-start = ((bf16[16,8,1536]{2,1,0:T(8,128)(2,1)}), bf16[16,8,1536]{2,1,0:T(8,128)(2,1)S(1)}, u32[]{:S(2)}, u32[]{:S(2)}) async-start(bf16[16,8,1536]{2,1,0:T(8,128)(2,1)} %bitcast.30), calls=%async_computation | async-start | bytes 786432 | tf_op jit(solution)/shard_map/all_to_all | solution.py:812
  30.7 19.2 %collective-permute-start.2 = (bf16[32,768]{1,0:T(8,128)(2,1)S(1)}, bf16[32,768]{1,0:T(8,128)(2,1)S(1)}, u32[]{:S(2)}, u32[]{:S(2)}) collective-permute-start(bf16[32,768]{1,0:T(8,128)(2,1)S(1)} %copy-done.14), channel_id=1, source_target_pairs={{0,0},{1,16},{2,32},{3,48},{4,64},{5,80},{6,96},{7,112},{8,1},{9,1... | collective-permute-start | bytes 147464 | tf_op jit(solution)/shard_map/ppermute | solution.py:792
  41.9 13.4 %collective-permute-start = (bf16[64,768]{1,0:T(8,128)(2,1)}, bf16[64,768]{1,0:T(8,128)(2,1)S(1)}, u32[]{:S(2)}, u32[]{:S(2)}) collective-permute-start(bf16[64,768]{1,0:T(8,128)(2,1)} %get-tuple-element.189), channel_id=1, source_target_pairs={{0,1},{1,2},{2,3},{3,4},{4,5},{5,6},{6,7},{7,8},{8,9},{9,10},{10,1... | collective-permute-start | bytes 294920 | tf_op jit(solution)/shard_map/ppermute | solution.py:830
  43.8 11.5 %collective-permute-start.1 = (bf16[64,768]{1,0:T(8,128)(2,1)S(1)}, bf16[64,768]{1,0:T(8,128)(2,1)S(1)}, u32[]{:S(2)}, u32[]{:S(2)}) collective-permute-start(bf16[64,768]{1,0:T(8,128)(2,1)S(1)} %get-tuple-element.188), channel_id=1, source_target_pairs={{1,0},{2,1},{3,2},{4,3},{5,4},{6,5},{7,6},{8,7},{9,8},{10,9},{11,1... | collective-permute-start | bytes 294920 | tf_op jit(solution)/shard_map/ppermute | solution.py:831
  50.7 0.7 copy-start.1
  55.3 31.9 %copy-start.3 = (bf16[64,768]{1,0:T(8,128)(2,1)}, bf16[64,768]{1,0:T(8,128)(2,1)S(1)}, u32[]{:S(2)}) copy-start(bf16[64,768]{1,0:T(8,128)(2,1)S(1)} %collective-permute-done.xl) | copy-start | bytes 294916
  55.3 31.9 %copy-start.4 = (bf16[64,768]{1,0:T(8,128)(2,1)}, bf16[64,768]{1,0:T(8,128)(2,1)S(1)}, u32[]{:S(2)}) copy-start(bf16[64,768]{1,0:T(8,128)(2,1)S(1)} %collective-permute-done.1.xr) | copy-start | bytes 294916
  87.2 51.1 %all-to-all-start.2 = ((bf16[16,64,1536]{2,1,0:T(8,128)(2,1)}), bf16[16,64,1536]{2,1,0:T(8,128)(2,1)}, u32[]{:S(2)}, u32[]{:S(2)}) async-start(bf16[16,64,1536]{2,1,0:T(8,128)(2,1)} %get-tuple-element.109), calls=%async_computation.2 | async-start | bytes 6291456 | tf_op jit(solution)/shard_map/all_to_all | solution.py:812
  93.7 44.6 %all-gather.6.cloned.1.call-start = ((), (), s32[]{:S(2)}) async-start(), calls=%async_computation.10 | async-start | bytes 2580480 | tf_op jit(solution)/shard_map/all_gather | solution.py:834
  94.4 80.0 %reduce-scatter.5.cloned.1.call-start = ((), (), s32[]{:S(2)}) async-start(), calls=%async_computation.9 | async-start | bytes 5308416 | tf_op jit(solution)/shard_map/reduce_scatter | solution.py:837
  110.7 105.8 %reduce-scatter.3.cloned.1.call-start = ((), (), s32[]{:S(2)}) async-start(), calls=%async_computation.8 | async-start | bytes 8847360 | tf_op jit(solution)/shard_map/reduce_scatter | solution.py:843
  161.1 1.0 copy-start.13
  162.1 9.9 %collective-permute-start.3 = (bf16[256,768]{1,0:T(8,128)(2,1)S(1)}, bf16[256,768]{1,0:T(8,128)(2,1)S(1)}, u32[]{:S(2)}, u32[]{:S(2)}) collective-permute-start(bf16[256,768]{1,0:T(8,128)(2,1)S(1)} %copy-done.13), channel_id=1, source_target_pairs={{0,4},{1,5},{2,6},{3,7},{4,8},{5,9},{6,10},{7,11},{8,12},{9,13},{1... | collective-permute-start | bytes 1179656 | tf_op jit(solution)/shard_map/ppermute | solution.py:847
  163.3 18.4 %collective-permute-start.4 = (bf16[256,768]{1,0:T(8,128)(2,1)}, bf16[256,768]{1,0:T(8,128)(2,1)}, u32[]{:S(2)}, u32[]{:S(2)}) collective-permute-start(bf16[256,768]{1,0:T(8,128)(2,1)} %get-tuple-element.125), channel_id=1, source_target_pairs={{0,8},{1,9},{2,10},{3,11},{4,12},{5,13},{6,14},{7,15},{8,0},{9,1},... | collective-permute-start | bytes 1179656 | tf_op jit(solution)/shard_map/ppermute | solution.py:847
  164.1 19.0 %collective-permute-start.5 = (bf16[256,768]{1,0:T(8,128)(2,1)}, bf16[256,768]{1,0:T(8,128)(2,1)}, u32[]{:S(2)}, u32[]{:S(2)}) collective-permute-start(bf16[256,768]{1,0:T(8,128)(2,1)} %get-tuple-element.126), channel_id=1, source_target_pairs={{0,12},{1,13},{2,14},{3,15},{4,0},{5,1},{6,2},{7,3},{8,4},{9,5},{1... | collective-permute-start | bytes 1179656 | tf_op jit(solution)/shard_map/ppermute | solution.py:847
  166.0 17.1 %collective-permute-start.6 = (bf16[256,768]{1,0:T(8,128)(2,1)}, bf16[256,768]{1,0:T(8,128)(2,1)}, u32[]{:S(2)}, u32[]{:S(2)}) collective-permute-start(bf16[256,768]{1,0:T(8,128)(2,1)} %get-tuple-element.128), channel_id=1, source_target_pairs={{0,1},{1,2},{2,3},{3,0},{4,5},{5,6},{6,7},{7,4},{8,9},{9,10},{10,1... | collective-permute-start | bytes 1179656 | tf_op jit(solution)/shard_map/ppermute | solution.py:847
  167.2 18.3 %collective-permute-start.7 = (bf16[256,768]{1,0:T(8,128)(2,1)}, bf16[256,768]{1,0:T(8,128)(2,1)}, u32[]{:S(2)}, u32[]{:S(2)}) collective-permute-start(bf16[256,768]{1,0:T(8,128)(2,1)} %get-tuple-element.129), channel_id=1, source_target_pairs={{0,2},{1,3},{2,0},{3,1},{4,6},{5,7},{6,4},{7,5},{8,10},{9,11},{10,... | collective-permute-start | bytes 1179656 | tf_op jit(solution)/shard_map/ppermute | solution.py:847
  172.0 13.6 %copy-start.2 = (bf16[256,768]{1,0:T(8,128)(2,1)}, bf16[256,768]{1,0:T(8,128)(2,1)S(1)}, u32[]{:S(2)}) copy-start(bf16[256,768]{1,0:T(8,128)(2,1)S(1)} %collective-permute-done.3.y1) | copy-start | bytes 1179652
  172.0 13.6 %collective-permute-start.8 = (bf16[256,768]{1,0:T(8,128)(2,1)}, bf16[256,768]{1,0:T(8,128)(2,1)}, u32[]{:S(2)}, u32[]{:S(2)}) collective-permute-start(bf16[256,768]{1,0:T(8,128)(2,1)} %get-tuple-element.130), channel_id=1, source_target_pairs={{0,3},{1,0},{2,1},{3,2},{4,7},{5,4},{6,5},{7,6},{8,11},{9,8},{10,9... | collective-permute-start | bytes 1179656 | tf_op jit(solution)/shard_map/ppermute | solution.py:847
  176.8 36.9 %all-to-all-start.3 = ((bf16[16,8,2304]{2,1,0:T(8,128)(2,1)}), bf16[16,8,2304]{2,1,0:T(8,128)(2,1)S(1)}, u32[]{:S(2)}, u32[]{:S(2)}) async-start(bf16[16,8,2304]{2,1,0:T(8,128)(2,1)} %bitcast.27), calls=%async_computation.5 | async-start | bytes 1179648 | tf_op jit(solution)/shard_map/all_to_all | solution.py:812
  188.7 13.0 %collective-permute-start.10 = (bf16[64,768]{1,0:T(8,128)(2,1)}, bf16[64,768]{1,0:T(8,128)(2,1)S(1)}, u32[]{:S(2)}, u32[]{:S(2)}) collective-permute-start(bf16[64,768]{1,0:T(8,128)(2,1)} %get-tuple-element.143), channel_id=1, source_target_pairs={{0,2},{1,3},{2,0},{3,1},{4,6},{5,7},{6,4},{7,5},{8,10},{9,11},{10,... | collective-permute-start | bytes 294920 | tf_op jit(solution)/shard_map/ppermute | solution.py:847
  189.9 15.3 %collective-permute-start.11 = (bf16[64,768]{1,0:T(8,128)(2,1)}, bf16[64,768]{1,0:T(8,128)(2,1)S(1)}, u32[]{:S(2)}, u32[]{:S(2)}) collective-permute-start(bf16[64,768]{1,0:T(8,128)(2,1)} %get-tuple-element.144), channel_id=1, source_target_pairs={{0,3},{1,0},{2,1},{3,2},{4,7},{5,4},{6,5},{7,6},{8,11},{9,8},{10,9... | collective-permute-start | bytes 294920 | tf_op jit(solution)/shard_map/ppermute | solution.py:847
  191.0 16.2 %collective-permute-start.12 = (bf16[64,768]{1,0:T(8,128)(2,1)}, bf16[64,768]{1,0:T(8,128)(2,1)S(1)}, u32[]{:S(2)}, u32[]{:S(2)}) collective-permute-start(bf16[64,768]{1,0:T(8,128)(2,1)} %get-tuple-element.146), channel_id=1, source_target_pairs={{0,4},{1,5},{2,6},{3,7},{4,8},{5,9},{6,10},{7,11},{8,12},{9,13},{1... | collective-permute-start | bytes 294920 | tf_op jit(solution)/shard_map/ppermute | solution.py:847
  191.0 16.3 %collective-permute-start.13 = (bf16[64,768]{1,0:T(8,128)(2,1)}, bf16[64,768]{1,0:T(8,128)(2,1)S(1)}, u32[]{:S(2)}, u32[]{:S(2)}) collective-permute-start(bf16[64,768]{1,0:T(8,128)(2,1)} %get-tuple-element.147), channel_id=1, source_target_pairs={{0,8},{1,9},{2,10},{3,11},{4,12},{5,13},{6,14},{7,15},{8,0},{9,1},... | collective-permute-start | bytes 294920 | tf_op jit(solution)/shard_map/ppermute | solution.py:847
  201.6 5.7 %collective-permute-start.14 = (bf16[64,768]{1,0:T(8,128)(2,1)}, bf16[64,768]{1,0:T(8,128)(2,1)S(1)}, u32[]{:S(2)}, u32[]{:S(2)}) collective-permute-start(bf16[64,768]{1,0:T(8,128)(2,1)} %get-tuple-element.148), channel_id=1, source_target_pairs={{0,12},{1,13},{2,14},{3,15},{4,0},{5,1},{6,2},{7,3},{8,4},{9,5},{1... | collective-permute-start | bytes 294920 | tf_op jit(solution)/shard_map/ppermute | solution.py:847
  201.6 12.1 %copy-start.5 = (bf16[64,768]{1,0:T(8,128)(2,1)}, bf16[64,768]{1,0:T(8,128)(2,1)S(1)}, u32[]{:S(2)}) copy-start(bf16[64,768]{1,0:T(8,128)(2,1)S(1)} %collective-permute-done.10.y2) | copy-start | bytes 294916
  201.6 6.3 %collective-permute-start.15 = (bf16[64,768]{1,0:T(8,128)(2,1)}, bf16[64,768]{1,0:T(8,128)(2,1)S(1)}, u32[]{:S(2)}, u32[]{:S(2)}) collective-permute-start(bf16[64,768]{1,0:T(8,128)(2,1)} %get-tuple-element.150), channel_id=1, source_target_pairs={{1,0},{2,1},{3,2},{4,3},{5,4},{6,5},{7,6},{8,7},{9,8},{10,9},{11,1... | collective-permute-start | bytes 294920 | tf_op jit(solution)/shard_map/ppermute | solution.py:863
  205.3 8.5 %copy-start.6 = (bf16[64,768]{1,0:T(8,128)(2,1)}, bf16[64,768]{1,0:T(8,128)(2,1)S(1)}, u32[]{:S(2)}) copy-start(bf16[64,768]{1,0:T(8,128)(2,1)S(1)} %collective-permute-done.11.y3) | copy-start | bytes 294916
  205.3 7.8 %collective-permute-start.16 = (bf16[64,768]{1,0:T(8,128)(2,1)}, bf16[64,768]{1,0:T(8,128)(2,1)S(1)}, u32[]{:S(2)}, u32[]{:S(2)}) collective-permute-start(bf16[64,768]{1,0:T(8,128)(2,1)} %get-tuple-element.151), channel_id=1, source_target_pairs={{0,1},{1,2},{2,3},{3,4},{4,5},{5,6},{6,7},{7,8},{8,9},{9,10},{10,1... | collective-permute-start | bytes 294920 | tf_op jit(solution)/shard_map/ppermute | solution.py:864
  207.2 6.5 %copy-start.7 = (bf16[64,768]{1,0:T(8,128)(2,1)}, bf16[64,768]{1,0:T(8,128)(2,1)S(1)}, u32[]{:S(2)}) copy-start(bf16[64,768]{1,0:T(8,128)(2,1)S(1)} %collective-permute-done.12.c1) | copy-start | bytes 294916
  207.2 6.5 %collective-permute-start.9 = (bf16[64,768]{1,0:T(8,128)(2,1)}, bf16[64,768]{1,0:T(8,128)(2,1)}, u32[]{:S(2)}, u32[]{:S(2)}) collective-permute-start(bf16[64,768]{1,0:T(8,128)(2,1)} %get-tuple-element.142), channel_id=1, source_target_pairs={{0,1},{1,2},{2,3},{3,0},{4,5},{5,6},{6,7},{7,4},{8,9},{9,10},{10,1... | collective-permute-start | bytes 294920 | tf_op jit(solution)/shard_map/ppermute | solution.py:847
  207.3 6.4 %copy-start.8 = (bf16[64,768]{1,0:T(8,128)(2,1)}, bf16[64,768]{1,0:T(8,128)(2,1)S(1)}, u32[]{:S(2)}) copy-start(bf16[64,768]{1,0:T(8,128)(2,1)S(1)} %collective-permute-done.13.c2) | copy-start | bytes 294916
  207.3 5.7 %copy-start.9 = (bf16[64,768]{1,0:T(8,128)(2,1)}, bf16[64,768]{1,0:T(8,128)(2,1)S(1)}, u32[]{:S(2)}) copy-start(bf16[64,768]{1,0:T(8,128)(2,1)S(1)} %collective-permute-done.14.c3) | copy-start | bytes 294916
  207.9 5.1 %copy-start.10 = (bf16[64,768]{1,0:T(8,128)(2,1)}, bf16[64,768]{1,0:T(8,128)(2,1)S(1)}, u32[]{:S(2)}) copy-start(bf16[64,768]{1,0:T(8,128)(2,1)S(1)} %collective-permute-done.15.hr) | copy-start | bytes 294916
  213.1 0.6 copy-start.11
  213.7 6.4 %copy-start = (bf16[16,8,2304]{2,1,0:T(8,128)(2,1)}, bf16[16,8,2304]{2,1,0:T(8,128)(2,1)S(1)}, u32[]{:S(2)}) copy-start(bf16[16,8,2304]{2,1,0:T(8,128)(2,1)S(1)} %all-to-all-done.3.got) | copy-start | bytes 1769476
  220.1 5.3 %copy-start.15 = (bf16[32,768]{1,0:T(8,128)(2,1)S(1)}, bf16[32,768]{1,0:T(8,128)(2,1)}, u32[]{:S(2)}) copy-start(bf16[32,768]{1,0:T(8,128)(2,1)} %get-tuple-element.187) | copy-start | bytes 147460
  220.1 29.6 %all-to-all-start.4 = ((bf16[16,8,5376]{2,1,0:T(8,128)(2,1)}), bf16[16,8,5376]{2,1,0:T(8,128)(2,1)}, u32[]{:S(2)}, u32[]{:S(2)}) async-start(bf16[16,8,5376]{2,1,0:T(8,128)(2,1)} %bitcast.26), calls=%async_computation.6 | async-start | bytes 2752512 | tf_op jit(solution)/shard_map/all_to_all | solution.py:812
  225.4 23.6 %collective-permute-start.17 = (bf16[32,768]{1,0:T(8,128)(2,1)S(1)}, bf16[32,768]{1,0:T(8,128)(2,1)S(1)}, u32[]{:S(2)}, u32[]{:S(2)}) collective-permute-start(bf16[32,768]{1,0:T(8,128)(2,1)S(1)} %copy-done.15), channel_id=1, source_target_pairs={{0,0},{16,1},{32,2},{48,3},{64,4},{80,5},{96,6},{112,7},{1,8},{17,... | collective-permute-start | bytes 147464 | tf_op jit(solution)/shard_map/ppermute | solution.py:889
Sparse Core Ops, SparseCore 0:
  11.7 75.3 all-gather.3
  96.8 25.7 all-gather.5
  125.0 36.2 reduce-scatter.4
  163.6 51.3 reduce-scatter.2
